TPU v7x, 512 devices: a whole 4x8x8 slice. The times are simulated.
512 devices in a mesh: tile: 64 (over z_hi, y, core), vert: 2 (over z_lo), dir: 4 (over x).
Axes of the slice: x: 4, y: 8, z: 8 (z_hi: 4, z_lo: 2; z = z_hi * 2 + z_lo), core: 2. Of those that a mesh axis runs over, the one named last changes fastest.
Arguments:
- tangent_in: float32 [8, 3, 64, 256, 128], P('dir', None, 'vert', 'tile'), may hold values from -6 to 6
- records: bfloat16 [16, 4, 64, 256, 128], P('dir', None, 'vert', 'tile'), may hold values from -2 to 10, as said below
- record_slot: int32 [16], replicated, may hold values from 0 to 15, each once
- step_record: int32 [2], replicated, may hold values from 0 to 15
- turbine_mask: int32 [64, 256, 128], P('vert', 'tile'), may hold values from 0 to 8
- group_weights: float32 [8, 8], P('dir'), may hold values from -1.2 to 1.2
Outputs:
- tangent_out: float32 [8, 3, 64, 256, 128], P('dir', None, 'vert', 'tile')
- power: float32 [8], P('dir')
Inputs may be any that keep to these rules, and one draw needn't show every extreme that they name: `records`: component 0 of every record lies in [4, 10], component 1 in [-2, 2], component 2 in [-1, 1], component 3 in [0.05, 0.5]. `record_slot`: each record is stored in exactly one slot.
All inputs are finite; a program needn't handle non-finite values.
Results may differ from a plain program's by a relative error of at most 0.0003.
Values may be sent and summed in bfloat16 or wider, within the bound.
No kernel may reach another device: no remote copies, remote signals or barrier semaphores. Data moves between devices by JAX's collectives and lax.ppermute only.
A program may use at most 64 MiB of HBM per device.

v0:
```python
import math

import jax
import jax.numpy as jnp
from jax import lax
from jax.sharding import PartitionSpec as P

STEPS = 2


TIME_STEP = 0.05
DRAG_COEFF = 0.5
POWER_SCALE = 0.01
VERTICAL_ASPECT = 400.0


def from_root(block, axis, source):
    block = jnp.where(lax.axis_index(axis) == source, block, jnp.zeros_like(block))
    return lax.psum(block, axis)


def padded_2(cells, sides, width):
    for axis, dim in sides:
        count = lax.axis_size(axis)
        ends = count - 1
        head = lax.slice_in_dim(cells, 0, width, axis=dim)
        tail = lax.slice_in_dim(cells, cells.shape[dim] - width, cells.shape[dim], axis=dim)
        cells = jnp.concatenate(
            [
                lax.ppermute(tail, axis, [(i, (i + 1) % count) for i in range(ends)]),
                cells,
                lax.ppermute(head, axis, [((i + 1) % count, i) for i in range(ends)]),
            ],
            axis=dim,
        )
    return cells


def shifted(padded, offset):
    inner_count = padded.shape[-2] - 4
    return lax.slice_in_dim(padded, 2 + offset, 2 + offset + inner_count, axis=padded.ndim - 2)


def x_slope(padded):
    return (
        8.0 * (shifted(padded, 1) - shifted(padded, -1))
        - (shifted(padded, 2) - shifted(padded, -2))
    ) / 12.0


def x_curve(padded):
    return shifted(padded, 1) - 2.0 * shifted(padded, 0) + shifted(padded, -1)


def y_slope(values_in):
    return (
        8.0 * (jnp.roll(values_in, -1, axis=-1) - jnp.roll(values_in, 1, axis=-1))
        - (jnp.roll(values_in, -2, axis=-1) - jnp.roll(values_in, 2, axis=-1))
    ) / 12.0


def y_curve(values_in):
    return jnp.roll(values_in, -1, axis=-1) - 2.0 * values_in + jnp.roll(values_in, 1, axis=-1)


def turbine_terms(turbine_mask, group_weights):
    turbine = (turbine_mask > 0).astype(jnp.float32)
    source = jnp.zeros((group_weights.shape[0],) + turbine_mask.shape, jnp.float32)
    for group_id in range(group_weights.shape[1]):
        source = (
            source
            + (turbine_mask == group_id + 1).astype(jnp.float32)[None]
            * group_weights[:, group_id][:, None, None, None]
        )
    return (turbine, source)


def horizontal_update(tangent, tangent_pad, background, background_pad, turbine, source):
    velocity = background[:3]
    viscosity = background[3]
    wind_speed = jnp.sqrt(velocity[0] * velocity[0] + velocity[1] * velocity[1])
    advect = velocity[0] * x_slope(tangent_pad) + velocity[1] * y_slope(tangent)
    produce = (
        tangent[:, 0:1] * x_slope(background_pad)[None] + tangent[:, 1:2] * y_slope(velocity)[None]
    )
    spread = viscosity * (x_curve(tangent_pad) + y_curve(tangent))
    parallel = (velocity[0] * tangent[:, 0] + velocity[1] * tangent[:, 1]) / wind_speed
    drag_term = -DRAG_COEFF * turbine * (wind_speed * tangent + velocity[None] * parallel[:, None])
    forcing = -source[:, None] * (wind_speed * velocity)[None]
    return tangent + TIME_STEP * (spread + drag_term + forcing - advect - produce)


def column_solve(rhs_levels, viscosity):
    stiff = VERTICAL_ASPECT * viscosity
    interior = 0.5 * (stiff[:-1] + stiff[1:])
    face_lower = jnp.concatenate([stiff[:1], interior], axis=0)
    face_upper = jnp.concatenate([interior, stiff[-1:]], axis=0)
    coeff_below = -TIME_STEP * face_lower
    coeff_above = -TIME_STEP * face_upper
    diagonal_main = 1.0 + TIME_STEP * (face_lower + face_upper)
    levels = jnp.moveaxis(rhs_levels, -3, 0)

    def forward(carried, inputs):
        ratio_prev, value_prev = carried
        below_now, center_now, above_now, rhs_now = inputs
        pivot_value = center_now - below_now * ratio_prev
        ratio_now = above_now / pivot_value
        value_now = (rhs_now - below_now * value_prev) / pivot_value
        return ((ratio_now, value_now), (ratio_now, value_now))

    initial = (
        jnp.zeros(viscosity.shape[1:], jnp.float32),
        jnp.zeros(levels.shape[1:], jnp.float32),
    )
    _, (ratios, values) = lax.scan(
        forward, initial, (coeff_below, diagonal_main, coeff_above, levels)
    )

    def backward(next_value, inputs):
        ratio_now, value_now = inputs
        result = value_now - ratio_now * next_value
        return (result, result)

    _, solved = lax.scan(
        backward, jnp.zeros(levels.shape[1:], jnp.float32), (ratios, values), reverse=True
    )
    return jnp.moveaxis(solved, 0, -3)


def power_terms(tangent, background, turbine):
    velocity = background[:3]
    wind_speed = jnp.sqrt(velocity[0] * velocity[0] + velocity[1] * velocity[1])
    return jnp.sum(
        turbine * wind_speed * (velocity[0] * tangent[:, 0] + velocity[1] * tangent[:, 1]),
        axis=(1, 2, 3),
    )


def fetch_record(store, slot_index):
    per_device = store.shape[0]
    local_record = lax.dynamic_index_in_dim(store, slot_index % per_device, 0, keepdims=False)
    return from_root(local_record, "dir", slot_index // per_device)


def add_power(power_sum, power_term):
    return power_sum + lax.psum(power_term, ("tile", "vert"))


def shards(tangent_in, records, record_slot, step_record, turbine_mask, group_weights):
    directions = tangent_in.shape[0]
    z_cells, x_cells, y_cells = (tangent_in.shape[2], tangent_in.shape[3], tangent_in.shape[4])
    turbine, source = turbine_terms(turbine_mask, group_weights)
    power_factor = POWER_SCALE / math.sqrt(
        z_cells * x_cells * y_cells * lax.axis_size("tile") * lax.axis_size("vert")
    )
    power_sum = jnp.zeros((directions,), jnp.float32)
    tangent = tangent_in
    for step_no in range(STEPS):
        slot_index = record_slot[step_record[step_no]]
        background_raw = fetch_record(records, slot_index)
        background = background_raw.astype(jnp.float32)
        background_pad = padded_2(background_raw[:3], (("tile", 2),), 2).astype(jnp.float32)
        tangent_pad = padded_2(tangent, (("tile", 3),), 2)
        partial_value = horizontal_update(
            tangent, tangent_pad, background, background_pad, turbine, source
        )
        stacked = jnp.concatenate(
            [tangent.reshape(3 * directions, z_cells, x_cells, y_cells), background[:3]], axis=0
        )
        stacked_pad = padded_2(stacked.astype(jnp.bfloat16), (("vert", 1),), 1).astype(
            stacked.dtype
        )
        level_slope = 0.5 * (stacked_pad[:, 2:] - stacked_pad[:, :-2])
        tangent_slope = level_slope[: 3 * directions].reshape(
            directions, 3, z_cells, x_cells, y_cells
        )
        wind_slope = level_slope[3 * directions :]
        rhs = partial_value - TIME_STEP * (
            background[2] * tangent_slope + tangent[:, 2:3] * wind_slope[None]
        )
        packed = jnp.concatenate(
            [rhs.reshape(3 * directions, z_cells, x_cells, y_cells), background[3:4]], axis=0
        )
        pieces = lax.all_to_all(packed, "vert", split_axis=2, concat_axis=1, tiled=True)
        levels_all = pieces.shape[1]
        x_local = pieces.shape[2]
        y_local = pieces.shape[3]
        rhs_columns = pieces[: 3 * directions].reshape(directions, 3, levels_all, x_local, y_local)
        solved = column_solve(rhs_columns, pieces[3 * directions])
        tangent = lax.all_to_all(
            solved.reshape(3 * directions, levels_all, x_local, y_local),
            "vert",
            split_axis=1,
            concat_axis=2,
            tiled=True,
        ).reshape(directions, 3, z_cells, x_cells, y_cells)
        power_sum = add_power(power_sum, power_terms(tangent, background, turbine))
    return (tangent, power_sum * power_factor)


def solution(mesh):
    in_specs = (
        P("dir", None, "vert", "tile", None),
        P("dir", None, "vert", "tile", None),
        P(),
        P(),
        P("vert", "tile", None),
        P("dir", None),
    )
    out_specs = (P("dir", None, "vert", "tile", None), P("dir"))
    return jax.shard_map(shards, mesh=mesh, in_specs=in_specs, out_specs=out_specs, check_vma=False)
```

profile of v0, /device:TPU:320, one launch (start us, length us, event | category | flops | bytes accessed | tf_op | source)
XLA Modules:
  0.0 541.3 jit_solution(7473651473160910213)
XLA Ops:
  7.2 2.1 fusion.78
  9.3 4.0 collective-permute-start
  13.3 1.9 collective-permute-start.1
  29.5 1.1 fusion.77
  30.6 49.4 %all-reduce.3.cloned.1.call-done = (bf16[4,32,4,128]{3,1,0,2:T(8,128)(2,1)}, bf16[4,32,4,128]{3,1,0,2:T(8,128)(2,1)}) async-done(((bf16[4,32,4,128]{3,1,0,2:T(8,128)(2,1)}, bf16[4,32,4,128]{3,1,0,2:T(8,128)(2,1)}), (bf16[4,32,4,128]{3,1,0,2:T(8,128)(2,1)}, bf16[4,32,4,128]{3,1,0,2:T(8,128)(2,1)})) %all-reduce.3.cloned.1.call-update) | async-done | bytes 262160 | tf_op jit(solution)/shard_map/psum | solution.py:19
  80.0 1.1 fusion.87
  81.7 0.9 copy-done.1
  84.0 0.8 fusion.81
  87.5 1.3 collective-permute-start.4
  88.8 4.5 collective-permute-start.5
  93.5 1.9 collective-permute-start.2
  96.8 7.9 %collective-permute-start.3 = (bf16[3,32,2,128]{3,1,0,2:T(8,128)(2,1)S(1)}, bf16[3,32,2,128]{3,1,0,2:T(8,128)(2,1)S(1)}, u32[]{:S(2)}, u32[]{:S(2)}) collective-permute-start(bf16[3,32,2,128]{3,1,0,2:T(8,128)(2,1)S(1)} %get-tuple-element.597), channel_id=1, source_target_pairs={{8,0},{16,8},{24,16},{32,24},{40,32},{48,40},{56,48},{64,56},{72,6... | collective-permute-start | bytes 147464 | tf_op jit(solution)/shard_map/ppermute | solution.py:32
  104.7 1.9 collective-permute-start.8
  107.0 0.8 copy-done.3
  107.8 7.9 %collective-permute-start.9 = (bf16[3,32,2,128]{3,1,0,2:T(8,128)(2,1)}, bf16[3,32,2,128]{3,1,0,2:T(8,128)(2,1)}, u32[]{:S(2)}, u32[]{:S(2)}) collective-permute-start(bf16[3,32,2,128]{3,1,0,2:T(8,128)(2,1)} %get-tuple-element.585), channel_id=1, source_target_pairs={{8,0},{16,8},{24,16},{32,24},{40,32},{48,40},{56,48},{64,56},{72,6... | collective-permute-start | bytes 147464 | tf_op jit(solution)/shard_map/ppermute | solution.py:32
  117.1 3.4 fusion.29
  120.6 0.8 pad_maximum_fusion
  121.4 3.6 all-to-all-start
  125.2 3.9 all-to-all-done
  130.0 8.4 %while.68 = (s32[]{:T(128)}, f32[2,128]{1,0:T(2,128)S(1)}, f32[2,3,2,128]{3,2,1,0:T(2,128)S(1)}, f32[64,2,128]{2,1,0:T(2,128)S(1)}, f32[64,2,3,2,128]{4,3,2,1,0:...) while((s32[]{:T(128)}, f32[2,128]{1,0:T(2,128)S(1)}, ...), condition=%wide.region_2.3_spmd.clone, body=%wide.region_1.2_spmd.clone.sunk | while | flops 7171 | bytes 52364 | solution.py:115
  138.4 0.8 broadcast.198.clone.1
  139.3 38.8 %while.69 = (s32[]{:T(128)}, f32[2,3,2,128]{3,2,1,0:T(2,128)S(1)}, f32[64,2,3,2,128]{4,3,2,1,0:T(2,128)}, f32[64,2,3,2,128]{4,3,2,1,0:T(2,128)S(1)}, f32[64,2,12...) while((s32[]{:T(128)}, f32[2,3,2,128]{3,2,1,0:T(2,128)S(1)}, ...), condition=%wide.region_4.5_spmd.clone, body=%wide.region_3.4_spmd.clone.sunk | while | flops 4612 | bytes 27763 | solution.py:124
  178.1 5.8 %all-to-all-start.1 = ((f32[6,64,2,128]{3,2,0,1:T(2,128)}), f32[6,64,2,128]{3,2,0,1:T(2,128)S(1)}, u32[]{:S(2)}, u32[]{:S(2)}) async-start(f32[6,64,2,128]{3,2,0,1:T(2,128)} %bitcast.22), calls=%async_computation.1 | async-start | bytes 786432 | tf_op jit(solution)/shard_map/all_to_all | solution.py:190
  184.3 0.8 copy-done.14
  185.2 0.8 copy-done.13
  187.1 0.8 copy-done.19
  187.9 0.8 copy-done.25
  188.8 0.8 copy-done.24
  189.6 0.8 copy-done.23
  190.6 0.9 maximum_convert_fusion.3
  193.3 1.3 collective-permute-start.10
  194.6 4.5 collective-permute-start.11
  199.1 1.9 collective-permute-start.6
  201.1 2.6 collective-permute-start.7
  204.2 9.9 %collective-permute-done.7 = f32[2,3,32,2,128]{4,3,2,1,0:T(2,128)S(1)} collective-permute-done((f32[2,3,32,2,128]{4,3,2,1,0:T(2,128)S(1)}, f32[2,3,32,2,128]{4,3,2,1,0:T(2,128)S(1)}, u32[]{:S(2)}, u32[]{:S(2)}) %collective-permute-start.7) | collective-permute-done | bytes 196640 | tf_op jit(solution)/shard_map/ppermute | solution.py:30
  214.1 2.3 fusion.20
  216.4 0.8 pad_maximum_fusion.1
  217.2 3.5 all-to-all-start.2
  220.7 4.2 all-to-all-done.2
  225.2 8.4 %while.70 = (s32[]{:T(128)}, f32[2,128]{1,0:T(2,128)S(1)}, f32[2,3,2,128]{3,2,1,0:T(2,128)S(1)}, f32[64,2,128]{2,1,0:T(2,128)S(1)}, f32[64,2,3,2,128]{4,3,2,1,0:...) while((s32[]{:T(128)}, f32[2,128]{1,0:T(2,128)S(1)}, ...), condition=%wide.region_7.8_spmd.clone, body=%wide.region_6.7_spmd.clone.sunk | while | flops 7171 | bytes 52364 | solution.py:115
  233.6 0.8 broadcast.198
  234.5 38.8 %while.71 = (s32[]{:T(128)}, f32[2,3,2,128]{3,2,1,0:T(2,128)S(1)}, f32[64,2,3,2,128]{4,3,2,1,0:T(2,128)}, f32[64,2,3,2,128]{4,3,2,1,0:T(2,128)S(1)}, f32[64,2,12...) while((s32[]{:T(128)}, f32[2,3,2,128]{3,2,1,0:T(2,128)S(1)}, ...), condition=%wide.region_9.10_spmd.clone, body=%wide.region_8.9_spmd.clone.sunk | while | flops 4612 | bytes 27763 | solution.py:124
  273.3 5.6 %all-to-all-start.3 = ((f32[6,64,2,128]{3,2,0,1:T(2,128)}), f32[6,64,2,128]{3,2,0,1:T(2,128)S(1)}, u32[]{:S(2)}, u32[]{:S(2)}) async-start(f32[6,64,2,128]{3,2,0,1:T(2,128)} %bitcast.50), calls=%async_computation.3 | async-start | bytes 786432 | tf_op jit(solution)/shard_map/all_to_all | solution.py:190
  279.0 0.8 copy-done.16
  280.0 2.8 all-to-all-done.3
  282.9 0.8 copy-done.26
  283.8 1.0 copy.166
  284.8 249.1 %psum.32 = f32[2]{0:T(128)S(1)} all-reduce(f32[2]{0:T(128)S(1)} %add.281), channel_id=1, replica_groups=mesh['tile'=64,'vert'=2,'dir'=4] {'tile','vert'}, use_global_device_ids=true, to_apply=%region_11.12 | all-reduce | flops 2 | bytes 16 | tf_op jit(solution)/shard_map/psum | solution.py:146
  (1087 shorter events, 107.0 us)
Async XLA Ops:
  7.2 18.4 %copy-start.27 = (bf16[4,4,32,4,128]{4,3,2,1,0:T(4,128)(2,1)S(1)}, bf16[4,4,32,4,128]{4,3,2,1,0:T(4,128)(2,1)}, u32[]{:S(2)}) copy-start(bf16[4,4,32,4,128]{4,3,2,1,0:T(4,128)(2,1)} %param.15) | copy-start | bytes 1572868
  7.2 72.8 %all-reduce.3.cloned.1.call-start = ((), (), s32[]{:S(2)}) async-start(), calls=%async_computation.4 | async-start | bytes 524288 | tf_op jit(solution)/shard_map/psum | solution.py:19
  9.3 6.0 %copy-start.31 = (s32[2]{0:T(128)S(1)}, s32[2]{0:T(128)}, u32[]{:S(2)}) copy-start(s32[2]{0:T(128)} %param.17) | copy-start | bytes 28
  9.3 106.7 %collective-permute-start = (f32[2,3,32,2,128]{4,3,2,1,0:T(2,128)}, f32[2,3,32,2,128]{4,3,2,1,0:T(2,128)}, u32[]{:S(2)}, u32[]{:S(2)}) collective-permute-start(f32[2,3,32,2,128]{4,3,2,1,0:T(2,128)} %get-tuple-element.562), channel_id=1, source_target_pairs={{8,0},{16,8},{24,16},{32,24},{40,32},{48,40},{56,48},{64,56},{72,6... | collective-permute-start | bytes 589832 | tf_op jit(solution)/shard_map/ppermute | solution.py:32
  13.3 102.7 %collective-permute-start.1 = (f32[2,3,32,2,128]{4,3,2,1,0:T(2,128)}, f32[2,3,32,2,128]{4,3,2,1,0:T(2,128)}, u32[]{:S(2)}, u32[]{:S(2)}) collective-permute-start(f32[2,3,32,2,128]{4,3,2,1,0:T(2,128)} %get-tuple-element.563), channel_id=1, source_target_pairs={{0,8},{8,16},{16,24},{24,32},{32,40},{40,48},{48,56},{56,64},{64,7... | collective-permute-start | bytes 589832 | tf_op jit(solution)/shard_map/ppermute | solution.py:30
  17.2 2.6 copy-start.30
  25.7 1.1 copy-start
  27.4 0.8 copy-start.21
  80.0 1.1 copy-start.2
  81.6 0.9 copy-start.1
  87.5 9.3 %collective-permute-start.4 = (bf16[9,1,4,128]{3,2,1,0:T(4,128)(2,1)S(1)}, bf16[9,1,4,128]{3,2,1,0:T(4,128)(2,1)S(1)}, u32[]{:S(2)}, u32[]{:S(2)}) collective-permute-start(bf16[9,1,4,128]{3,2,1,0:T(4,128)(2,1)S(1)} %get-tuple-element.566), channel_id=1, source_target_pairs={{0,4},{1,5},{2,6},{3,7},{8,12},{9,13},{10,14},{11,15},{16,20},{17,... | collective-permute-start | bytes 27656 | tf_op jit(solution)/shard_map/ppermute | solution.py:30
  88.8 15.9 %collective-permute-start.5 = (bf16[9,1,4,128]{3,2,1,0:T(4,128)(2,1)S(1)}, bf16[9,1,4,128]{3,2,1,0:T(4,128)(2,1)S(1)}, u32[]{:S(2)}, u32[]{:S(2)}) collective-permute-start(bf16[9,1,4,128]{3,2,1,0:T(4,128)(2,1)S(1)} %get-tuple-element.567), channel_id=1, source_target_pairs={{4,0},{5,1},{6,2},{7,3},{12,8},{13,9},{14,10},{15,11},{20,16},{21,... | collective-permute-start | bytes 27656 | tf_op jit(solution)/shard_map/ppermute | solution.py:32
  93.4 2.0 copy-start.15
  93.5 2.0 copy-start.17
  93.5 14.4 %collective-permute-start.2 = (bf16[3,32,2,128]{3,1,0,2:T(8,128)(2,1)S(1)}, bf16[3,32,2,128]{3,1,0,2:T(8,128)(2,1)S(1)}, u32[]{:S(2)}, u32[]{:S(2)}) collective-permute-start(bf16[3,32,2,128]{3,1,0,2:T(8,128)(2,1)S(1)} %get-tuple-element.596), channel_id=1, source_target_pairs={{0,8},{8,16},{16,24},{24,32},{32,40},{40,48},{48,56},{56,64},{64,7... | collective-permute-start | bytes 147464 | tf_op jit(solution)/shard_map/ppermute | solution.py:30
  96.8 18.9 %collective-permute-start.3 = (bf16[3,32,2,128]{3,1,0,2:T(8,128)(2,1)S(1)}, bf16[3,32,2,128]{3,1,0,2:T(8,128)(2,1)S(1)}, u32[]{:S(2)}, u32[]{:S(2)}) collective-permute-start(bf16[3,32,2,128]{3,1,0,2:T(8,128)(2,1)S(1)} %get-tuple-element.597), channel_id=1, source_target_pairs={{8,0},{16,8},{24,16},{32,24},{40,32},{48,40},{56,48},{64,56},{72,6... | collective-permute-start | bytes 147464 | tf_op jit(solution)/shard_map/ppermute | solution.py:32
  104.7 85.9 %collective-permute-start.8 = (bf16[3,32,2,128]{3,1,0,2:T(8,128)(2,1)}, bf16[3,32,2,128]{3,1,0,2:T(8,128)(2,1)}, u32[]{:S(2)}, u32[]{:S(2)}) collective-permute-start(bf16[3,32,2,128]{3,1,0,2:T(8,128)(2,1)} %get-tuple-element.584), channel_id=1, source_target_pairs={{0,8},{8,16},{16,24},{24,32},{32,40},{40,48},{48,56},{56,64},{64,7... | collective-permute-start | bytes 147464 | tf_op jit(solution)/shard_map/ppermute | solution.py:30
  107.0 0.9 copy-start.3
  107.8 82.8 %collective-permute-start.9 = (bf16[3,32,2,128]{3,1,0,2:T(8,128)(2,1)}, bf16[3,32,2,128]{3,1,0,2:T(8,128)(2,1)}, u32[]{:S(2)}, u32[]{:S(2)}) collective-permute-start(bf16[3,32,2,128]{3,1,0,2:T(8,128)(2,1)} %get-tuple-element.585), channel_id=1, source_target_pairs={{8,0},{16,8},{24,16},{32,24},{40,32},{48,40},{56,48},{64,56},{72,6... | collective-permute-start | bytes 147464 | tf_op jit(solution)/shard_map/ppermute | solution.py:32
  115.8 0.9 slice-start.1
  115.8 1.1 copy-start.4
  115.8 1.2 copy-start.5
  115.8 1.3 slice-start
  121.4 3.6 copy-start.12
  121.4 7.6 %all-to-all-start = ((f32[7,32,4,128]{3,1,0,2:T(8,128)}), f32[7,32,4,128]{3,1,0,2:T(8,128)S(1)}, u32[]{:S(2)}, u32[]{:S(2)}) async-start(f32[7,32,4,128]{3,1,0,2:T(8,128)} %pad_maximum_fusion), calls=%async_computation | async-start | bytes 917504 | tf_op jit(solution)/shard_map/all_to_all | solution.py:184
  138.4 45.5 %copy-start.10 = (f32[3,32,4,1]{3,1,0,2:T(8,128)S(1)}, f32[3,32,4,1]{3,1,0,2:T(8,128)}, u32[]{:S(2)}) copy-start(f32[3,32,4,1]{3,1,0,2:T(8,128)} %get-tuple-element.592) | copy-start | bytes 4612
  138.4 45.5 %copy-start.11 = (f32[3,32,4,1]{3,1,0,2:T(8,128)S(1)}, f32[3,32,4,1]{3,1,0,2:T(8,128)}, u32[]{:S(2)}) copy-start(f32[3,32,4,1]{3,1,0,2:T(8,128)} %get-tuple-element.593) | copy-start | bytes 4612
  178.1 5.8 %copy-start.6 = (f32[3,32,4,2]{3,1,0,2:T(8,128)S(1)}, f32[3,32,4,2]{3,1,0,2:T(8,128)}, u32[]{:S(2)}) copy-start(f32[3,32,4,2]{3,1,0,2:T(8,128)} %get-tuple-element.588) | copy-start | bytes 9220
  178.1 5.8 %copy-start.7 = (f32[3,32,4,2]{3,1,0,2:T(8,128)S(1)}, f32[3,32,4,2]{3,1,0,2:T(8,128)}, u32[]{:S(2)}) copy-start(f32[3,32,4,2]{3,1,0,2:T(8,128)} %get-tuple-element.589) | copy-start | bytes 9220
  178.1 5.8 %copy-start.8 = (f32[3,32,4,126]{3,1,0,2:T(8,128)S(1)}, f32[3,32,4,126]{3,1,0,2:T(8,128)}, u32[]{:S(2)}) copy-start(f32[3,32,4,126]{3,1,0,2:T(8,128)} %get-tuple-element.590) | copy-start | bytes 580612
  178.1 5.8 %copy-start.9 = (f32[3,32,4,126]{3,1,0,2:T(8,128)S(1)}, f32[3,32,4,126]{3,1,0,2:T(8,128)}, u32[]{:S(2)}) copy-start(f32[3,32,4,126]{3,1,0,2:T(8,128)} %get-tuple-element.591) | copy-start | bytes 580612
  178.1 13.6 %all-to-all-start.1 = ((f32[6,64,2,128]{3,2,0,1:T(2,128)}), f32[6,64,2,128]{3,2,0,1:T(2,128)S(1)}, u32[]{:S(2)}, u32[]{:S(2)}) async-start(f32[6,64,2,128]{3,2,0,1:T(2,128)} %bitcast.22), calls=%async_computation.1 | async-start | bytes 786432 | tf_op jit(solution)/shard_map/all_to_all | solution.py:190
  184.3 0.8 copy-start.14
  185.1 0.8 copy-start.13
  186.2 0.8 copy-start.20
  187.0 0.8 copy-start.19
  187.9 0.8 copy-start.25
  188.7 0.8 copy-start.24
  193.3 10.4 %collective-permute-start.10 = (bf16[9,1,4,128]{3,2,1,0:T(4,128)(2,1)S(1)}, bf16[9,1,4,128]{3,2,1,0:T(4,128)(2,1)S(1)}, u32[]{:S(2)}, u32[]{:S(2)}) collective-permute-start(bf16[9,1,4,128]{3,2,1,0:T(4,128)(2,1)S(1)} %get-tuple-element.564), channel_id=1, source_target_pairs={{0,4},{1,5},{2,6},{3,7},{8,12},{9,13},{10,14},{11,15},{16,20},{17,... | collective-permute-start | bytes 27656 | tf_op jit(solution)/shard_map/ppermute | solution.py:30
  194.6 9.2 %collective-permute-start.11 = (bf16[9,1,4,128]{3,2,1,0:T(4,128)(2,1)S(1)}, bf16[9,1,4,128]{3,2,1,0:T(4,128)(2,1)S(1)}, u32[]{:S(2)}, u32[]{:S(2)}) collective-permute-start(bf16[9,1,4,128]{3,2,1,0:T(4,128)(2,1)S(1)} %get-tuple-element.565), channel_id=1, source_target_pairs={{4,0},{5,1},{6,2},{7,3},{12,8},{13,9},{14,10},{15,11},{20,16},{21,... | collective-permute-start | bytes 27656 | tf_op jit(solution)/shard_map/ppermute | solution.py:32
  199.1 5.1 collective-permute-start.6
  201.1 13.0 %collective-permute-start.7 = (f32[2,3,32,2,128]{4,3,2,1,0:T(2,128)S(1)}, f32[2,3,32,2,128]{4,3,2,1,0:T(2,128)S(1)}, u32[]{:S(2)}, u32[]{:S(2)}) collective-permute-start(f32[2,3,32,2,128]{4,3,2,1,0:T(2,128)S(1)} %get-tuple-element.549), channel_id=1, source_target_pairs={{0,8},{8,16},{16,24},{24,32},{32,40},{40,48},{48,56},{56,64},{64,7... | collective-permute-start | bytes 589832 | tf_op jit(solution)/shard_map/ppermute | solution.py:30
  217.2 7.7 %all-to-all-start.2 = ((f32[7,32,4,128]{3,1,0,2:T(8,128)}), f32[7,32,4,128]{3,1,0,2:T(8,128)S(1)}, u32[]{:S(2)}, u32[]{:S(2)}) async-start(f32[7,32,4,128]{3,1,0,2:T(8,128)} %pad_maximum_fusion.1), calls=%async_computation.2 | async-start | bytes 917504 | tf_op jit(solution)/shard_map/all_to_all | solution.py:184
  273.3 5.6 %copy-start.22 = (f32[32,4,128]{2,0,1:T(8,128)S(1)}, f32[32,4,128]{2,0,1:T(8,128)}, u32[]{:S(2)}) copy-start(f32[32,4,128]{2,0,1:T(8,128)} %get-tuple-element.529) | copy-start | bytes 196612
  273.3 9.5 %all-to-all-start.3 = ((f32[6,64,2,128]{3,2,0,1:T(2,128)}), f32[6,64,2,128]{3,2,0,1:T(2,128)S(1)}, u32[]{:S(2)}, u32[]{:S(2)}) async-start(f32[6,64,2,128]{3,2,0,1:T(2,128)} %bitcast.50), calls=%async_computation.3 | async-start | bytes 786432 | tf_op jit(solution)/shard_map/all_to_all | solution.py:190
  278.9 0.8 copy-start.16
  278.9 0.9 copy-start.18
  282.8 0.8 copy-start.26
  (3 other events, 2.2 us)
Sparse Core Ops, SparseCore 0:
  26.6 53.2 all-reduce.2
where the time goes:
time: 543 us; the launch traced here: 541 us
  blocking collectives  249 us (46%)
  other arithmetic  96.4 us (18%)
  waiting for transfers between devices  70.2 us (13%)
  starting transfers between devices  60.2 us (11%)
  local copies, waits for them, and re-layouts  34.6 us (6%)
  between operations  24.3 us (4%)
  loops' own time  6.45 us (1%)
    psum x1, blocking collectives, add_power(): return power_sum + lax.psum(power_term, ('tile', 'vert'))  249 us
    dynamic_update_slice x384, other arithmetic, column_solve(): lax.scan(forward, initial, (coeff_below, diagonal_main, coeff_above, leve...  82.3 us
    psum x1, waiting for transfers between devices, from_root(): return lax.psum(block, axis)  49.4 us
    ppermute x6, starting transfers between devices, padded_2(): lax.ppermute(head, axis, [((i + 1) % count, i) for i in range(ends)])  30.7 us
    unnamed x65, local copies, waits for them, and re-layouts  12.2 us
    all_to_all x2, starting transfers between devices, shards(): lax.all_to_all(solved.reshape(3 * directions, levels_all, x_local, y_loca...  11.4 us
    ppermute x6, starting transfers between devices, padded_2(): lax.ppermute(tail, axis, [(i, (i + 1) % count) for i in range(ends)])  10.9 us
  transfers between devices with their start and end apart: 17, of which 5 were waited for; matrix products, arithmetic and copies ran while one was open for 12% of the time, Pallas kernels for 0%

commit v1 on v0

v1 whole, which is shorter than its diff:
```python
import functools
import math

import jax
import jax.numpy as jnp
from jax import lax
from jax.experimental import pallas as pl
from jax.experimental.pallas import tpu as pltpu
from jax.sharding import Mesh
from jax.sharding import PartitionSpec as P

STEPS = 2
TIME_STEP = 0.05
DRAG_COEFF = 0.5
POWER_SCALE = 0.01
VERTICAL_ASPECT = 400.0
TILE = ("row", "core")
HALF = 0.5 * TIME_STEP
FACE = 0.5 * TIME_STEP * VERTICAL_ASPECT

RHS, DIAG, VISC, WIND, RAW, DIAG2, VISC2, WIND2, WROW, FIELDS = 0, 6, 7, 8, 11, 17, 18, 19, 22, 24


def window(ref, field, level, offset=0):
    return ref[field, level, 2 + offset : 10 + offset, :]


def roll_y(values, offset):
    return pltpu.roll(values, (-offset) % values.shape[-1], 1)


def wind_terms(winds, turbines, level, above, below, sign, beyond=None):
    wind = [window(winds, c, level) for c in range(3)]
    visc = TIME_STEP * window(winds, 3, level)
    mask = turbines[level, 2:10, :]
    turbine = jnp.where(mask > 0.5, 1.0, 0.0)
    square = wind[0] * wind[0] + wind[1] * wind[1]
    inverse = lax.rsqrt(square)
    speed = square * inverse
    drag = (DRAG_COEFF * TIME_STEP) * turbine
    along = drag * inverse
    by_first, by_second, by_third = [], [], []
    for c in range(3):
        near = window(winds, c, level, 1) - window(winds, c, level, -1)
        far = window(winds, c, level, 2) - window(winds, c, level, -2)
        slope = (TIME_STEP * 8.0 / 12.0) * near - (TIME_STEP / 12.0) * far
        by_first.append(slope + along * wind[c] * wind[0])
        near = roll_y(wind[c], 1) - roll_y(wind[c], -1)
        far = roll_y(wind[c], 2) - roll_y(wind[c], -2)
        slope = (TIME_STEP * 8.0 / 12.0) * near - (TIME_STEP / 12.0) * far
        by_second.append(slope + along * wind[c] * wind[1])
        vertical = jnp.zeros_like(speed)
        if beyond is not None:
            vertical = vertical + beyond[c]
        elif above is not None:
            vertical = vertical + window(winds, c, above)
        if below is not None:
            vertical = vertical - window(winds, c, below)
        by_third.append((HALF * sign) * vertical)
    first = (TIME_STEP * 8.0 / 12.0) * wind[0]
    second = (TIME_STEP * 8.0 / 12.0) * wind[1]
    return dict(
        wind=wind,
        mask=mask,
        turbine=turbine,
        speed=speed,
        center=1.0 - 4.0 * visc - drag * speed,
        x_up=visc - first,
        x_down=visc + first,
        x_far=0.125 * first,
        y_up=visc - second,
        y_down=visc + second,
        y_far=0.125 * second,
        z=(HALF * sign) * wind[2],
        by=(by_first, by_second, by_third),
    )


def right_side(tangents, weights, terms, level, above, below, beyond=None):
    speed_step = TIME_STEP * terms["speed"]
    groups = weights.shape[1]
    hits = [terms["mask"] == float(g + 1) for g in range(groups)]
    rows = []
    for d in range(weights.shape[0]):
        source = jnp.zeros_like(speed_step)
        for g in range(groups):
            source = jnp.where(hits[g], weights[d, g], source)
        force = source * speed_step
        own = [window(tangents, 3 * d + i, level) for i in range(3)]
        for i in range(3):
            field = 3 * d + i
            value = terms["center"] * own[i]
            value += terms["x_up"] * window(tangents, field, level, 1)
            value += terms["x_down"] * window(tangents, field, level, -1)
            value += terms["x_far"] * (
                window(tangents, field, level, 2) - window(tangents, field, level, -2)
            )
            value += terms["y_up"] * roll_y(own[i], 1)
            value += terms["y_down"] * roll_y(own[i], -1)
            value += terms["y_far"] * (roll_y(own[i], 2) - roll_y(own[i], -2))
            vertical = None
            if beyond is not None:
                vertical = beyond[field]
            elif above is not None:
                vertical = window(tangents, field, above)
            if below is not None:
                lower = window(tangents, field, below)
                vertical = -lower if vertical is None else vertical - lower
            if vertical is not None:
                value -= terms["z"] * vertical
            for c in range(3):
                value -= terms["by"][c][i] * own[c]
            value -= force * terms["wind"][i]
            rows.append(value)
    return rows


def first_kernel(place, weights, left, own, right, low, high, rec_a, rec_b, groups,
                 message, ratio_out, value_out, power_out, ratio2_out, inverse2_out, face2_out,
                 wrow_out, tangents, winds, winds2, turbines):
    levels = own.shape[2]
    last = levels - 1
    sign = place[0].astype(jnp.float32)
    base = place[1]
    step = place[0]

    def at(j):
        return base + step * j

    for field in range(6):
        d, i = divmod(field, 3)
        tangents[field, :, 0:4, :] = left[d, i]
        tangents[field, :, 4:8, :] = own[d, i]
        tangents[field, :, 8:12, :] = right[d, i]
    for c in range(4):
        winds[c, :, 0:4, :] = low[c].astype(jnp.float32)
        winds[c, :, 4:8, :] = rec_a[c].astype(jnp.float32)
        winds[c, :, 8:12, :] = high[c].astype(jnp.float32)
        winds2[c, :, 4:8, :] = rec_b[c].astype(jnp.float32)
    turbines[:, 0:4, :] = low[7].astype(jnp.float32)
    turbines[:, 4:8, :] = groups[...].astype(jnp.float32)
    turbines[:, 8:12, :] = high[7].astype(jnp.float32)

    def level_rows(j, above, below):
        k = at(j)
        terms = wind_terms(winds, turbines, k, above, below, sign)
        rows = right_side(tangents, weights, terms, k, above, below)
        for c in range(2):
            power_out[c, k] = terms["turbine"] * terms["speed"] * terms["wind"][c]
        wind2 = [window(winds2, c, k) for c in range(2)]
        square = wind2[0] * wind2[0] + wind2[1] * wind2[1]
        scale = terms["turbine"] * (square * lax.rsqrt(square))
        return rows, [scale * wind2[0], scale * wind2[1]]

    def eliminate(j, above, below, carry):
        face_prev, ratio_prev, values_prev, face2_prev, ratio2_prev, w_prev = carry
        k = at(j)
        rows, wrows = level_rows(j, above, below)
        face = FACE * (window(winds, 3, k) + window(winds, 3, above))
        inverse = 1.0 / (1.0 + face + face_prev * (1.0 - ratio_prev))
        ratio = face * inverse
        values = [(r + face_prev * v) * inverse for r, v in zip(rows, values_prev)]
        ratio_out[k] = ratio
        for field in range(6):
            value_out[field, k] = values[field]
        face2 = FACE * (window(winds2, 3, k) + window(winds2, 3, above))
        inverse2 = 1.0 / (1.0 + face2 + face2_prev * (1.0 - ratio2_prev))
        ratio2 = face2 * inverse2
        ws = [(r + face2_prev * v) * inverse2 for r, v in zip(wrows, w_prev)]
        ratio2_out[k] = ratio2
        inverse2_out[k] = inverse2
        face2_out[k] = face2
        for c in range(2):
            wrow_out[c, k] = ws[c]
        return face, ratio, tuple(values), face2, ratio2, tuple(ws)

    zero = jnp.zeros((8, own.shape[4]), jnp.float32)
    carry = (
        (2.0 * FACE) * window(winds, 3, at(0)), zero, (zero,) * 6,
        (2.0 * FACE) * window(winds2, 3, at(0)), zero, (zero,) * 2,
    )
    carry = eliminate(0, at(1), None, carry)
    carry = lax.fori_loop(
        1, last, lambda j, c: eliminate(j, at(j + 1), at(j - 1), c), carry
    )
    face, ratio, values, face2, ratio2, ws = carry
    k = at(last)
    rows, wrows = level_rows(last, None, at(last - 1))
    for field in range(6):
        message[RHS + field] = rows[field] + face * values[field]
        message[RAW + field] = window(tangents, field, k)
    message[DIAG] = 1.0 + face * (1.0 - ratio)
    message[VISC] = window(winds, 3, k)
    message[DIAG2] = 1.0 + face2 * (1.0 - ratio2)
    message[VISC2] = window(winds2, 3, k)
    for c in range(3):
        message[WIND + c] = window(winds, c, k)
        message[WIND2 + c] = window(winds2, c, k)
    for c in range(2):
        message[WROW + c] = wrows[c] + face2 * ws[c]


def second_kernel(place, weights, mine, theirs, ratio_in, value_in, power_in, ratio2_in, inverse2_in,
                  face2_in, wrow_in, low, high, rec_b, groups,
                  row_out, value_out, middle_out, sums_out, tangents, winds, turbines, adjoint):
    levels = rec_b.shape[1]
    last = levels - 1
    sign = place[0].astype(jnp.float32)
    base = place[1]
    step = place[0]

    def at(j):
        return base + step * j

    for c in range(3):
        winds[c, :, 0:4, :] = low[4 + c].astype(jnp.float32)
        winds[c, :, 8:12, :] = high[4 + c].astype(jnp.float32)
    for c in range(4):
        winds[c, :, 4:8, :] = rec_b[c].astype(jnp.float32)
    turbines[:, 4:8, :] = groups[...].astype(jnp.float32)

    zero = jnp.zeros((8, rec_b.shape[3]), jnp.float32)
    layer = lax.broadcasted_iota(jnp.int32, zero.shape, 0)
    inside = jnp.logical_and(layer >= place[2], layer < place[3])
    center = jnp.logical_and(layer >= 2, layer < 6)

    face = FACE * (mine[VISC] + theirs[VISC])
    pivot, pivot_far = mine[DIAG] + face, theirs[DIAG] + face
    inverse = 1.0 / (pivot * pivot_far - face * face)
    nexts, beyond = [], []
    for field in range(6):
        d, i = divmod(field, 3)
        row = mine[RHS + field] - (HALF * sign) * (
            mine[WIND + 2] * theirs[RAW + field] + mine[RAW + 3 * d + 2] * theirs[WIND + i]
        )
        row_far = theirs[RHS + field] + (HALF * sign) * (
            theirs[WIND + 2] * mine[RAW + field] + theirs[RAW + 3 * d + 2] * mine[WIND + i]
        )
        nexts.append(jnp.where(inside, (row * pivot_far + face * row_far) * inverse, 0.0))
        beyond.append(jnp.where(inside, (row_far * pivot + face * row) * inverse, 0.0))
    face2 = FACE * (mine[VISC2] + theirs[VISC2])
    pivot, pivot_far = mine[DIAG2] + face2, theirs[DIAG2] + face2
    inverse = 1.0 / (pivot * pivot_far - face2 * face2)
    near_part, far_part = pivot_far * inverse, face2 * inverse
    middle_out[0] = near_part
    middle_out[1] = far_part
    ws = [near_part * mine[WROW + c] + far_part * theirs[WROW + c] for c in range(2)]

    def keep(k, values, ws, sums):
        for field in range(6):
            tangents[field, k, 2:10, :] = values[field]
        for c in range(2):
            adjoint[c, k] = ws[c]
        return tuple(
            sums[d] + power_in[0, k] * values[3 * d] + power_in[1, k] * values[3 * d + 1]
            for d in range(2)
        )

    sums = keep(at(last), nexts, ws, (zero, zero))

    def back(n, carry):
        values, ws, sums = carry
        k = at(last - 1 - n)
        ratio = ratio_in[k]
        values = tuple(
            jnp.where(inside, value_in[f, k] + ratio * values[f], 0.0) for f in range(6)
        )
        ratio2 = ratio2_in[k]
        ws = tuple(wrow_in[c, k] + ratio2 * ws[c] for c in range(2))
        return values, ws, keep(k, values, ws, sums)

    _, _, sums = lax.fori_loop(0, last, back, (tuple(nexts), tuple(ws), sums))

    def level_rows(j, above, below, sums, winds_beyond=None, values_beyond=None):
        k = at(j)
        terms = wind_terms(winds, turbines, k, above, below, sign, winds_beyond)
        rows = right_side(tangents, weights, terms, k, above, below, values_beyond)
        sums = tuple(
            sums[d] + adjoint[0, k] * rows[3 * d] + adjoint[1, k] * rows[3 * d + 1]
            for d in range(2)
        )
        return rows, sums

    def eliminate(j, above, below, carry):
        face_prev, values_prev, sums = carry
        k = at(j)
        rows, sums = level_rows(j, above, below, sums)
        inverse = inverse2_in[k]
        values = tuple((r + face_prev * v) * inverse for r, v in zip(rows, values_prev))
        for field in range(6):
            value_out[field, k] = values[field]
        return face2_in[k], values, sums

    carry = eliminate(0, at(1), None, (zero, (zero,) * 6, sums))
    face, values, sums = lax.fori_loop(
        1, last, lambda j, c: eliminate(j, at(j + 1), at(j - 1), c), carry
    )
    rows, sums = level_rows(
        last, None, at(last - 1), sums, [theirs[WIND2 + c] for c in range(3)], beyond
    )
    for field in range(6):
        row_out[field] = rows[field] + face * values[field]
    for d in range(2):
        sums_out[d : d + 1, :] = jnp.sum(jnp.where(center, sums[d], 0.0), axis=0, keepdims=True)


def third_kernel(place, mine, theirs, middle, ratio_in, value_in, out):
    levels = ratio_in.shape[0]
    last = levels - 1
    base = place[1]
    step = place[0]
    values = tuple(middle[0] * mine[f] + middle[1] * theirs[f] for f in range(6))

    def keep(k, values):
        for field in range(6):
            d, i = divmod(field, 3)
            out[d, i, k] = values[field][2:6]

    keep(base + step * last, values)

    def back(n, values):
        k = base + step * (last - 1 - n)
        ratio = ratio_in[k]
        values = tuple(value_in[f, k] + ratio * values[f] for f in range(6))
        keep(k, values)
        return values

    lax.fori_loop(0, last, back, values)


def call(kernel, scalars, arrays, outs, scratch):
    return pl.pallas_call(
        kernel,
        out_shape=[jax.ShapeDtypeStruct(shape, jnp.float32) for shape in outs],
        in_specs=[pl.BlockSpec(memory_space=pltpu.SMEM)] * len(scalars)
        + [pl.BlockSpec(memory_space=pltpu.VMEM)] * len(arrays),
        out_specs=[pl.BlockSpec(memory_space=pltpu.VMEM)] * len(outs),
        scratch_shapes=[pltpu.VMEM(shape, jnp.float32) for shape in scratch],
        compiler_params=pltpu.CompilerParams(vmem_limit_bytes=40 * 1024 * 1024),
    )(*scalars, *arrays)


def fetch_records(first, second, owner_first, owner_second):
    count = lax.axis_size("dir")
    here = lax.axis_index("dir")

    def spread(record, owner):
        result = record
        for k in range(1, count):
            target = (owner + k) % count
            got = lax.ppermute(record, "dir", [(owner, target)])
            result = jnp.where(here == target, got, result)
        return result

    def branch(a, b):
        return lambda x, y: (spread(x, a), spread(y, b))

    branches = [branch(a, b) for a in range(count) for b in range(count)]
    return lax.switch(owner_first * count + owner_second, branches, first, second)


def shards(tangent_in, records, record_slot, step_record, turbine_mask, group_weights):
    directions, components, levels, layers, spans = tangent_in.shape
    fields = directions * components
    tiles = lax.axis_size("row") * lax.axis_size("core")
    tile = lax.axis_index("row") * lax.axis_size("core") + lax.axis_index("core")
    vert = lax.axis_index("vert")
    up = [(i, i + 1) for i in range(tiles - 1)]
    down = [(i + 1, i) for i in range(tiles - 1)]
    swap = [(0, 1), (1, 0)]
    per_device = records.shape[0]

    left = lax.ppermute(tangent_in, TILE, up)
    right = lax.ppermute(tangent_in, TILE, down)

    slots = [record_slot[step_record[s]] for s in range(STEPS)]
    stored = [lax.dynamic_index_in_dim(records, s % per_device, 0, keepdims=False) for s in slots]
    rec_a, rec_b = fetch_records(*stored, *[s // per_device for s in slots])

    edge = jnp.concatenate([rec_a, rec_b[:3], turbine_mask.astype(jnp.bfloat16)[None]], axis=0)
    low = lax.ppermute(edge, TILE, up)
    high = lax.ppermute(edge, TILE, down)

    place = jnp.stack([
        1 - 2 * vert,
        vert * (levels - 1),
        jnp.where(tile == 0, 2, 0),
        jnp.where(tile == tiles - 1, 6, 8),
    ]).astype(jnp.int32)

    def block(*lead):
        return (*lead, 8, spans)

    def wide(*lead):
        return (*lead, 16, spans)

    message, ratio, value, power, ratio2, inverse2, face2, wrow = call(
        first_kernel,
        (place, group_weights),
        (left, tangent_in, right, low, high, rec_a, rec_b, turbine_mask),
        (block(FIELDS), block(levels), block(fields, levels), block(2, levels),
         block(levels), block(levels), block(levels), block(2, levels)),
        (wide(fields, levels), wide(4, levels), wide(4, levels), wide(levels)),
    )
    answer = lax.ppermute(message, "vert", swap)
    row, value2, middle, sums = call(
        second_kernel,
        (place, group_weights),
        (message, answer, ratio, value, power, ratio2, inverse2, face2, wrow, low, high, rec_b, turbine_mask),
        (block(fields), block(fields, levels), block(2), (directions, spans)),
        (wide(fields, levels), wide(4, levels), wide(levels), block(2, levels)),
    )
    answer2 = lax.ppermute(row, "vert", swap)

    sums = lax.psum(sums, "core")
    count = lax.axis_size("row") * lax.axis_size("vert")
    gathered = lax.all_to_all(
        jnp.broadcast_to(sums[None], (count, directions, spans)), ("row", "vert"), 0, 0, tiled=True
    )
    cells = levels * lax.axis_size("vert") * layers * tiles * spans
    power_out = jnp.sum(gathered, axis=(0, 2)) * (POWER_SCALE / math.sqrt(cells))

    (tangent_out,) = call(
        third_kernel,
        (place,),
        (row, answer2, middle, ratio2, value2),
        (tangent_in.shape,),
        (),
    )
    return tangent_out, power_out


def solution(mesh):
    tiles, verts, dirs = mesh.devices.shape
    fine = Mesh(mesh.devices.reshape(tiles // 2, 2, verts, dirs), (*TILE, "vert", "dir"))
    in_specs = (
        P("dir", None, "vert", TILE, None),
        P("dir", None, "vert", TILE, None),
        P(),
        P(),
        P("vert", TILE, None),
        P("dir", None),
    )
    out_specs = (P("dir", None, "vert", TILE, None), P("dir"))
    return jax.shard_map(shards, mesh=fine, in_specs=in_specs, out_specs=out_specs, check_vma=False)
```

time: 543 us -> 100 us (0.18)
  the two profiles are of different devices: /device:TPU:320 before, /device:TPU:1 now
where the time goes in v1:
time: 100 us; the launch traced here: 99.7 us
  starting transfers between devices  53.8 us (54%)
  waiting for transfers between devices  15.3 us (15%)
  Pallas kernels  11.8 us (12%)
  between operations  9.93 us (10%)
  local copies, waits for them, and re-layouts  4.51 us (5%)
  blocking collectives  2.48 us (2%)
  other arithmetic  1.7 us (2%)
    all_to_all x1, starting transfers between devices, shards(): lax.all_to_all(jnp.broadcast_to(sums[None], (count, directions, spans)),...  23.3 us
    pallas_call x3, Pallas kernels, call(): pl.pallas_call(kernel, out_shape=[jax.ShapeDtypeStruct(shape, jnp.float32...  11.8 us
    ppermute x6, starting transfers between devices, spread(): got = lax.ppermute(record, 'dir', [(owner, target)])  10.1 us
    ppermute x1, starting transfers between devices, shards(): left = lax.ppermute(tangent_in, TILE, up)  5.19 us
    all_to_all x1, waiting for transfers between devices, shards(): lax.all_to_all(jnp.broadcast_to(sums[None], (count, directions, spans)),...  4.45 us
    ppermute x1, starting transfers between devices, shards(): answer = lax.ppermute(message, 'vert', swap)  4 us
    ppermute x1, starting transfers between devices, shards(): low = lax.ppermute(edge, TILE, up)  3.64 us
    ppermute x6, waiting for transfers between devices, spread(): got = lax.ppermute(record, 'dir', [(owner, target)])  3.59 us
  transfers between devices with their start and end apart: 13, of which 5 were waited for; matrix products, arithmetic and copies ran while one was open for 2% of the time, Pallas kernels for 2%

profile of v1, /device:TPU:1, one launch (start us, length us, event | category | flops | bytes accessed | tf_op | source)
XLA Modules:
  0.0 99.7 jit_solution(5775722975269856234)
XLA Ops:
  0.6 0.0 copy-start.4
  0.6 0.6 copy-done.4
  1.3 0.6 fusion.1
  5.1 0.0 copy-start.3
  5.8 0.0 copy-done.3
  5.8 0.6 fusion
  11.6 0.0 copy-start.1
  11.6 0.0 copy-start
  11.6 16.6 %conditional.1 = (bf16[4,32,4,128]{3,2,1,0:T(4,128)(2,1)S(1)}, bf16[4,32,4,128]{3,2,1,0:T(4,128)(2,1)}, bf16[3,32,4,128]{3,2,1,0:T(4,128)(2,1)S(1)}) conditional(s32[]{:T(128)} %clamp.3, (s32[]{:T(128)}, s32[]{:T(128)}, bf16[4,4,32,4,128]{4,3,2,1,0:T(4,128)(2,1)}, s32[]{:T(128)}) %tuple.88, (s32[]{:T(128)}, ...), branch_computations={%region_0.1_spmd, %region_1.2_spmd, %region_2.3_spmd, %region_3.4_... | conditional | flops 393226 | bytes 5177726 | solution.py:359
  11.7 1.1 %dynamic-slice_bitcast_fusion.16 = (bf16[4,32,4,128]{3,2,1,0:T(4,128)(2,1)S(1)}, bf16[4,32,4,128]{3,2,1,0:T(4,128)(2,1)S(1)}) fusion(bf16[4,4,32,4,128]{4,3,2,1,0:T(4,128)(2,1)} %get-tuple-element.498, s32[]{:T(128)S(6)} %select_n.541, s32[]{:T(128)S(6)} %select_n.535), kind=kLoop, calls=%fused_computation.33 | loop fusion | bytes 524296 | tf_op jit(solution)/shard_map/jit(dynamic_index_in_dim)/squeeze | solution.py:377
  12.8 4.0 %collective-permute-start.53 = (bf16[4,32,4,128]{3,2,1,0:T(4,128)(2,1)S(1)}, bf16[4,32,4,128]{3,2,1,0:T(4,128)(2,1)S(1)}, u32[]{:S(2)}, u32[]{:S(2)}) collective-permute-start(bf16[4,32,4,128]{3,2,1,0:T(4,128)(2,1)S(1)} %get-tuple-element.577), channel_id=1, source_target_pairs={{0,1},{4,5},{8,9},{12,13},{16,17},{20,21},{24,25},{28,29},{32,33},... | collective-permute-start | bytes 393224 | tf_op jit(solution)/shard_map/cond/branch_8_fun/ppermute | solution.py:351
  16.7 2.2 %collective-permute-start.52 = (bf16[4,32,4,128]{3,2,1,0:T(4,128)(2,1)S(1)}, bf16[4,32,4,128]{3,2,1,0:T(4,128)(2,1)S(1)}, u32[]{:S(2)}, u32[]{:S(2)}) collective-permute-start(bf16[4,32,4,128]{3,2,1,0:T(4,128)(2,1)S(1)} %get-tuple-element.577), channel_id=1, source_target_pairs={{0,2},{4,6},{8,10},{12,14},{16,18},{20,22},{24,26},{28,30},{32,34}... | collective-permute-start | bytes 393224 | tf_op jit(solution)/shard_map/cond/branch_8_fun/ppermute | solution.py:351
  19.0 1.3 %collective-permute-start.51 = (bf16[4,32,4,128]{3,2,1,0:T(4,128)(2,1)S(1)}, bf16[4,32,4,128]{3,2,1,0:T(4,128)(2,1)S(1)}, u32[]{:S(2)}, u32[]{:S(2)}) collective-permute-start(bf16[4,32,4,128]{3,2,1,0:T(4,128)(2,1)S(1)} %get-tuple-element.577), channel_id=1, source_target_pairs={{0,3},{4,7},{8,11},{12,15},{16,19},{20,23},{24,27},{28,31},{32,35}... | collective-permute-start | bytes 393224 | tf_op jit(solution)/shard_map/cond/branch_8_fun/ppermute | solution.py:351
  20.3 0.7 collective-permute-start.50
  20.9 1.3 %collective-permute-start.49 = (bf16[4,32,4,128]{3,2,1,0:T(4,128)(2,1)S(1)}, bf16[4,32,4,128]{3,2,1,0:T(4,128)(2,1)S(1)}, u32[]{:S(2)}, u32[]{:S(2)}) collective-permute-start(bf16[4,32,4,128]{3,2,1,0:T(4,128)(2,1)S(1)} %get-tuple-element.578), channel_id=1, source_target_pairs={{2,0},{6,4},{10,8},{14,12},{18,16},{22,20},{26,24},{30,28},{34,32}... | collective-permute-start | bytes 393224 | tf_op jit(solution)/shard_map/cond/branch_8_fun/ppermute | solution.py:351
  22.2 0.0 collective-permute-done.53
  22.3 0.7 collective-permute-start.48
  22.9 0.0 collective-permute-done.52
  22.9 0.0 collective-permute-done.51
  23.0 0.7 select_select_fusion.16
  23.6 0.9 slice.65
  24.6 0.0 collective-permute-done.50
  24.6 3.6 %collective-permute-done.49 = bf16[4,32,4,128]{3,2,1,0:T(4,128)(2,1)S(1)} collective-permute-done((bf16[4,32,4,128]{3,2,1,0:T(4,128)(2,1)S(1)}, bf16[4,32,4,128]{3,2,1,0:T(4,128)(2,1)S(1)}, u32[]{:S(2)}, u32[]{:S(2)}) %collective-permute-start.49) | collective-permute-done | bytes 131104 | tf_op jit(solution)/shard_map/cond/branch_8_fun/ppermute | solution.py:351
  28.2 0.0 collective-permute-done.48
  28.2 0.0 copy-done.1
  28.2 5.2 %collective-permute-start.96 = (f32[2,3,32,4,128]{4,3,2,1,0:T(4,128)S(1)}, f32[2,3,32,4,128]{4,3,2,1,0:T(4,128)S(1)}, u32[]{:S(2)}, u32[]{:S(2)}) collective-permute-start(f32[2,3,32,4,128]{4,3,2,1,0:T(4,128)S(1)} %copy-done.1), channel_id=1, source_target_pairs={{0,8},{8,16},{16,24},{24,32},{32,40},{40,48},{48,56},{56,64},{64,7... | collective-permute-start | bytes 1179656 | tf_op jit(solution)/shard_map/ppermute | solution.py:373
  33.4 2.7 %collective-permute-start.97 = (f32[2,3,32,4,128]{4,3,2,1,0:T(4,128)S(1)}, f32[2,3,32,4,128]{4,3,2,1,0:T(4,128)S(1)}, u32[]{:S(2)}, u32[]{:S(2)}) collective-permute-start(f32[2,3,32,4,128]{4,3,2,1,0:T(4,128)S(1)} %copy-done.1), channel_id=1, source_target_pairs={{8,0},{16,8},{24,16},{32,24},{40,32},{48,40},{56,48},{64,56},{72,6... | collective-permute-start | bytes 1179656 | tf_op jit(solution)/shard_map/ppermute | solution.py:374
  36.1 0.2 pad_maximum_fusion
  36.3 1.9 %collective-permute-start.99 = (bf16[8,32,4,128]{3,2,1,0:T(4,128)(2,1)S(1)}, bf16[8,32,4,128]{3,2,1,0:T(4,128)(2,1)S(1)}, u32[]{:S(2)}, u32[]{:S(2)}) collective-permute-start(bf16[8,32,4,128]{3,2,1,0:T(4,128)(2,1)S(1)} %pad_maximum_fusion), channel_id=1, source_target_pairs={{8,0},{16,8},{24,16},{32,24},{40,32},{48,40},{56,48},{64,56},{72,6... | collective-permute-start | bytes 786440 | tf_op jit(solution)/shard_map/ppermute | solution.py:382
  38.3 3.6 %collective-permute-start.98 = (bf16[8,32,4,128]{3,2,1,0:T(4,128)(2,1)S(1)}, bf16[8,32,4,128]{3,2,1,0:T(4,128)(2,1)S(1)}, u32[]{:S(2)}, u32[]{:S(2)}) collective-permute-start(bf16[8,32,4,128]{3,2,1,0:T(4,128)(2,1)S(1)} %pad_maximum_fusion), channel_id=1, source_target_pairs={{0,8},{8,16},{16,24},{24,32},{32,40},{40,48},{48,56},{56,64},{64,7... | collective-permute-start | bytes 786440 | tf_op jit(solution)/shard_map/ppermute | solution.py:381
  41.9 0.1 pad_add_fusion.place
  42.0 3.3 %collective-permute-done.99.high = bf16[8,32,4,128]{3,2,1,0:T(4,128)(2,1)S(1)} collective-permute-done((bf16[8,32,4,128]{3,2,1,0:T(4,128)(2,1)S(1)}, bf16[8,32,4,128]{3,2,1,0:T(4,128)(2,1)S(1)}, u32[]{:S(2)}, u32[]{:S(2)}) %collective-permute-start.99) | collective-permute-done | bytes 262176 | tf_op jit(solution)/shard_map/ppermute | solution.py:382
  45.3 0.0 collective-permute-done.98.low
  45.3 0.0 collective-permute-done.96.left
  45.3 0.0 collective-permute-done.97.right
  45.4 5.0 %shard_map.77 = (f32[24,8,128]{2,1,0:T(8,128)S(1)}, f32[32,8,128]{2,1,0:T(8,128)S(1)}, f32[6,32,8,128]{3,2,1,0:T(8,128)S(1)}, f32[2,32,8,128]{3,2,1,0:T(8,128)S(...) custom-call(s32[4]{0:T(128)S(1)} %pad_add_fusion.place, ...), custom_call_target="tpu_custom_call" | custom-call | tf_op jit(solution)/shard_map/pallas_call | solution.py:332
  50.4 4.0 %collective-permute-start.100 = (f32[24,8,128]{2,1,0:T(8,128)S(1)}, f32[24,8,128]{2,1,0:T(8,128)S(1)}, u32[]{:S(2)}, u32[]{:S(2)}) collective-permute-start(f32[24,8,128]{2,1,0:T(8,128)S(1)} %get-tuple-element.549.mine), channel_id=1, source_target_pairs={{0,4},{4,0},{1,5},{5,1},{2,6},{6,2},{3,7},{7,3},{8,12},{12,8},{9,1... | collective-permute-start | bytes 294920 | tf_op jit(solution)/shard_map/ppermute | solution.py:405
  54.4 2.0 %collective-permute-done.100.theirs = f32[24,8,128]{2,1,0:T(8,128)S(1)} collective-permute-done((f32[24,8,128]{2,1,0:T(8,128)S(1)}, f32[24,8,128]{2,1,0:T(8,128)S(1)}, u32[]{:S(2)}, u32[]{:S(2)}) %collective-permute-start.100) | collective-permute-done | bytes 98336 | tf_op jit(solution)/shard_map/ppermute | solution.py:405
  56.4 5.2 %shard_map.78 = (f32[6,8,128]{2,1,0:T(8,128)S(1)}, f32[6,32,8,128]{3,2,1,0:T(8,128)S(1)}, f32[2,8,128]{2,1,0:T(8,128)S(1)}, f32[2,128]{1,0:T(2,128)S(1)}) custom-call(s32[4]{0:T(128)S(1)} %pad_add_fusion.place, f32[2,8]{1,0:T(2,128)S(1)} %copy-done.2, f32[24,8,128]{2,1,0:T(8,128)S(1)} %get-tuple-element.549.mine, ...), custom_call_target="tpu_custom_call" | custom-call | tf_op jit(solution)/shard_map/pallas_call | solution.py:332
  61.6 2.5 %psum.7 = f32[2,128]{1,0:T(2,128)S(1)} all-reduce(f32[2,128]{1,0:T(2,128)S(1)} %get-tuple-element.560), channel_id=1, replica_groups=mesh['row'=32,'core'=2,'vert'=2,'dir'=4] {'core'}, use_global_device_ids=true, to_apply=%region_16.17 | all-reduce | flops 256 | bytes 2048 | tf_op jit(solution)/shard_map/psum | solution.py:415
  64.1 0.6 broadcast_in_dim.10
  64.7 23.3 %all-to-all-start = ((f32[64,2,128]{2,1,0:T(2,128)}), f32[64,2,128]{2,1,0:T(2,128)S(1)}, u32[]{:S(2)}, u32[]{:S(2)}) async-start(f32[64,2,128]{2,1,0:T(2,128)} %broadcast_in_dim.10), calls=%async_computation | async-start | bytes 131072 | tf_op jit(solution)/shard_map/all_to_all | solution.py:417
  88.1 2.9 %collective-permute-start.101 = (f32[6,8,128]{2,1,0:T(8,128)S(1)}, f32[6,8,128]{2,1,0:T(8,128)S(1)}, u32[]{:S(2)}, u32[]{:S(2)}) collective-permute-start(f32[6,8,128]{2,1,0:T(8,128)S(1)} %get-tuple-element.557.mine), channel_id=1, source_target_pairs={{0,4},{4,0},{1,5},{5,1},{2,6},{6,2},{3,7},{7,3},{8,12},{12,8},{9,1... | collective-permute-start | bytes 73736 | tf_op jit(solution)/shard_map/ppermute | solution.py:413
  91.0 1.9 %collective-permute-done.101.theirs = f32[6,8,128]{2,1,0:T(8,128)S(1)} collective-permute-done((f32[6,8,128]{2,1,0:T(8,128)S(1)}, f32[6,8,128]{2,1,0:T(8,128)S(1)}, u32[]{:S(2)}, u32[]{:S(2)}) %collective-permute-start.101) | collective-permute-done | bytes 24608 | tf_op jit(solution)/shard_map/ppermute | solution.py:413
  93.0 1.6 %shard_map.79 = f32[2,3,32,4,128]{4,3,2,1,0:T(4,128)} custom-call(s32[4]{0:T(128)S(1)} %pad_add_fusion.place, f32[6,8,128]{2,1,0:T(8,128)S(1)} %get-tuple-element.557.mine, f32[6,8,128]{2,1,0:T(8,128)S(1)} %collective-permute-done.101.theirs, f32[2,8,128]{2,1,0:T(8,128)S(1)} %get-tuple-element.558.middle, ...), custom_call_target="tpu_custom_call" | custom-call | tf_op jit(solution)/shard_map/pallas_call | solution.py:332
  94.5 4.4 %all-to-all-done = f32[64,2,128]{2,1,0:T(2,128)S(1)} async-done(((f32[64,2,128]{2,1,0:T(2,128)}), f32[64,2,128]{2,1,0:T(2,128)S(1)}, u32[]{:S(2)}, u32[]{:S(2)}) %all-to-all-start) | async-done | bytes 65568 | tf_op jit(solution)/shard_map/all_to_all | solution.py:417
  99.0 0.2 reduce_sum.9
  99.2 0.5 broadcast_multiply_fusion
  (5 shorter events, 0.0 us)
Async XLA Ops:
  0.6 0.7 copy-start.4
  5.1 0.7 copy-start.3
  11.6 16.6 %copy-start.1 = (f32[2,3,32,4,128]{4,3,2,1,0:T(4,128)S(1)}, f32[2,3,32,4,128]{4,3,2,1,0:T(4,128)}, u32[]{:S(2)}) copy-start(f32[2,3,32,4,128]{4,3,2,1,0:T(4,128)} %own.1) | copy-start | bytes 1179652
  11.6 24.5 %copy-start = (s32[32,4,128]{2,1,0:T(4,128)S(1)}, s32[32,4,128]{2,1,0:T(4,128)}, u32[]{:S(2)}) copy-start(s32[32,4,128]{2,1,0:T(4,128)} %groups.3) | copy-start | bytes 196612
  12.8 9.5 %collective-permute-start.53 = (bf16[4,32,4,128]{3,2,1,0:T(4,128)(2,1)S(1)}, bf16[4,32,4,128]{3,2,1,0:T(4,128)(2,1)S(1)}, u32[]{:S(2)}, u32[]{:S(2)}) collective-permute-start(bf16[4,32,4,128]{3,2,1,0:T(4,128)(2,1)S(1)} %get-tuple-element.577), channel_id=1, source_target_pairs={{0,1},{4,5},{8,9},{12,13},{16,17},{20,21},{24,25},{28,29},{32,33},... | collective-permute-start | bytes 393224 | tf_op jit(solution)/shard_map/cond/branch_8_fun/ppermute | solution.py:351
  16.7 6.2 %collective-permute-start.52 = (bf16[4,32,4,128]{3,2,1,0:T(4,128)(2,1)S(1)}, bf16[4,32,4,128]{3,2,1,0:T(4,128)(2,1)S(1)}, u32[]{:S(2)}, u32[]{:S(2)}) collective-permute-start(bf16[4,32,4,128]{3,2,1,0:T(4,128)(2,1)S(1)} %get-tuple-element.577), channel_id=1, source_target_pairs={{0,2},{4,6},{8,10},{12,14},{16,18},{20,22},{24,26},{28,30},{32,34}... | collective-permute-start | bytes 393224 | tf_op jit(solution)/shard_map/cond/branch_8_fun/ppermute | solution.py:351
  19.0 4.0 %collective-permute-start.51 = (bf16[4,32,4,128]{3,2,1,0:T(4,128)(2,1)S(1)}, bf16[4,32,4,128]{3,2,1,0:T(4,128)(2,1)S(1)}, u32[]{:S(2)}, u32[]{:S(2)}) collective-permute-start(bf16[4,32,4,128]{3,2,1,0:T(4,128)(2,1)S(1)} %get-tuple-element.577), channel_id=1, source_target_pairs={{0,3},{4,7},{8,11},{12,15},{16,19},{20,23},{24,27},{28,31},{32,35}... | collective-permute-start | bytes 393224 | tf_op jit(solution)/shard_map/cond/branch_8_fun/ppermute | solution.py:351
  20.3 4.3 %collective-permute-start.50 = (bf16[4,32,4,128]{3,2,1,0:T(4,128)(2,1)S(1)}, bf16[4,32,4,128]{3,2,1,0:T(4,128)(2,1)S(1)}, u32[]{:S(2)}, u32[]{:S(2)}) collective-permute-start(bf16[4,32,4,128]{3,2,1,0:T(4,128)(2,1)S(1)} %get-tuple-element.578), channel_id=1, source_target_pairs={{2,3},{6,7},{10,11},{14,15},{18,19},{22,23},{26,27},{30,31},{34,35... | collective-permute-start | bytes 393224 | tf_op jit(solution)/shard_map/cond/branch_8_fun/ppermute | solution.py:351
  20.9 7.2 %collective-permute-start.49 = (bf16[4,32,4,128]{3,2,1,0:T(4,128)(2,1)S(1)}, bf16[4,32,4,128]{3,2,1,0:T(4,128)(2,1)S(1)}, u32[]{:S(2)}, u32[]{:S(2)}) collective-permute-start(bf16[4,32,4,128]{3,2,1,0:T(4,128)(2,1)S(1)} %get-tuple-element.578), channel_id=1, source_target_pairs={{2,0},{6,4},{10,8},{14,12},{18,16},{22,20},{26,24},{30,28},{34,32}... | collective-permute-start | bytes 393224 | tf_op jit(solution)/shard_map/cond/branch_8_fun/ppermute | solution.py:351
  22.3 5.9 %collective-permute-start.48 = (bf16[4,32,4,128]{3,2,1,0:T(4,128)(2,1)S(1)}, bf16[4,32,4,128]{3,2,1,0:T(4,128)(2,1)S(1)}, u32[]{:S(2)}, u32[]{:S(2)}) collective-permute-start(bf16[4,32,4,128]{3,2,1,0:T(4,128)(2,1)S(1)} %get-tuple-element.578), channel_id=1, source_target_pairs={{2,1},{6,5},{10,9},{14,13},{18,17},{22,21},{26,25},{30,29},{34,33}... | collective-permute-start | bytes 393224 | tf_op jit(solution)/shard_map/cond/branch_8_fun/ppermute | solution.py:351
  28.2 17.1 %collective-permute-start.96 = (f32[2,3,32,4,128]{4,3,2,1,0:T(4,128)S(1)}, f32[2,3,32,4,128]{4,3,2,1,0:T(4,128)S(1)}, u32[]{:S(2)}, u32[]{:S(2)}) collective-permute-start(f32[2,3,32,4,128]{4,3,2,1,0:T(4,128)S(1)} %copy-done.1), channel_id=1, source_target_pairs={{0,8},{8,16},{16,24},{24,32},{32,40},{40,48},{48,56},{56,64},{64,7... | collective-permute-start | bytes 1179656 | tf_op jit(solution)/shard_map/ppermute | solution.py:373
  33.4 11.9 %collective-permute-start.97 = (f32[2,3,32,4,128]{4,3,2,1,0:T(4,128)S(1)}, f32[2,3,32,4,128]{4,3,2,1,0:T(4,128)S(1)}, u32[]{:S(2)}, u32[]{:S(2)}) collective-permute-start(f32[2,3,32,4,128]{4,3,2,1,0:T(4,128)S(1)} %copy-done.1), channel_id=1, source_target_pairs={{8,0},{16,8},{24,16},{32,24},{40,32},{48,40},{56,48},{64,56},{72,6... | collective-permute-start | bytes 1179656 | tf_op jit(solution)/shard_map/ppermute | solution.py:374
  36.3 9.0 %collective-permute-start.99 = (bf16[8,32,4,128]{3,2,1,0:T(4,128)(2,1)S(1)}, bf16[8,32,4,128]{3,2,1,0:T(4,128)(2,1)S(1)}, u32[]{:S(2)}, u32[]{:S(2)}) collective-permute-start(bf16[8,32,4,128]{3,2,1,0:T(4,128)(2,1)S(1)} %pad_maximum_fusion), channel_id=1, source_target_pairs={{8,0},{16,8},{24,16},{32,24},{40,32},{48,40},{56,48},{64,56},{72,6... | collective-permute-start | bytes 786440 | tf_op jit(solution)/shard_map/ppermute | solution.py:382
  38.3 7.1 %collective-permute-start.98 = (bf16[8,32,4,128]{3,2,1,0:T(4,128)(2,1)S(1)}, bf16[8,32,4,128]{3,2,1,0:T(4,128)(2,1)S(1)}, u32[]{:S(2)}, u32[]{:S(2)}) collective-permute-start(bf16[8,32,4,128]{3,2,1,0:T(4,128)(2,1)S(1)} %pad_maximum_fusion), channel_id=1, source_target_pairs={{0,8},{8,16},{16,24},{24,32},{32,40},{40,48},{48,56},{56,64},{64,7... | collective-permute-start | bytes 786440 | tf_op jit(solution)/shard_map/ppermute | solution.py:381
  42.0 3.3 %copy-start.2 = (f32[2,8]{1,0:T(2,128)S(1)}, f32[2,8]{1,0:T(2,128)}, u32[]{:S(2)}) copy-start(f32[2,8]{1,0:T(2,128)} %weights.3) | copy-start | bytes 196
  50.4 6.0 %collective-permute-start.100 = (f32[24,8,128]{2,1,0:T(8,128)S(1)}, f32[24,8,128]{2,1,0:T(8,128)S(1)}, u32[]{:S(2)}, u32[]{:S(2)}) collective-permute-start(f32[24,8,128]{2,1,0:T(8,128)S(1)} %get-tuple-element.549.mine), channel_id=1, source_target_pairs={{0,4},{4,0},{1,5},{5,1},{2,6},{6,2},{3,7},{7,3},{8,12},{12,8},{9,1... | collective-permute-start | bytes 294920 | tf_op jit(solution)/shard_map/ppermute | solution.py:405
  64.7 34.2 %all-to-all-start = ((f32[64,2,128]{2,1,0:T(2,128)}), f32[64,2,128]{2,1,0:T(2,128)S(1)}, u32[]{:S(2)}, u32[]{:S(2)}) async-start(f32[64,2,128]{2,1,0:T(2,128)} %broadcast_in_dim.10), calls=%async_computation | async-start | bytes 131072 | tf_op jit(solution)/shard_map/all_to_all | solution.py:417
  88.1 4.9 %collective-permute-start.101 = (f32[6,8,128]{2,1,0:T(8,128)S(1)}, f32[6,8,128]{2,1,0:T(8,128)S(1)}, u32[]{:S(2)}, u32[]{:S(2)}) collective-permute-start(f32[6,8,128]{2,1,0:T(8,128)S(1)} %get-tuple-element.557.mine), channel_id=1, source_target_pairs={{0,4},{4,0},{1,5},{5,1},{2,6},{6,2},{3,7},{7,3},{8,12},{12,8},{9,1... | collective-permute-start | bytes 73736 | tf_op jit(solution)/shard_map/ppermute | solution.py:413

commit v2 on v1

--- a/solution.py
+++ b/solution.py
@@ -115,7 +115,7 @@
     return rows
 
 
-def first_kernel(place, weights, left, own, right, low, high, rec_a, rec_b, groups,
+def first_kernel(place, weights, mate, own, other, edge_mate, edge, edge_other,
                  message, ratio_out, value_out, power_out, ratio2_out, inverse2_out, face2_out,
                  wrow_out, tangents, winds, winds2, turbines):
     levels = own.shape[2]
@@ -129,17 +129,25 @@
 
     for field in range(6):
         d, i = divmod(field, 3)
-        tangents[field, :, 0:4, :] = left[d, i]
         tangents[field, :, 4:8, :] = own[d, i]
-        tangents[field, :, 8:12, :] = right[d, i]
     for c in range(4):
-        winds[c, :, 0:4, :] = low[c].astype(jnp.float32)
-        winds[c, :, 4:8, :] = rec_a[c].astype(jnp.float32)
-        winds[c, :, 8:12, :] = high[c].astype(jnp.float32)
-        winds2[c, :, 4:8, :] = rec_b[c].astype(jnp.float32)
-    turbines[:, 0:4, :] = low[7].astype(jnp.float32)
-    turbines[:, 4:8, :] = groups[...].astype(jnp.float32)
-    turbines[:, 8:12, :] = high[7].astype(jnp.float32)
+        winds[c, :, 4:8, :] = edge[c].astype(jnp.float32)
+        winds2[c, :, 4:8, :] = edge[4 + c].astype(jnp.float32)
+    turbines[:, 4:8, :] = edge[8].astype(jnp.float32)
+
+    def sides(low, high, low_edge, high_edge):
+        for field in range(6):
+            d, i = divmod(field, 3)
+            tangents[field, :, 0:4, :] = low[d, i]
+            tangents[field, :, 8:12, :] = high[d, i]
+        for c in range(4):
+            winds[c, :, 0:4, :] = low_edge[c].astype(jnp.float32)
+            winds[c, :, 8:12, :] = high_edge[c].astype(jnp.float32)
+        turbines[:, 0:4, :] = low_edge[8].astype(jnp.float32)
+        turbines[:, 8:12, :] = high_edge[8].astype(jnp.float32)
+
+    pl.when(place[4] == 0)(lambda: sides(other, mate, edge_other, edge_mate))
+    pl.when(place[4] == 1)(lambda: sides(mate, other, edge_mate, edge_other))
 
     def level_rows(j, above, below):
         k = at(j)
@@ -201,9 +209,9 @@
 
 
 def second_kernel(place, weights, mine, theirs, ratio_in, value_in, power_in, ratio2_in, inverse2_in,
-                  face2_in, wrow_in, low, high, rec_b, groups,
+                  face2_in, wrow_in, edge_mate, edge, edge_other,
                   row_out, value_out, middle_out, sums_out, tangents, winds, turbines, adjoint):
-    levels = rec_b.shape[1]
+    levels = edge.shape[1]
     last = levels - 1
     sign = place[0].astype(jnp.float32)
     base = place[1]
@@ -212,14 +220,19 @@
     def at(j):
         return base + step * j
 
-    for c in range(3):
-        winds[c, :, 0:4, :] = low[4 + c].astype(jnp.float32)
-        winds[c, :, 8:12, :] = high[4 + c].astype(jnp.float32)
     for c in range(4):
-        winds[c, :, 4:8, :] = rec_b[c].astype(jnp.float32)
-    turbines[:, 4:8, :] = groups[...].astype(jnp.float32)
-
-    zero = jnp.zeros((8, rec_b.shape[3]), jnp.float32)
+        winds[c, :, 4:8, :] = edge[4 + c].astype(jnp.float32)
+    turbines[:, 4:8, :] = edge[8].astype(jnp.float32)
+
+    def sides(low_edge, high_edge):
+        for c in range(3):
+            winds[c, :, 0:4, :] = low_edge[4 + c].astype(jnp.float32)
+            winds[c, :, 8:12, :] = high_edge[4 + c].astype(jnp.float32)
+
+    pl.when(place[4] == 0)(lambda: sides(edge_other, edge_mate))
+    pl.when(place[4] == 1)(lambda: sides(edge_mate, edge_other))
+
+    zero = jnp.zeros((8, edge.shape[3]), jnp.float32)
     layer = lax.broadcasted_iota(jnp.int32, zero.shape, 0)
     inside = jnp.logical_and(layer >= place[2], layer < place[3])
     center = jnp.logical_and(layer >= 2, layer < 6)
@@ -340,23 +353,64 @@
     )(*scalars, *arrays)
 
 
-def fetch_records(first, second, owner_first, owner_second):
+def prepare_kernel(slots, steps, records, code, first, second, arrived):
+    per_device = records.shape[0]
+    slot_a, slot_b = slots[steps[0]], slots[steps[1]]
+    copy_a = pltpu.make_async_copy(records.at[lax.rem(slot_a, per_device)], first, arrived.at[0])
+    copy_b = pltpu.make_async_copy(records.at[lax.rem(slot_b, per_device)], second, arrived.at[1])
+    copy_a.start()
+    copy_b.start()
+    owners = slots.shape[0] // per_device
+    code[0] = lax.div(slot_a, per_device) * owners + lax.div(slot_b, per_device)
+    copy_a.wait()
+    copy_b.wait()
+
+
+def prepare(record_slot, step_record, records):
+    block = jax.ShapeDtypeStruct(records.shape[1:], records.dtype)
+    return pl.pallas_call(
+        prepare_kernel,
+        out_shape=[jax.ShapeDtypeStruct((1,), jnp.int32), block, block],
+        in_specs=[pl.BlockSpec(memory_space=pltpu.SMEM)] * 2 + [pl.BlockSpec(memory_space=pl.ANY)],
+        out_specs=[pl.BlockSpec(memory_space=pltpu.SMEM)] + [pl.BlockSpec(memory_space=pltpu.VMEM)] * 2,
+        scratch_shapes=[pltpu.SemaphoreType.DMA((2,))],
+    )(record_slot, step_record, records)
+
+
+def swap_tiles(block):
+    count = lax.axis_size("row")
+    pairs = [(2 * i + 1, 2 * i + 2) for i in range(count - 1)]
+    pairs += [(right, left) for left, right in pairs]
+    return lax.ppermute(block, "core", [(0, 1), (1, 0)]), lax.ppermute(block, TILE, pairs)
+
+
+def gather_inputs(code, first, second, tangent_in, mask):
     count = lax.axis_size("dir")
     here = lax.axis_index("dir")
 
-    def spread(record, owner):
-        result = record
-        for k in range(1, count):
-            target = (owner + k) % count
-            got = lax.ppermute(record, "dir", [(owner, target)])
-            result = jnp.where(here == target, got, result)
-        return result
+    def send(record, owner):
+        return [
+            lax.ppermute(record, "dir", [(owner, (owner + k) % count)]) for k in range(1, count)
+        ]
+
+    def take(record, owner, got):
+        for k, piece in enumerate(got, 1):
+            record = jnp.where(here == (owner + k) % count, piece, record)
+        return record
 
     def branch(a, b):
-        return lambda x, y: (spread(x, a), spread(y, b))
+        def run(x, y, tangent, groups):
+            got_a, got_b = send(x, a), send(y, b)
+            tangents = swap_tiles(tangent)
+            edge = jnp.concatenate(
+                [take(x, a, got_a), take(y, b, got_b), groups.astype(x.dtype)[None]], axis=0
+            )
+            return edge, *tangents, *swap_tiles(edge)
+
+        return run
 
     branches = [branch(a, b) for a in range(count) for b in range(count)]
-    return lax.switch(owner_first * count + owner_second, branches, first, second)
+    return lax.switch(code, branches, first, second, tangent_in, mask)
 
 
 def shards(tangent_in, records, record_slot, step_record, turbine_mask, group_weights):
@@ -365,27 +419,19 @@
     tiles = lax.axis_size("row") * lax.axis_size("core")
     tile = lax.axis_index("row") * lax.axis_size("core") + lax.axis_index("core")
     vert = lax.axis_index("vert")
-    up = [(i, i + 1) for i in range(tiles - 1)]
-    down = [(i + 1, i) for i in range(tiles - 1)]
     swap = [(0, 1), (1, 0)]
-    per_device = records.shape[0]
-
-    left = lax.ppermute(tangent_in, TILE, up)
-    right = lax.ppermute(tangent_in, TILE, down)
-
-    slots = [record_slot[step_record[s]] for s in range(STEPS)]
-    stored = [lax.dynamic_index_in_dim(records, s % per_device, 0, keepdims=False) for s in slots]
-    rec_a, rec_b = fetch_records(*stored, *[s // per_device for s in slots])
-
-    edge = jnp.concatenate([rec_a, rec_b[:3], turbine_mask.astype(jnp.bfloat16)[None]], axis=0)
-    low = lax.ppermute(edge, TILE, up)
-    high = lax.ppermute(edge, TILE, down)
+
+    code, first, second = prepare(record_slot, step_record, records)
+    edge, mate, other, edge_mate, edge_other = gather_inputs(
+        code[0], first, second, tangent_in, turbine_mask
+    )
 
     place = jnp.stack([
         1 - 2 * vert,
         vert * (levels - 1),
         jnp.where(tile == 0, 2, 0),
         jnp.where(tile == tiles - 1, 6, 8),
+        lax.axis_index("core"),
     ]).astype(jnp.int32)
 
     def block(*lead):
@@ -397,7 +443,7 @@
     message, ratio, value, power, ratio2, inverse2, face2, wrow = call(
         first_kernel,
         (place, group_weights),
-        (left, tangent_in, right, low, high, rec_a, rec_b, turbine_mask),
+        (mate, tangent_in, other, edge_mate, edge, edge_other),
         (block(FIELDS), block(levels), block(fields, levels), block(2, levels),
          block(levels), block(levels), block(levels), block(2, levels)),
         (wide(fields, levels), wide(4, levels), wide(4, levels), wide(levels)),
@@ -406,13 +452,14 @@
     row, value2, middle, sums = call(
         second_kernel,
         (place, group_weights),
-        (message, answer, ratio, value, power, ratio2, inverse2, face2, wrow, low, high, rec_b, turbine_mask),
+        (message, answer, ratio, value, power, ratio2, inverse2, face2, wrow, edge_mate, edge, edge_other),
         (block(fields), block(fields, levels), block(2), (directions, spans)),
         (wide(fields, levels), wide(4, levels), wide(levels), block(2, levels)),
     )
     answer2 = lax.ppermute(row, "vert", swap)
 
     sums = lax.psum(sums, "core")
+    sums, answer2 = lax.optimization_barrier((sums, answer2))
     count = lax.axis_size("row") * lax.axis_size("vert")
     gathered = lax.all_to_all(
         jnp.broadcast_to(sums[None], (count, directions, spans)), ("row", "vert"), 0, 0, tiled=True

time: 100 us -> 87.6 us (0.88)
  between operations: 9.93 us -> 1.38 us
  starting transfers between devices: 53.8 us -> 47.2 us
  Pallas kernels: 11.8 us -> 14.9 us
  local copies, waits for them, and re-layouts: 4.51 us -> 1.41 us
  waiting for transfers between devices: 15.3 us -> 17.4 us
    all_to_all x1, starting transfers between devices: 23.3 us -> 18.4 us  [shards(): lax.all_to_all(jnp.broadcast_to(sums[None], (count, directions, spans)),...]
    all_to_all x1, waiting for transfers between devices: 4.45 us -> 9.34 us  [shards(): lax.all_to_all(jnp.broadcast_to(sums[None], (count, directions, spans)),...]
    ppermute x10, waiting for transfers between devices: 6.9 us -> 4.5 us  [the longest x2 4.48 us: swap_tiles(): lax.ppermute(block, TILE, pairs)]
    pallas_call x0 -> x1, Pallas kernels: none -> 2.31 us  [prepare(): pl.pallas_call(prepare_kernel, out_shape=[jax.ShapeDtypeStruct((1,), jnp....]
    ppermute x1, starting transfers between devices: 4 us -> 1.92 us  [shards(): answer = lax.ppermute(message, 'vert', swap)]
    ppermute x1, waiting for transfers between devices: 1.95 us -> 0.16 us  [shards(): answer2 = lax.ppermute(row, 'vert', swap)]
    slice x2 -> x0, local copies, waits for them, and re-layouts: 1.51 us -> none  [the longest x1 0.93 us: shards(): rec_b[:3]]
    ppermute x10, starting transfers between devices: 23.5 us -> 25 us  [the longest x6 11.6 us: send(): lax.ppermute(record, 'dir', [(owner, (owner + k) % count)])]
  transfers between devices with their start and end apart: 13 -> 13, of which waited for: 5 -> 4; matrix products, arithmetic and copies ran while one was open for 2% -> 1% of each run, Pallas kernels for 2% -> 2%
where the time goes in v2:
time: 87.6 us; the launch traced here: 86.9 us
  starting transfers between devices  47.2 us (54%)
  waiting for transfers between devices  17.4 us (20%)
  Pallas kernels  14.9 us (17%)
  blocking collectives  2.48 us (3%)
  other arithmetic  1.72 us (2%)
  local copies, waits for them, and re-layouts  1.41 us (2%)
  between operations  1.38 us (2%)
    all_to_all x1, starting transfers between devices, shards(): lax.all_to_all(jnp.broadcast_to(sums[None], (count, directions, spans)),...  18.4 us
    pallas_call x3, Pallas kernels, call(): pl.pallas_call(kernel, out_shape=[jax.ShapeDtypeStruct(shape, jnp.float32...  12.6 us
    ppermute x6, starting transfers between devices, send(): lax.ppermute(record, 'dir', [(owner, (owner + k) % count)])  11.6 us
    all_to_all x1, waiting for transfers between devices, shards(): lax.all_to_all(jnp.broadcast_to(sums[None], (count, directions, spans)),...  9.34 us
    ppermute x2, starting transfers between devices, swap_tiles(): lax.ppermute(block, 'core', [(0, 1), (1, 0)])  7.22 us
    ppermute x2, starting transfers between devices, swap_tiles(): lax.ppermute(block, TILE, pairs)  6.24 us
    ppermute x2, waiting for transfers between devices, swap_tiles(): lax.ppermute(block, TILE, pairs)  4.48 us
    ppermute x1, waiting for transfers between devices, shards(): answer = lax.ppermute(message, 'vert', swap)  3.43 us
  transfers between devices with their start and end apart: 13, of which 4 were waited for; matrix products, arithmetic and copies ran while one was open for 1% of the time, Pallas kernels for 2%

profile of v2, /device:TPU:1, one launch (start us, length us, event | category | flops | bytes accessed | tf_op | source)
XLA Modules:
  0.0 86.9 jit_solution(12983460167864150700)
XLA Ops:
  0.6 0.0 copy-start.2
  0.7 0.0 copy-start.1
  0.7 2.3 %shard_map.77 = (s32[1]{0:T(128)}, bf16[4,32,4,128]{3,2,1,0:T(4,128)(2,1)S(1)}, bf16[4,32,4,128]{3,2,1,0:T(4,128)(2,1)S(1)}) custom-call(s32[16]{0:T(128)} %slots.1, s32[2]{0:T(128)} %steps.1, bf16[4,4,32,4,128]{4,3,2,1,0:T(4,128)(2,1)} %records.1), custom_call_target="tpu_custom_call" | custom-call | tf_op jit(solution)/shard_map/pallas_call | solution.py:371
  3.6 0.0 copy-done.2
  3.6 0.0 copy-done.1
  3.7 30.9 %conditional.1 = (bf16[9,32,4,128]{3,2,1,0:T(4,128)(2,1)}, f32[2,3,32,4,128]{4,3,2,1,0:T(4,128)}, f32[2,3,32,4,128]{4,3,2,1,0:T(4,128)}, bf16[9,32,4,128]{3,2,1,0:T(4,128)(2,1)}, bf16[9,32,4,128]{3,2,1,0:T(4,128)(2,1)}) conditional(s32[]{:T(128)} %bitcast.21, (s32[]{:T(128)}, bf16[4,32,4,128]{3,2,1,0:T(4,128)(2,1)S(1)}, ...), branch_computations={%region_0.1_spmd, %region_1.2_spmd, %region_2.3_spmd, %region_3.4_... | conditional | flops 704516 | bytes 10650082 | solution.py:413
  3.9 1.3 %collective-permute-start.122 = (bf16[4,32,4,128]{3,2,1,0:T(4,128)(2,1)S(1)}, bf16[4,32,4,128]{3,2,1,0:T(4,128)(2,1)S(1)}, u32[]{:S(2)}, u32[]{:S(2)}) collective-permute-start(bf16[4,32,4,128]{3,2,1,0:T(4,128)(2,1)S(1)} %get-tuple-element.221), channel_id=1, source_target_pairs={{3,0},{7,4},{11,8},{15,12},{19,16},{23,20},{27,24},{31,28},{35,32}... | collective-permute-start | bytes 393224 | tf_op jit(solution)/shard_map/cond/branch_12_fun/ppermute | solution.py:393
  5.2 0.7 collective-permute-start.121
  5.9 0.7 collective-permute-start.120
  6.5 4.0 %collective-permute-start.125 = (bf16[4,32,4,128]{3,2,1,0:T(4,128)(2,1)S(1)}, bf16[4,32,4,128]{3,2,1,0:T(4,128)(2,1)S(1)}, u32[]{:S(2)}, u32[]{:S(2)}) collective-permute-start(bf16[4,32,4,128]{3,2,1,0:T(4,128)(2,1)S(1)} %get-tuple-element.222), channel_id=1, source_target_pairs={{0,1},{4,5},{8,9},{12,13},{16,17},{20,21},{24,25},{28,29},{32,33},... | collective-permute-start | bytes 393224 | tf_op jit(solution)/shard_map/cond/branch_12_fun/ppermute | solution.py:393
  10.5 2.2 %collective-permute-start.124 = (bf16[4,32,4,128]{3,2,1,0:T(4,128)(2,1)S(1)}, bf16[4,32,4,128]{3,2,1,0:T(4,128)(2,1)S(1)}, u32[]{:S(2)}, u32[]{:S(2)}) collective-permute-start(bf16[4,32,4,128]{3,2,1,0:T(4,128)(2,1)S(1)} %get-tuple-element.222), channel_id=1, source_target_pairs={{0,2},{4,6},{8,10},{12,14},{16,18},{20,22},{24,26},{28,30},{32,34}... | collective-permute-start | bytes 393224 | tf_op jit(solution)/shard_map/cond/branch_12_fun/ppermute | solution.py:393
  12.7 0.0 collective-permute-done.122
  12.7 2.8 %collective-permute-start.123 = (bf16[4,32,4,128]{3,2,1,0:T(4,128)(2,1)S(1)}, bf16[4,32,4,128]{3,2,1,0:T(4,128)(2,1)S(1)}, u32[]{:S(2)}, u32[]{:S(2)}) collective-permute-start(bf16[4,32,4,128]{3,2,1,0:T(4,128)(2,1)S(1)} %get-tuple-element.222), channel_id=1, source_target_pairs={{0,3},{4,7},{8,11},{12,15},{16,19},{20,23},{24,27},{28,31},{32,35}... | collective-permute-start | bytes 393224 | tf_op jit(solution)/shard_map/cond/branch_12_fun/ppermute | solution.py:393
  15.5 0.0 collective-permute-done.121
  15.5 4.3 %collective-permute-start.127 = (f32[2,3,32,4,128]{4,3,2,1,0:T(4,128)S(1)}, f32[2,3,32,4,128]{4,3,2,1,0:T(4,128)}, u32[]{:S(2)}, u32[]{:S(2)}) collective-permute-start(f32[2,3,32,4,128]{4,3,2,1,0:T(4,128)S(1)} %get-tuple-element.224), channel_id=1, source_target_pairs={{8,16},{24,32},{40,48},{56,64},{72,80},{88,96},{104,112},{120,128}... | collective-permute-start | bytes 1179656 | tf_op jit(solution)/shard_map/cond/branch_12_fun/ppermute | solution.py:384
  19.9 0.0 collective-permute-done.120
  19.9 5.3 %collective-permute-start.126 = (f32[2,3,32,4,128]{4,3,2,1,0:T(4,128)S(1)}, f32[2,3,32,4,128]{4,3,2,1,0:T(4,128)}, u32[]{:S(2)}, u32[]{:S(2)}) collective-permute-start(f32[2,3,32,4,128]{4,3,2,1,0:T(4,128)S(1)} %get-tuple-element.224), channel_id=1, source_target_pairs={{0,8},{8,0},{1,9},{9,1},{2,10},{10,2},{3,11},{11,3},{4,12},{12,4},... | collective-permute-start | bytes 1179656 | tf_op jit(solution)/shard_map/cond/branch_12_fun/ppermute | solution.py:384
  25.2 0.0 collective-permute-done.125
  25.2 0.0 collective-permute-done.124
  25.2 0.0 collective-permute-done.123
  25.3 0.9 %pad_maximum_fusion.12 = bf16[9,32,4,128]{3,2,1,0:T(4,128)(2,1)} fusion(bf16[1,32,4,128]{3,2,1,0:T(4,128)(2,1)S(1)} %convert_bitcast_fusion.12, bf16[4,32,4,128]{3,2,1,0:T(4,128)(2,1)S(1)} %bitcast.258, bf16[4,32,4,128]{3,2,1,0:T(4,128)(2,1)S(1)} %bitcast.239), kind=kLoop, calls=%fused_computation.48 | loop fusion | flops 294912 | bytes 589824 | tf_op jit(solution)/shard_map/cond/branch_12_fun/concatenate | solution.py:405
  26.2 1.9 %collective-permute-start.129 = (bf16[9,32,4,128]{3,2,1,0:T(4,128)(2,1)}, bf16[9,32,4,128]{3,2,1,0:T(4,128)(2,1)}, u32[]{:S(2)}, u32[]{:S(2)}) collective-permute-start(bf16[9,32,4,128]{3,2,1,0:T(4,128)(2,1)} %pad_maximum_fusion.12), channel_id=1, source_target_pairs={{8,16},{24,32},{40,48},{56,64},{72,80},{88,96},{104,112},{120,128}... | collective-permute-start | bytes 884744 | tf_op jit(solution)/shard_map/cond/branch_12_fun/ppermute | solution.py:384
  28.2 1.9 %collective-permute-start.128 = (bf16[9,32,4,128]{3,2,1,0:T(4,128)(2,1)}, bf16[9,32,4,128]{3,2,1,0:T(4,128)(2,1)}, u32[]{:S(2)}, u32[]{:S(2)}) collective-permute-start(bf16[9,32,4,128]{3,2,1,0:T(4,128)(2,1)} %pad_maximum_fusion.12), channel_id=1, source_target_pairs={{0,8},{8,0},{1,9},{9,1},{2,10},{10,2},{3,11},{11,3},{4,12},{12,4},... | collective-permute-start | bytes 884744 | tf_op jit(solution)/shard_map/cond/branch_12_fun/ppermute | solution.py:384
  30.1 0.0 collective-permute-done.127
  30.1 0.0 collective-permute-done.126
  30.1 4.5 %collective-permute-done.129 = bf16[9,32,4,128]{3,2,1,0:T(4,128)(2,1)} collective-permute-done((bf16[9,32,4,128]{3,2,1,0:T(4,128)(2,1)}, bf16[9,32,4,128]{3,2,1,0:T(4,128)(2,1)}, u32[]{:S(2)}, u32[]{:S(2)}) %collective-permute-start.129) | collective-permute-done | bytes 294944 | tf_op jit(solution)/shard_map/cond/branch_12_fun/ppermute | solution.py:384
  34.6 0.0 collective-permute-done.128
  34.6 0.1 stack.23.place
  34.7 0.0 copy-start
  34.7 0.7 copy-done
  35.4 5.6 %shard_map.78 = (f32[24,8,128]{2,1,0:T(8,128)S(1)}, f32[32,8,128]{2,1,0:T(8,128)S(1)}, f32[6,32,8,128]{3,2,1,0:T(8,128)S(1)}, f32[2,32,8,128]{3,2,1,0:T(8,128)S(...) custom-call(s32[5]{0:T(128)S(1)} %stack.23.place, ...), custom_call_target="tpu_custom_call" | custom-call | tf_op jit(solution)/shard_map/pallas_call | solution.py:345
  40.9 1.9 %collective-permute-start.160 = (f32[24,8,128]{2,1,0:T(8,128)S(1)}, f32[24,8,128]{2,1,0:T(8,128)S(1)}, u32[]{:S(2)}, u32[]{:S(2)}) collective-permute-start(f32[24,8,128]{2,1,0:T(8,128)S(1)} %get-tuple-element.272.mine), channel_id=1, source_target_pairs={{0,4},{4,0},{1,5},{5,1},{2,6},{6,2},{3,7},{7,3},{8,12},{12,8},{9,1... | collective-permute-start | bytes 294920 | tf_op jit(solution)/shard_map/ppermute | solution.py:451
  42.8 3.4 %collective-permute-done.160.theirs = f32[24,8,128]{2,1,0:T(8,128)S(1)} collective-permute-done((f32[24,8,128]{2,1,0:T(8,128)S(1)}, f32[24,8,128]{2,1,0:T(8,128)S(1)}, u32[]{:S(2)}, u32[]{:S(2)}) %collective-permute-start.160) | collective-permute-done | bytes 98336 | tf_op jit(solution)/shard_map/ppermute | solution.py:451
  46.3 5.5 %shard_map.79 = (f32[6,8,128]{2,1,0:T(8,128)S(1)}, f32[6,32,8,128]{3,2,1,0:T(8,128)S(1)}, f32[2,8,128]{2,1,0:T(8,128)S(1)}, f32[2,128]{1,0:T(2,128)S(1)}) custom-call(s32[5]{0:T(128)S(1)} %stack.23.place, f32[2,8]{1,0:T(2,128)S(1)} %copy-done, f32[24,8,128]{2,1,0:T(8,128)S(1)} %get-tuple-element.272.mine, f32[24,8,128]{2,1,0:T(8,128)S(1)} %collective-permute-done.160.theirs, ...), custom_call_target="tpu_custom_call" | custom-call | tf_op jit(solution)/shard_map/pallas_call | solution.py:345
  51.7 1.9 %collective-permute-start.161 = (f32[6,8,128]{2,1,0:T(8,128)S(1)}, f32[6,8,128]{2,1,0:T(8,128)S(1)}, u32[]{:S(2)}, u32[]{:S(2)}) collective-permute-start(f32[6,8,128]{2,1,0:T(8,128)S(1)} %get-tuple-element.280.mine), channel_id=1, source_target_pairs={{0,4},{4,0},{1,5},{5,1},{2,6},{6,2},{3,7},{7,3},{8,12},{12,8},{9,1... | collective-permute-start | bytes 73736 | tf_op jit(solution)/shard_map/ppermute | solution.py:459
  53.7 2.5 %psum.7 = f32[2,128]{1,0:T(2,128)S(1)} all-reduce(f32[2,128]{1,0:T(2,128)S(1)} %get-tuple-element.281), channel_id=1, replica_groups=mesh['row'=32,'core'=2,'vert'=2,'dir'=4] {'core'}, use_global_device_ids=true, to_apply=%region_16.17 | all-reduce | flops 256 | bytes 2048 | tf_op jit(solution)/shard_map/psum | solution.py:461
  56.2 0.2 collective-permute-done.161.theirs
  56.3 0.6 broadcast_in_dim.54
  57.0 18.4 %all-to-all-start = ((f32[64,2,128]{2,1,0:T(2,128)}), f32[64,2,128]{2,1,0:T(2,128)S(1)}, u32[]{:S(2)}, u32[]{:S(2)}) async-start(f32[64,2,128]{2,1,0:T(2,128)} %broadcast_in_dim.54), calls=%async_computation | async-start | bytes 131072 | tf_op jit(solution)/shard_map/all_to_all | solution.py:464
  75.3 1.6 %shard_map.80 = f32[2,3,32,4,128]{4,3,2,1,0:T(4,128)} custom-call(s32[5]{0:T(128)S(1)} %stack.23.place, f32[6,8,128]{2,1,0:T(8,128)S(1)} %get-tuple-element.280.mine, f32[6,8,128]{2,1,0:T(8,128)S(1)} %collective-permute-done.161.theirs, f32[2,8,128]{2,1,0:T(8,128)S(1)} %get-tuple-element.283.middle, f32[32,8,128]{2,1,0:T(8,128)S(1)} %get-tuple-element.276.ratio2_in.ratio_in, ...), custom_call_target="tpu_custom_call" | custom-call | tf_op jit(solution)/shard_map/pallas_call | solution.py:345
  76.9 9.3 %all-to-all-done = f32[64,2,128]{2,1,0:T(2,128)S(1)} async-done(((f32[64,2,128]{2,1,0:T(2,128)}), f32[64,2,128]{2,1,0:T(2,128)S(1)}, u32[]{:S(2)}, u32[]{:S(2)}) %all-to-all-start) | async-done | bytes 65568 | tf_op jit(solution)/shard_map/all_to_all | solution.py:464
  86.2 0.2 reduce_sum.9
  86.4 0.5 broadcast_multiply_fusion
  (3 shorter events, 0.1 us)
Async XLA Ops:
  0.6 3.0 %copy-start.2 = (f32[2,3,32,4,128]{4,3,2,1,0:T(4,128)S(1)}, f32[2,3,32,4,128]{4,3,2,1,0:T(4,128)}, u32[]{:S(2)}) copy-start(f32[2,3,32,4,128]{4,3,2,1,0:T(4,128)} %own.1) | copy-start | bytes 1179652
  0.7 3.0 %copy-start.1 = (s32[32,4,128]{2,1,0:T(4,128)S(1)}, s32[32,4,128]{2,1,0:T(4,128)}, u32[]{:S(2)}) copy-start(s32[32,4,128]{2,1,0:T(4,128)} %param.26) | copy-start | bytes 196612
  3.9 8.9 %collective-permute-start.122 = (bf16[4,32,4,128]{3,2,1,0:T(4,128)(2,1)S(1)}, bf16[4,32,4,128]{3,2,1,0:T(4,128)(2,1)S(1)}, u32[]{:S(2)}, u32[]{:S(2)}) collective-permute-start(bf16[4,32,4,128]{3,2,1,0:T(4,128)(2,1)S(1)} %get-tuple-element.221), channel_id=1, source_target_pairs={{3,0},{7,4},{11,8},{15,12},{19,16},{23,20},{27,24},{31,28},{35,32}... | collective-permute-start | bytes 393224 | tf_op jit(solution)/shard_map/cond/branch_12_fun/ppermute | solution.py:393
  5.2 10.4 %collective-permute-start.121 = (bf16[4,32,4,128]{3,2,1,0:T(4,128)(2,1)S(1)}, bf16[4,32,4,128]{3,2,1,0:T(4,128)(2,1)S(1)}, u32[]{:S(2)}, u32[]{:S(2)}) collective-permute-start(bf16[4,32,4,128]{3,2,1,0:T(4,128)(2,1)S(1)} %get-tuple-element.221), channel_id=1, source_target_pairs={{3,1},{7,5},{11,9},{15,13},{19,17},{23,21},{27,25},{31,29},{35,33}... | collective-permute-start | bytes 393224 | tf_op jit(solution)/shard_map/cond/branch_12_fun/ppermute | solution.py:393
  5.9 14.0 %collective-permute-start.120 = (bf16[4,32,4,128]{3,2,1,0:T(4,128)(2,1)S(1)}, bf16[4,32,4,128]{3,2,1,0:T(4,128)(2,1)S(1)}, u32[]{:S(2)}, u32[]{:S(2)}) collective-permute-start(bf16[4,32,4,128]{3,2,1,0:T(4,128)(2,1)S(1)} %get-tuple-element.221), channel_id=1, source_target_pairs={{3,2},{7,6},{11,10},{15,14},{19,18},{23,22},{27,26},{31,30},{35,34... | collective-permute-start | bytes 393224 | tf_op jit(solution)/shard_map/cond/branch_12_fun/ppermute | solution.py:393
  6.5 18.7 %collective-permute-start.125 = (bf16[4,32,4,128]{3,2,1,0:T(4,128)(2,1)S(1)}, bf16[4,32,4,128]{3,2,1,0:T(4,128)(2,1)S(1)}, u32[]{:S(2)}, u32[]{:S(2)}) collective-permute-start(bf16[4,32,4,128]{3,2,1,0:T(4,128)(2,1)S(1)} %get-tuple-element.222), channel_id=1, source_target_pairs={{0,1},{4,5},{8,9},{12,13},{16,17},{20,21},{24,25},{28,29},{32,33},... | collective-permute-start | bytes 393224 | tf_op jit(solution)/shard_map/cond/branch_12_fun/ppermute | solution.py:393
  10.5 14.7 %collective-permute-start.124 = (bf16[4,32,4,128]{3,2,1,0:T(4,128)(2,1)S(1)}, bf16[4,32,4,128]{3,2,1,0:T(4,128)(2,1)S(1)}, u32[]{:S(2)}, u32[]{:S(2)}) collective-permute-start(bf16[4,32,4,128]{3,2,1,0:T(4,128)(2,1)S(1)} %get-tuple-element.222), channel_id=1, source_target_pairs={{0,2},{4,6},{8,10},{12,14},{16,18},{20,22},{24,26},{28,30},{32,34}... | collective-permute-start | bytes 393224 | tf_op jit(solution)/shard_map/cond/branch_12_fun/ppermute | solution.py:393
  12.7 12.5 %collective-permute-start.123 = (bf16[4,32,4,128]{3,2,1,0:T(4,128)(2,1)S(1)}, bf16[4,32,4,128]{3,2,1,0:T(4,128)(2,1)S(1)}, u32[]{:S(2)}, u32[]{:S(2)}) collective-permute-start(bf16[4,32,4,128]{3,2,1,0:T(4,128)(2,1)S(1)} %get-tuple-element.222), channel_id=1, source_target_pairs={{0,3},{4,7},{8,11},{12,15},{16,19},{20,23},{24,27},{28,31},{32,35}... | collective-permute-start | bytes 393224 | tf_op jit(solution)/shard_map/cond/branch_12_fun/ppermute | solution.py:393
  15.5 14.5 %collective-permute-start.127 = (f32[2,3,32,4,128]{4,3,2,1,0:T(4,128)S(1)}, f32[2,3,32,4,128]{4,3,2,1,0:T(4,128)}, u32[]{:S(2)}, u32[]{:S(2)}) collective-permute-start(f32[2,3,32,4,128]{4,3,2,1,0:T(4,128)S(1)} %get-tuple-element.224), channel_id=1, source_target_pairs={{8,16},{24,32},{40,48},{56,64},{72,80},{88,96},{104,112},{120,128}... | collective-permute-start | bytes 1179656 | tf_op jit(solution)/shard_map/cond/branch_12_fun/ppermute | solution.py:384
  19.9 10.2 %collective-permute-start.126 = (f32[2,3,32,4,128]{4,3,2,1,0:T(4,128)S(1)}, f32[2,3,32,4,128]{4,3,2,1,0:T(4,128)}, u32[]{:S(2)}, u32[]{:S(2)}) collective-permute-start(f32[2,3,32,4,128]{4,3,2,1,0:T(4,128)S(1)} %get-tuple-element.224), channel_id=1, source_target_pairs={{0,8},{8,0},{1,9},{9,1},{2,10},{10,2},{3,11},{11,3},{4,12},{12,4},... | collective-permute-start | bytes 1179656 | tf_op jit(solution)/shard_map/cond/branch_12_fun/ppermute | solution.py:384
  26.2 8.3 %collective-permute-start.129 = (bf16[9,32,4,128]{3,2,1,0:T(4,128)(2,1)}, bf16[9,32,4,128]{3,2,1,0:T(4,128)(2,1)}, u32[]{:S(2)}, u32[]{:S(2)}) collective-permute-start(bf16[9,32,4,128]{3,2,1,0:T(4,128)(2,1)} %pad_maximum_fusion.12), channel_id=1, source_target_pairs={{8,16},{24,32},{40,48},{56,64},{72,80},{88,96},{104,112},{120,128}... | collective-permute-start | bytes 884744 | tf_op jit(solution)/shard_map/cond/branch_12_fun/ppermute | solution.py:384
  28.2 6.4 %collective-permute-start.128 = (bf16[9,32,4,128]{3,2,1,0:T(4,128)(2,1)}, bf16[9,32,4,128]{3,2,1,0:T(4,128)(2,1)}, u32[]{:S(2)}, u32[]{:S(2)}) collective-permute-start(bf16[9,32,4,128]{3,2,1,0:T(4,128)(2,1)} %pad_maximum_fusion.12), channel_id=1, source_target_pairs={{0,8},{8,0},{1,9},{9,1},{2,10},{10,2},{3,11},{11,3},{4,12},{12,4},... | collective-permute-start | bytes 884744 | tf_op jit(solution)/shard_map/cond/branch_12_fun/ppermute | solution.py:384
  34.7 0.7 copy-start
  40.9 5.4 %collective-permute-start.160 = (f32[24,8,128]{2,1,0:T(8,128)S(1)}, f32[24,8,128]{2,1,0:T(8,128)S(1)}, u32[]{:S(2)}, u32[]{:S(2)}) collective-permute-start(f32[24,8,128]{2,1,0:T(8,128)S(1)} %get-tuple-element.272.mine), channel_id=1, source_target_pairs={{0,4},{4,0},{1,5},{5,1},{2,6},{6,2},{3,7},{7,3},{8,12},{12,8},{9,1... | collective-permute-start | bytes 294920 | tf_op jit(solution)/shard_map/ppermute | solution.py:451
  51.7 4.6 %collective-permute-start.161 = (f32[6,8,128]{2,1,0:T(8,128)S(1)}, f32[6,8,128]{2,1,0:T(8,128)S(1)}, u32[]{:S(2)}, u32[]{:S(2)}) collective-permute-start(f32[6,8,128]{2,1,0:T(8,128)S(1)} %get-tuple-element.280.mine), channel_id=1, source_target_pairs={{0,4},{4,0},{1,5},{5,1},{2,6},{6,2},{3,7},{7,3},{8,12},{12,8},{9,1... | collective-permute-start | bytes 73736 | tf_op jit(solution)/shard_map/ppermute | solution.py:459
  57.0 29.3 %all-to-all-start = ((f32[64,2,128]{2,1,0:T(2,128)}), f32[64,2,128]{2,1,0:T(2,128)S(1)}, u32[]{:S(2)}, u32[]{:S(2)}) async-start(f32[64,2,128]{2,1,0:T(2,128)} %broadcast_in_dim.54), calls=%async_computation | async-start | bytes 131072 | tf_op jit(solution)/shard_map/all_to_all | solution.py:464

commit v3 on v2

--- a/solution.py
+++ b/solution.py
@@ -15,6 +15,7 @@
 POWER_SCALE = 0.01
 VERTICAL_ASPECT = 400.0
 TILE = ("row", "core")
+UNROLL = 10
 HALF = 0.5 * TIME_STEP
 FACE = 0.5 * TIME_STEP * VERTICAL_ASPECT
 
@@ -189,7 +190,7 @@
     )
     carry = eliminate(0, at(1), None, carry)
     carry = lax.fori_loop(
-        1, last, lambda j, c: eliminate(j, at(j + 1), at(j - 1), c), carry
+        1, last, lambda j, c: eliminate(j, at(j + 1), at(j - 1), c), carry, unroll=UNROLL
     )
     face, ratio, values, face2, ratio2, ws = carry
     k = at(last)
@@ -282,7 +283,7 @@
         ws = tuple(wrow_in[c, k] + ratio2 * ws[c] for c in range(2))
         return values, ws, keep(k, values, ws, sums)
 
-    _, _, sums = lax.fori_loop(0, last, back, (tuple(nexts), tuple(ws), sums))
+    _, _, sums = lax.fori_loop(0, last, back, (tuple(nexts), tuple(ws), sums), unroll=True)
 
     def level_rows(j, above, below, sums, winds_beyond=None, values_beyond=None):
         k = at(j)
@@ -306,7 +307,7 @@
 
     carry = eliminate(0, at(1), None, (zero, (zero,) * 6, sums))
     face, values, sums = lax.fori_loop(
-        1, last, lambda j, c: eliminate(j, at(j + 1), at(j - 1), c), carry
+        1, last, lambda j, c: eliminate(j, at(j + 1), at(j - 1), c), carry, unroll=UNROLL
     )
     rows, sums = level_rows(
         last, None, at(last - 1), sums, [theirs[WIND2 + c] for c in range(3)], beyond
@@ -338,7 +339,7 @@
         keep(k, values)
         return values
 
-    lax.fori_loop(0, last, back, values)
+    lax.fori_loop(0, last, back, values, unroll=True)
 
 
 def call(kernel, scalars, arrays, outs, scratch):
@@ -353,27 +354,34 @@
     )(*scalars, *arrays)
 
 
-def prepare_kernel(slots, steps, records, code, first, second, arrived):
-    per_device = records.shape[0]
+def prepare_kernel(slots, steps, records, code, both, send, arrived):
+    per_device, fields = records.shape[0], records.shape[1]
+    owners = slots.shape[0] // per_device
     slot_a, slot_b = slots[steps[0]], slots[steps[1]]
-    copy_a = pltpu.make_async_copy(records.at[lax.rem(slot_a, per_device)], first, arrived.at[0])
-    copy_b = pltpu.make_async_copy(records.at[lax.rem(slot_b, per_device)], second, arrived.at[1])
-    copy_a.start()
-    copy_b.start()
-    owners = slots.shape[0] // per_device
-    code[0] = lax.div(slot_a, per_device) * owners + lax.div(slot_b, per_device)
-    copy_a.wait()
-    copy_b.wait()
+    owner_b = lax.div(slot_b, per_device)
+    chosen = jnp.where(lax.axis_index("dir") == owner_b, slot_b, slot_a)
+    targets = (send, both.at[0:fields], both.at[fields : 2 * fields])
+    copies = [
+        pltpu.make_async_copy(records.at[lax.rem(slot, per_device)], target, arrived.at[n])
+        for n, (slot, target) in enumerate(zip((chosen, slot_a, slot_b), targets))
+    ]
+    for copy in copies:
+        copy.start()
+    code[0] = lax.div(slot_a, per_device) * owners + owner_b
+    for copy in copies:
+        copy.wait()
 
 
 def prepare(record_slot, step_record, records):
-    block = jax.ShapeDtypeStruct(records.shape[1:], records.dtype)
+    fields, *block = records.shape[1:]
+    shapes = [(2 * fields, *block), (fields, *block)]
     return pl.pallas_call(
         prepare_kernel,
-        out_shape=[jax.ShapeDtypeStruct((1,), jnp.int32), block, block],
+        out_shape=[jax.ShapeDtypeStruct((1,), jnp.int32)]
+        + [jax.ShapeDtypeStruct(shape, records.dtype) for shape in shapes],
         in_specs=[pl.BlockSpec(memory_space=pltpu.SMEM)] * 2 + [pl.BlockSpec(memory_space=pl.ANY)],
         out_specs=[pl.BlockSpec(memory_space=pltpu.SMEM)] + [pl.BlockSpec(memory_space=pltpu.VMEM)] * 2,
-        scratch_shapes=[pltpu.SemaphoreType.DMA((2,))],
+        scratch_shapes=[pltpu.SemaphoreType.DMA((3,))],
     )(record_slot, step_record, records)
 
 
@@ -384,14 +392,10 @@
     return lax.ppermute(block, "core", [(0, 1), (1, 0)]), lax.ppermute(block, TILE, pairs)
 
 
-def gather_inputs(code, first, second, tangent_in, mask):
+def gather_inputs(code, both, send, tangent_in, mask):
     count = lax.axis_size("dir")
     here = lax.axis_index("dir")
-
-    def send(record, owner):
-        return [
-            lax.ppermute(record, "dir", [(owner, (owner + k) % count)]) for k in range(1, count)
-        ]
+    fields = send.shape[0]
 
     def take(record, owner, got):
         for k, piece in enumerate(got, 1):
@@ -399,18 +403,24 @@
         return record
 
     def branch(a, b):
-        def run(x, y, tangent, groups):
-            got_a, got_b = send(x, a), send(y, b)
+        def run(both, send, tangent, groups):
+            block = both if a == b else send
+            got = [
+                lax.ppermute(block, "dir", [(o, (o + k) % count) for o in sorted({a, b})])
+                for k in range(1, count)
+            ]
             tangents = swap_tiles(tangent)
-            edge = jnp.concatenate(
-                [take(x, a, got_a), take(y, b, got_b), groups.astype(x.dtype)[None]], axis=0
-            )
+            if a == b:
+                recs = [take(both, a, got)]
+            else:
+                recs = [take(both[:fields], a, got), take(both[fields:], b, got)]
+            edge = jnp.concatenate([*recs, groups.astype(send.dtype)[None]], axis=0)
             return edge, *tangents, *swap_tiles(edge)
 
         return run
 
     branches = [branch(a, b) for a in range(count) for b in range(count)]
-    return lax.switch(code, branches, first, second, tangent_in, mask)
+    return lax.switch(code, branches, both, send, tangent_in, mask)
 
 
 def shards(tangent_in, records, record_slot, step_record, turbine_mask, group_weights):
@@ -421,11 +431,6 @@
     vert = lax.axis_index("vert")
     swap = [(0, 1), (1, 0)]
 
-    code, first, second = prepare(record_slot, step_record, records)
-    edge, mate, other, edge_mate, edge_other = gather_inputs(
-        code[0], first, second, tangent_in, turbine_mask
-    )
-
     place = jnp.stack([
         1 - 2 * vert,
         vert * (levels - 1),
@@ -433,6 +438,11 @@
         jnp.where(tile == tiles - 1, 6, 8),
         lax.axis_index("core"),
     ]).astype(jnp.int32)
+
+    code, both, send = prepare(record_slot, step_record, records)
+    edge, mate, other, edge_mate, edge_other = gather_inputs(
+        code[0], both, send, tangent_in, turbine_mask
+    )
 
     def block(*lead):
         return (*lead, 8, spans)

time: 87.6 us -> 81.8 us (0.934)
  the two profiles are of different devices: /device:TPU:1 before, /device:TPU:2 now
where the time goes in v3:
time: 81.8 us; the launch traced here: 81.3 us
  starting transfers between devices  48.2 us (59%)
  waiting for transfers between devices  15.2 us (19%)
  Pallas kernels  10.7 us (13%)
  blocking collectives  2.47 us (3%)
  other arithmetic  1.82 us (2%)
  local copies, waits for them, and re-layouts  1.42 us (2%)
  between operations  1.38 us (2%)
    all_to_all x1, starting transfers between devices, shards(): lax.all_to_all(jnp.broadcast_to(sums[None], (count, directions, spans)),...  19.9 us
    all_to_all x1, waiting for transfers between devices, shards(): lax.all_to_all(jnp.broadcast_to(sums[None], (count, directions, spans)),...  10.6 us
    ppermute x3, starting transfers between devices, run(): lax.ppermute(block, 'dir', [(o, (o + k) % count) for o in sorted({a, b})])  10.4 us
    pallas_call x3, Pallas kernels, call(): pl.pallas_call(kernel, out_shape=[jax.ShapeDtypeStruct(shape, jnp.float32...  8.34 us
    ppermute x2, starting transfers between devices, swap_tiles(): lax.ppermute(block, 'core', [(0, 1), (1, 0)])  6.49 us
    ppermute x1, starting transfers between devices, shards(): answer = lax.ppermute(message, 'vert', swap)  4.28 us
    ppermute x1, starting transfers between devices, shards(): answer2 = lax.ppermute(row, 'vert', swap)  4.26 us
    ppermute x1, waiting for transfers between devices, shards(): answer = lax.ppermute(message, 'vert', swap)  3.05 us
  transfers between devices with their start and end apart: 10, of which 3 were waited for; matrix products, arithmetic and copies ran while one was open for 1% of the time, Pallas kernels for 2%

profile of v3, /device:TPU:2, one launch (start us, length us, event | category | flops | bytes accessed | tf_op | source)
XLA Modules:
  0.0 81.3 jit_solution(11398269899116583395)
XLA Ops:
  0.6 0.0 copy-start.2
  0.7 0.0 copy-start.1
  0.7 2.4 %shard_map.77 = (s32[1]{0:T(128)}, bf16[8,32,4,128]{3,2,1,0:T(4,128)(2,1)S(1)}, bf16[4,32,4,128]{3,2,1,0:T(4,128)(2,1)S(1)}) custom-call(s32[16]{0:T(128)} %slots.1, s32[2]{0:T(128)} %steps.1, bf16[4,4,32,4,128]{4,3,2,1,0:T(4,128)(2,1)} %records.1), custom_call_target="tpu_custom_call" | custom-call | tf_op jit(solution)/shard_map/pallas_call | solution.py:378
  3.7 0.0 copy-done.2
  3.7 0.0 copy-done.1
  3.7 22.5 %conditional.1 = (bf16[9,32,4,128]{3,2,1,0:T(4,128)(2,1)}, f32[2,3,32,4,128]{4,3,2,1,0:T(4,128)}, f32[2,3,32,4,128]{4,3,2,1,0:T(4,128)}, bf16[9,32,4,128]{3,2,1,0:T(4,128)(2,1)}, bf16[9,32,4,128]{3,2,1,0:T(4,128)(2,1)}) conditional(s32[]{:T(128)} %bitcast.21, (s32[]{:T(128)}, bf16[8,32,4,128]{3,2,1,0:T(4,128)(2,1)S(1)}, ...), branch_computations={%region_0.1_spmd, %region_1.2_spmd, %region_2.3_spmd, %region_3.4_... | conditional | flops 704516 | bytes 10649950 | solution.py:423
  3.8 3.4 %collective-permute-start.30 = (bf16[4,32,4,128]{3,2,1,0:T(4,128)(2,1)S(1)}, bf16[4,32,4,128]{3,2,1,0:T(4,128)(2,1)S(1)}, u32[]{:S(2)}, u32[]{:S(2)}) collective-permute-start(bf16[4,32,4,128]{3,2,1,0:T(4,128)(2,1)S(1)} %get-tuple-element.172), channel_id=1, source_target_pairs={{0,1},{1,2},{4,5},{5,6},{8,9},{9,10},{12,13},{13,14},{16,17},{17,1... | collective-permute-start | bytes 393224 | tf_op jit(solution)/shard_map/cond/branch_4_fun/ppermute | solution.py:409
  7.2 1.3 %collective-permute-start.29 = (bf16[4,32,4,128]{3,2,1,0:T(4,128)(2,1)S(1)}, bf16[4,32,4,128]{3,2,1,0:T(4,128)(2,1)S(1)}, u32[]{:S(2)}, u32[]{:S(2)}) collective-permute-start(bf16[4,32,4,128]{3,2,1,0:T(4,128)(2,1)S(1)} %get-tuple-element.172), channel_id=1, source_target_pairs={{0,2},{1,3},{4,6},{5,7},{8,10},{9,11},{12,14},{13,15},{16,18},{17,... | collective-permute-start | bytes 393224 | tf_op jit(solution)/shard_map/cond/branch_4_fun/ppermute | solution.py:409
  8.5 5.7 %collective-permute-start.28 = (bf16[4,32,4,128]{3,2,1,0:T(4,128)(2,1)S(1)}, bf16[4,32,4,128]{3,2,1,0:T(4,128)(2,1)S(1)}, u32[]{:S(2)}, u32[]{:S(2)}) collective-permute-start(bf16[4,32,4,128]{3,2,1,0:T(4,128)(2,1)S(1)} %get-tuple-element.172), channel_id=1, source_target_pairs={{0,3},{1,0},{4,7},{5,4},{8,11},{9,8},{12,15},{13,12},{16,19},{17,1... | collective-permute-start | bytes 393224 | tf_op jit(solution)/shard_map/cond/branch_4_fun/ppermute | solution.py:409
  14.2 1.4 %collective-permute-start.32 = (f32[2,3,32,4,128]{4,3,2,1,0:T(4,128)S(1)}, f32[2,3,32,4,128]{4,3,2,1,0:T(4,128)}, u32[]{:S(2)}, u32[]{:S(2)}) collective-permute-start(f32[2,3,32,4,128]{4,3,2,1,0:T(4,128)S(1)} %get-tuple-element.175), channel_id=1, source_target_pairs={{8,16},{24,32},{40,48},{56,64},{72,80},{88,96},{104,112},{120,128}... | collective-permute-start | bytes 1179656 | tf_op jit(solution)/shard_map/cond/branch_4_fun/ppermute | solution.py:392
  15.6 2.3 %collective-permute-start.31 = (f32[2,3,32,4,128]{4,3,2,1,0:T(4,128)S(1)}, f32[2,3,32,4,128]{4,3,2,1,0:T(4,128)}, u32[]{:S(2)}, u32[]{:S(2)}) collective-permute-start(f32[2,3,32,4,128]{4,3,2,1,0:T(4,128)S(1)} %get-tuple-element.175), channel_id=1, source_target_pairs={{0,8},{8,0},{1,9},{9,1},{2,10},{10,2},{3,11},{11,3},{4,12},{12,4},... | collective-permute-start | bytes 1179656 | tf_op jit(solution)/shard_map/cond/branch_4_fun/ppermute | solution.py:392
  18.0 0.0 collective-permute-done.30
  18.0 0.0 collective-permute-done.29
  18.1 0.0 collective-permute-done.28
  18.1 0.2 select_select_fusion.8
  18.2 0.9 %pad_maximum_fusion.4 = bf16[9,32,4,128]{3,2,1,0:T(4,128)(2,1)} fusion(bf16[1,32,4,128]{3,2,1,0:T(4,128)(2,1)S(1)} %convert_bitcast_fusion.4, bf16[4,32,4,128]{3,2,1,0:T(4,128)(2,1)S(1)} %get-tuple-element.281, bf16[4,32,4,128]{3,2,1,0:T(4,128)(2,1)S(1)} %get-tuple-element.280), kind=kLoop, calls=%fused_computation.15 | loop fusion | flops 294912 | bytes 589824 | tf_op jit(solution)/shard_map/cond/branch_4_fun/concatenate | solution.py:417
  19.2 1.4 %collective-permute-start.34 = (bf16[9,32,4,128]{3,2,1,0:T(4,128)(2,1)}, bf16[9,32,4,128]{3,2,1,0:T(4,128)(2,1)}, u32[]{:S(2)}, u32[]{:S(2)}) collective-permute-start(bf16[9,32,4,128]{3,2,1,0:T(4,128)(2,1)} %pad_maximum_fusion.4), channel_id=1, source_target_pairs={{8,16},{24,32},{40,48},{56,64},{72,80},{88,96},{104,112},{120,128}... | collective-permute-start | bytes 884744 | tf_op jit(solution)/shard_map/cond/branch_4_fun/ppermute | solution.py:392
  20.5 4.1 %collective-permute-start.33 = (bf16[9,32,4,128]{3,2,1,0:T(4,128)(2,1)}, bf16[9,32,4,128]{3,2,1,0:T(4,128)(2,1)}, u32[]{:S(2)}, u32[]{:S(2)}) collective-permute-start(bf16[9,32,4,128]{3,2,1,0:T(4,128)(2,1)} %pad_maximum_fusion.4), channel_id=1, source_target_pairs={{0,8},{8,0},{1,9},{9,1},{2,10},{10,2},{3,11},{11,3},{4,12},{12,4},... | collective-permute-start | bytes 884744 | tf_op jit(solution)/shard_map/cond/branch_4_fun/ppermute | solution.py:392
  24.7 0.0 collective-permute-done.32
  24.7 0.0 collective-permute-done.31
  24.7 0.0 collective-permute-done.34
  24.7 1.5 %collective-permute-done.33 = bf16[9,32,4,128]{3,2,1,0:T(4,128)(2,1)} collective-permute-done((bf16[9,32,4,128]{3,2,1,0:T(4,128)(2,1)}, bf16[9,32,4,128]{3,2,1,0:T(4,128)(2,1)}, u32[]{:S(2)}, u32[]{:S(2)}) %collective-permute-start.33) | collective-permute-done | bytes 294944 | tf_op jit(solution)/shard_map/cond/branch_4_fun/ppermute | solution.py:392
  26.2 0.1 stack.23.place
  26.3 0.0 copy-start
  26.3 0.7 copy-done
  27.0 3.7 %shard_map.78 = (f32[24,8,128]{2,1,0:T(8,128)S(1)}, f32[32,8,128]{2,1,0:T(8,128)S(1)}, f32[6,32,8,128]{3,2,1,0:T(8,128)S(1)}, f32[2,32,8,128]{3,2,1,0:T(8,128)S(...) custom-call(s32[5]{0:T(128)S(1)} %stack.23.place, ...), custom_call_target="tpu_custom_call" | custom-call | tf_op jit(solution)/shard_map/pallas_call | solution.py:346
  30.7 4.3 %collective-permute-start.112 = (f32[24,8,128]{2,1,0:T(8,128)S(1)}, f32[24,8,128]{2,1,0:T(8,128)S(1)}, u32[]{:S(2)}, u32[]{:S(2)}) collective-permute-start(f32[24,8,128]{2,1,0:T(8,128)S(1)} %get-tuple-element.260.mine), channel_id=1, source_target_pairs={{0,4},{4,0},{1,5},{5,1},{2,6},{6,2},{3,7},{7,3},{8,12},{12,8},{9,1... | collective-permute-start | bytes 294920 | tf_op jit(solution)/shard_map/ppermute | solution.py:461
  35.0 3.1 %collective-permute-done.112.theirs = f32[24,8,128]{2,1,0:T(8,128)S(1)} collective-permute-done((f32[24,8,128]{2,1,0:T(8,128)S(1)}, f32[24,8,128]{2,1,0:T(8,128)S(1)}, u32[]{:S(2)}, u32[]{:S(2)}) %collective-permute-start.112) | collective-permute-done | bytes 98336 | tf_op jit(solution)/shard_map/ppermute | solution.py:461
  38.0 3.2 %shard_map.79 = (f32[6,8,128]{2,1,0:T(8,128)S(1)}, f32[6,32,8,128]{3,2,1,0:T(8,128)S(1)}, f32[2,8,128]{2,1,0:T(8,128)S(1)}, f32[2,128]{1,0:T(2,128)S(1)}) custom-call(s32[5]{0:T(128)S(1)} %stack.23.place, f32[2,8]{1,0:T(2,128)S(1)} %copy-done, f32[24,8,128]{2,1,0:T(8,128)S(1)} %get-tuple-element.260.mine, f32[24,8,128]{2,1,0:T(8,128)S(1)} %collective-permute-done.112.theirs, ...), custom_call_target="tpu_custom_call" | custom-call | tf_op jit(solution)/shard_map/pallas_call | solution.py:346
  41.2 4.3 %collective-permute-start.113 = (f32[6,8,128]{2,1,0:T(8,128)S(1)}, f32[6,8,128]{2,1,0:T(8,128)S(1)}, u32[]{:S(2)}, u32[]{:S(2)}) collective-permute-start(f32[6,8,128]{2,1,0:T(8,128)S(1)} %get-tuple-element.268.mine), channel_id=1, source_target_pairs={{0,4},{4,0},{1,5},{5,1},{2,6},{6,2},{3,7},{7,3},{8,12},{12,8},{9,1... | collective-permute-start | bytes 73736 | tf_op jit(solution)/shard_map/ppermute | solution.py:469
  45.5 2.5 %psum.7 = f32[2,128]{1,0:T(2,128)S(1)} all-reduce(f32[2,128]{1,0:T(2,128)S(1)} %get-tuple-element.269), channel_id=1, replica_groups=mesh['row'=32,'core'=2,'vert'=2,'dir'=4] {'core'}, use_global_device_ids=true, to_apply=%region_16.17 | all-reduce | flops 256 | bytes 2048 | tf_op jit(solution)/shard_map/psum | solution.py:471
  48.0 0.0 collective-permute-done.113.theirs
  48.0 0.6 broadcast_in_dim.54
  48.6 19.9 %all-to-all-start = ((f32[64,2,128]{2,1,0:T(2,128)}), f32[64,2,128]{2,1,0:T(2,128)S(1)}, u32[]{:S(2)}, u32[]{:S(2)}) async-start(f32[64,2,128]{2,1,0:T(2,128)} %broadcast_in_dim.54), calls=%async_computation | async-start | bytes 131072 | tf_op jit(solution)/shard_map/all_to_all | solution.py:474
  68.5 1.4 %shard_map.80 = f32[2,3,32,4,128]{4,3,2,1,0:T(4,128)} custom-call(s32[5]{0:T(128)S(1)} %stack.23.place, f32[6,8,128]{2,1,0:T(8,128)S(1)} %get-tuple-element.268.mine, f32[6,8,128]{2,1,0:T(8,128)S(1)} %collective-permute-done.113.theirs, f32[2,8,128]{2,1,0:T(8,128)S(1)} %get-tuple-element.271.middle, f32[32,8,128]{2,1,0:T(8,128)S(1)} %get-tuple-element.264.ratio2_in.ratio_in, ...), custom_call_target="tpu_custom_call" | custom-call | tf_op jit(solution)/shard_map/pallas_call | solution.py:346
  70.0 10.6 %all-to-all-done = f32[64,2,128]{2,1,0:T(2,128)S(1)} async-done(((f32[64,2,128]{2,1,0:T(2,128)}), f32[64,2,128]{2,1,0:T(2,128)S(1)}, u32[]{:S(2)}, u32[]{:S(2)}) %all-to-all-start) | async-done | bytes 65568 | tf_op jit(solution)/shard_map/all_to_all | solution.py:474
  80.6 0.2 reduce_sum.9
  80.8 0.5 broadcast_multiply_fusion
  (1 shorter events, 0.0 us)
Async XLA Ops:
  0.6 3.1 %copy-start.2 = (f32[2,3,32,4,128]{4,3,2,1,0:T(4,128)S(1)}, f32[2,3,32,4,128]{4,3,2,1,0:T(4,128)}, u32[]{:S(2)}) copy-start(f32[2,3,32,4,128]{4,3,2,1,0:T(4,128)} %own.1) | copy-start | bytes 1179652
  0.7 3.1 %copy-start.1 = (s32[32,4,128]{2,1,0:T(4,128)S(1)}, s32[32,4,128]{2,1,0:T(4,128)}, u32[]{:S(2)}) copy-start(s32[32,4,128]{2,1,0:T(4,128)} %param.26) | copy-start | bytes 196612
  3.8 14.3 %collective-permute-start.30 = (bf16[4,32,4,128]{3,2,1,0:T(4,128)(2,1)S(1)}, bf16[4,32,4,128]{3,2,1,0:T(4,128)(2,1)S(1)}, u32[]{:S(2)}, u32[]{:S(2)}) collective-permute-start(bf16[4,32,4,128]{3,2,1,0:T(4,128)(2,1)S(1)} %get-tuple-element.172), channel_id=1, source_target_pairs={{0,1},{1,2},{4,5},{5,6},{8,9},{9,10},{12,13},{13,14},{16,17},{17,1... | collective-permute-start | bytes 393224 | tf_op jit(solution)/shard_map/cond/branch_4_fun/ppermute | solution.py:409
  7.2 10.9 %collective-permute-start.29 = (bf16[4,32,4,128]{3,2,1,0:T(4,128)(2,1)S(1)}, bf16[4,32,4,128]{3,2,1,0:T(4,128)(2,1)S(1)}, u32[]{:S(2)}, u32[]{:S(2)}) collective-permute-start(bf16[4,32,4,128]{3,2,1,0:T(4,128)(2,1)S(1)} %get-tuple-element.172), channel_id=1, source_target_pairs={{0,2},{1,3},{4,6},{5,7},{8,10},{9,11},{12,14},{13,15},{16,18},{17,... | collective-permute-start | bytes 393224 | tf_op jit(solution)/shard_map/cond/branch_4_fun/ppermute | solution.py:409
  8.5 9.6 %collective-permute-start.28 = (bf16[4,32,4,128]{3,2,1,0:T(4,128)(2,1)S(1)}, bf16[4,32,4,128]{3,2,1,0:T(4,128)(2,1)S(1)}, u32[]{:S(2)}, u32[]{:S(2)}) collective-permute-start(bf16[4,32,4,128]{3,2,1,0:T(4,128)(2,1)S(1)} %get-tuple-element.172), channel_id=1, source_target_pairs={{0,3},{1,0},{4,7},{5,4},{8,11},{9,8},{12,15},{13,12},{16,19},{17,1... | collective-permute-start | bytes 393224 | tf_op jit(solution)/shard_map/cond/branch_4_fun/ppermute | solution.py:409
  14.2 10.5 %collective-permute-start.32 = (f32[2,3,32,4,128]{4,3,2,1,0:T(4,128)S(1)}, f32[2,3,32,4,128]{4,3,2,1,0:T(4,128)}, u32[]{:S(2)}, u32[]{:S(2)}) collective-permute-start(f32[2,3,32,4,128]{4,3,2,1,0:T(4,128)S(1)} %get-tuple-element.175), channel_id=1, source_target_pairs={{8,16},{24,32},{40,48},{56,64},{72,80},{88,96},{104,112},{120,128}... | collective-permute-start | bytes 1179656 | tf_op jit(solution)/shard_map/cond/branch_4_fun/ppermute | solution.py:392
  15.6 9.1 %collective-permute-start.31 = (f32[2,3,32,4,128]{4,3,2,1,0:T(4,128)S(1)}, f32[2,3,32,4,128]{4,3,2,1,0:T(4,128)}, u32[]{:S(2)}, u32[]{:S(2)}) collective-permute-start(f32[2,3,32,4,128]{4,3,2,1,0:T(4,128)S(1)} %get-tuple-element.175), channel_id=1, source_target_pairs={{0,8},{8,0},{1,9},{9,1},{2,10},{10,2},{3,11},{11,3},{4,12},{12,4},... | collective-permute-start | bytes 1179656 | tf_op jit(solution)/shard_map/cond/branch_4_fun/ppermute | solution.py:392
  19.2 5.5 %collective-permute-start.34 = (bf16[9,32,4,128]{3,2,1,0:T(4,128)(2,1)}, bf16[9,32,4,128]{3,2,1,0:T(4,128)(2,1)}, u32[]{:S(2)}, u32[]{:S(2)}) collective-permute-start(bf16[9,32,4,128]{3,2,1,0:T(4,128)(2,1)} %pad_maximum_fusion.4), channel_id=1, source_target_pairs={{8,16},{24,32},{40,48},{56,64},{72,80},{88,96},{104,112},{120,128}... | collective-permute-start | bytes 884744 | tf_op jit(solution)/shard_map/cond/branch_4_fun/ppermute | solution.py:392
  20.5 5.7 %collective-permute-start.33 = (bf16[9,32,4,128]{3,2,1,0:T(4,128)(2,1)}, bf16[9,32,4,128]{3,2,1,0:T(4,128)(2,1)}, u32[]{:S(2)}, u32[]{:S(2)}) collective-permute-start(bf16[9,32,4,128]{3,2,1,0:T(4,128)(2,1)} %pad_maximum_fusion.4), channel_id=1, source_target_pairs={{0,8},{8,0},{1,9},{9,1},{2,10},{10,2},{3,11},{11,3},{4,12},{12,4},... | collective-permute-start | bytes 884744 | tf_op jit(solution)/shard_map/cond/branch_4_fun/ppermute | solution.py:392
  26.3 0.7 copy-start
  30.7 7.3 %collective-permute-start.112 = (f32[24,8,128]{2,1,0:T(8,128)S(1)}, f32[24,8,128]{2,1,0:T(8,128)S(1)}, u32[]{:S(2)}, u32[]{:S(2)}) collective-permute-start(f32[24,8,128]{2,1,0:T(8,128)S(1)} %get-tuple-element.260.mine), channel_id=1, source_target_pairs={{0,4},{4,0},{1,5},{5,1},{2,6},{6,2},{3,7},{7,3},{8,12},{12,8},{9,1... | collective-permute-start | bytes 294920 | tf_op jit(solution)/shard_map/ppermute | solution.py:461
  41.2 6.7 %collective-permute-start.113 = (f32[6,8,128]{2,1,0:T(8,128)S(1)}, f32[6,8,128]{2,1,0:T(8,128)S(1)}, u32[]{:S(2)}, u32[]{:S(2)}) collective-permute-start(f32[6,8,128]{2,1,0:T(8,128)S(1)} %get-tuple-element.268.mine), channel_id=1, source_target_pairs={{0,4},{4,0},{1,5},{5,1},{2,6},{6,2},{3,7},{7,3},{8,12},{12,8},{9,1... | collective-permute-start | bytes 73736 | tf_op jit(solution)/shard_map/ppermute | solution.py:469
  48.6 32.0 %all-to-all-start = ((f32[64,2,128]{2,1,0:T(2,128)}), f32[64,2,128]{2,1,0:T(2,128)S(1)}, u32[]{:S(2)}, u32[]{:S(2)}) async-start(f32[64,2,128]{2,1,0:T(2,128)} %broadcast_in_dim.54), calls=%async_computation | async-start | bytes 131072 | tf_op jit(solution)/shard_map/all_to_all | solution.py:474

commit v4 on v3

--- a/solution.py
+++ b/solution.py
@@ -30,7 +30,7 @@
     return pltpu.roll(values, (-offset) % values.shape[-1], 1)
 
 
-def wind_terms(winds, turbines, level, above, below, sign, beyond=None):
+def wind_terms(winds, turbines, weights, level, above, below, sign):
     wind = [window(winds, c, level) for c in range(3)]
     visc = TIME_STEP * window(winds, 3, level)
     mask = turbines[level, 2:10, :]
@@ -51,18 +51,23 @@
         slope = (TIME_STEP * 8.0 / 12.0) * near - (TIME_STEP / 12.0) * far
         by_second.append(slope + along * wind[c] * wind[1])
         vertical = jnp.zeros_like(speed)
-        if beyond is not None:
-            vertical = vertical + beyond[c]
-        elif above is not None:
+        if above is not None:
             vertical = vertical + window(winds, c, above)
         if below is not None:
             vertical = vertical - window(winds, c, below)
         by_third.append((HALF * sign) * vertical)
+    speed_step = TIME_STEP * speed
+    force = []
+    for d in range(weights.shape[0]):
+        source = jnp.zeros_like(speed_step)
+        for g in range(weights.shape[1]):
+            source = jnp.where(mask == float(g + 1), weights[d, g], source)
+        force.append(source * speed_step)
     first = (TIME_STEP * 8.0 / 12.0) * wind[0]
     second = (TIME_STEP * 8.0 / 12.0) * wind[1]
     return dict(
         wind=wind,
-        mask=mask,
+        force=force,
         turbine=turbine,
         speed=speed,
         center=1.0 - 4.0 * visc - drag * speed,
@@ -77,16 +82,9 @@
     )
 
 
-def right_side(tangents, weights, terms, level, above, below, beyond=None):
-    speed_step = TIME_STEP * terms["speed"]
-    groups = weights.shape[1]
-    hits = [terms["mask"] == float(g + 1) for g in range(groups)]
+def right_side(tangents, terms, level, above, below, beyond=None):
     rows = []
-    for d in range(weights.shape[0]):
-        source = jnp.zeros_like(speed_step)
-        for g in range(groups):
-            source = jnp.where(hits[g], weights[d, g], source)
-        force = source * speed_step
+    for d, force in enumerate(terms["force"]):
         own = [window(tangents, 3 * d + i, level) for i in range(3)]
         for i in range(3):
             field = 3 * d + i
@@ -152,8 +150,8 @@
 
     def level_rows(j, above, below):
         k = at(j)
-        terms = wind_terms(winds, turbines, k, above, below, sign)
-        rows = right_side(tangents, weights, terms, k, above, below)
+        terms = wind_terms(winds, turbines, weights, k, above, below, sign)
+        rows = right_side(tangents, terms, k, above, below)
         for c in range(2):
             power_out[c, k] = terms["turbine"] * terms["speed"] * terms["wind"][c]
         wind2 = [window(winds2, c, k) for c in range(2)]
@@ -209,14 +207,17 @@
         message[WROW + c] = wrows[c] + face2 * ws[c]
 
 
-def second_kernel(place, weights, mine, theirs, ratio_in, value_in, power_in, ratio2_in, inverse2_in,
-                  face2_in, wrow_in, edge_mate, edge, edge_other,
-                  row_out, value_out, middle_out, sums_out, tangents, winds, turbines, adjoint):
+SINGLE = ("center", "x_up", "x_down", "x_far", "y_up", "y_down", "y_far", "z")
+TERMS = len(SINGLE) + 3 + 9
+
+
+def terms_kernel(place, weights, edge_mate, edge, edge_other, out, winds, turbines):
     levels = edge.shape[1]
     last = levels - 1
     sign = place[0].astype(jnp.float32)
     base = place[1]
     step = place[0]
+    directions = weights.shape[0]
 
     def at(j):
         return base + step * j
@@ -233,7 +234,49 @@
     pl.when(place[4] == 0)(lambda: sides(edge_other, edge_mate))
     pl.when(place[4] == 1)(lambda: sides(edge_mate, edge_other))
 
-    zero = jnp.zeros((8, edge.shape[3]), jnp.float32)
+    def level_terms(j, above, below):
+        k = at(j)
+        terms = wind_terms(winds, turbines, weights, k, above, below, sign)
+        values = [terms[name] for name in SINGLE] + terms["wind"] + terms["force"]
+        for part in terms["by"]:
+            values += part
+        for n, value in enumerate(values):
+            out[n, k] = value
+
+    level_terms(0, at(1), None)
+
+    def body(j, carry):
+        level_terms(j, at(j + 1), at(j - 1))
+        return carry
+
+    lax.fori_loop(1, last, body, 0, unroll=UNROLL)
+    level_terms(last, None, at(last - 1))
+
+
+def stored_terms(store, level):
+    terms = {name: store[n, level] for n, name in enumerate(SINGLE)}
+    start = len(SINGLE)
+    terms["wind"] = [store[start + i, level] for i in range(3)]
+    count = store.shape[0] - TERMS
+    terms["force"] = [store[start + 3 + d, level] for d in range(count)]
+    start += 3 + count
+    terms["by"] = [[store[start + 3 * c + i, level] for i in range(3)] for c in range(3)]
+    return terms
+
+
+def second_kernel(scale, place, mine, theirs, ratio_in, value_in, power_in, ratio2_in, inverse2_in,
+                  face2_in, wrow_in, store,
+                  row_out, value_out, middle_out, sums_out, tangents, adjoint):
+    levels = ratio_in.shape[0]
+    last = levels - 1
+    sign = place[0].astype(jnp.float32)
+    base = place[1]
+    step = place[0]
+
+    def at(j):
+        return base + step * j
+
+    zero = jnp.zeros(ratio_in.shape[1:], jnp.float32)
     layer = lax.broadcasted_iota(jnp.int32, zero.shape, 0)
     inside = jnp.logical_and(layer >= place[2], layer < place[3])
     center = jnp.logical_and(layer >= 2, layer < 6)
@@ -285,10 +328,13 @@
 
     _, _, sums = lax.fori_loop(0, last, back, (tuple(nexts), tuple(ws), sums), unroll=True)
 
-    def level_rows(j, above, below, sums, winds_beyond=None, values_beyond=None):
+    def level_rows(j, above, below, sums, values_beyond=None):
         k = at(j)
-        terms = wind_terms(winds, turbines, k, above, below, sign, winds_beyond)
-        rows = right_side(tangents, weights, terms, k, above, below, values_beyond)
+        terms = stored_terms(store, k)
+        if values_beyond is not None:
+            for i in range(3):
+                terms["by"][2][i] += (HALF * sign) * theirs[WIND2 + i]
+        rows = right_side(tangents, terms, k, above, below, values_beyond)
         sums = tuple(
             sums[d] + adjoint[0, k] * rows[3 * d] + adjoint[1, k] * rows[3 * d + 1]
             for d in range(2)
@@ -309,13 +355,13 @@
     face, values, sums = lax.fori_loop(
         1, last, lambda j, c: eliminate(j, at(j + 1), at(j - 1), c), carry, unroll=UNROLL
     )
-    rows, sums = level_rows(
-        last, None, at(last - 1), sums, [theirs[WIND2 + c] for c in range(3)], beyond
-    )
+    rows, sums = level_rows(last, None, at(last - 1), sums, beyond)
     for field in range(6):
         row_out[field] = rows[field] + face * values[field]
     for d in range(2):
-        sums_out[d : d + 1, :] = jnp.sum(jnp.where(center, sums[d], 0.0), axis=0, keepdims=True)
+        sums_out[d : d + 1, :] = scale * jnp.sum(
+            jnp.where(center, sums[d], 0.0), axis=0, keepdims=True
+        )
 
 
 def third_kernel(place, mine, theirs, middle, ratio_in, value_in, out):
@@ -354,7 +400,7 @@
     )(*scalars, *arrays)
 
 
-def prepare_kernel(slots, steps, records, code, both, send, arrived):
+def prepare_kernel(slots, steps, records, groups, code, both, send, mask, groups_here, arrived):
     per_device, fields = records.shape[0], records.shape[1]
     owners = slots.shape[0] // per_device
     slot_a, slot_b = slots[steps[0]], slots[steps[1]]
@@ -365,24 +411,30 @@
         pltpu.make_async_copy(records.at[lax.rem(slot, per_device)], target, arrived.at[n])
         for n, (slot, target) in enumerate(zip((chosen, slot_a, slot_b), targets))
     ]
+    copies.append(pltpu.make_async_copy(groups, groups_here, arrived.at[3]))
     for copy in copies:
         copy.start()
     code[0] = lax.div(slot_a, per_device) * owners + owner_b
-    for copy in copies:
+    copies[3].wait()
+    mask[0] = groups_here[...].astype(jnp.float32).astype(mask.dtype)
+    for copy in copies[:3]:
         copy.wait()
 
 
-def prepare(record_slot, step_record, records):
+def prepare(record_slot, step_record, records, turbine_mask):
     fields, *block = records.shape[1:]
-    shapes = [(2 * fields, *block), (fields, *block)]
+    shapes = [(2 * fields, *block), (fields, *block), (1, *block)]
     return pl.pallas_call(
         prepare_kernel,
         out_shape=[jax.ShapeDtypeStruct((1,), jnp.int32)]
         + [jax.ShapeDtypeStruct(shape, records.dtype) for shape in shapes],
-        in_specs=[pl.BlockSpec(memory_space=pltpu.SMEM)] * 2 + [pl.BlockSpec(memory_space=pl.ANY)],
-        out_specs=[pl.BlockSpec(memory_space=pltpu.SMEM)] + [pl.BlockSpec(memory_space=pltpu.VMEM)] * 2,
-        scratch_shapes=[pltpu.SemaphoreType.DMA((3,))],
-    )(record_slot, step_record, records)
+        in_specs=[pl.BlockSpec(memory_space=pltpu.SMEM)] * 2 + [pl.BlockSpec(memory_space=pl.ANY)] * 2,
+        out_specs=[pl.BlockSpec(memory_space=pltpu.SMEM)] + [pl.BlockSpec(memory_space=pltpu.VMEM)] * 3,
+        scratch_shapes=[
+            pltpu.VMEM(turbine_mask.shape, turbine_mask.dtype),
+            pltpu.SemaphoreType.DMA((4,)),
+        ],
+    )(record_slot, step_record, records, turbine_mask)
 
 
 def swap_tiles(block):
@@ -403,7 +455,7 @@
         return record
 
     def branch(a, b):
-        def run(both, send, tangent, groups):
+        def run(both, send, tangent, mask):
             block = both if a == b else send
             got = [
                 lax.ppermute(block, "dir", [(o, (o + k) % count) for o in sorted({a, b})])
@@ -414,7 +466,7 @@
                 recs = [take(both, a, got)]
             else:
                 recs = [take(both[:fields], a, got), take(both[fields:], b, got)]
-            edge = jnp.concatenate([*recs, groups.astype(send.dtype)[None]], axis=0)
+            edge = jnp.concatenate([*recs, mask], axis=0)
             return edge, *tangents, *swap_tiles(edge)
 
         return run
@@ -439,9 +491,9 @@
         lax.axis_index("core"),
     ]).astype(jnp.int32)
 
-    code, both, send = prepare(record_slot, step_record, records)
+    code, both, send, mask = prepare(record_slot, step_record, records, turbine_mask)
     edge, mate, other, edge_mate, edge_other = gather_inputs(
-        code[0], both, send, tangent_in, turbine_mask
+        code[0], both, send, tangent_in, mask
     )
 
     def block(*lead):
@@ -459,23 +511,29 @@
         (wide(fields, levels), wide(4, levels), wide(4, levels), wide(levels)),
     )
     answer = lax.ppermute(message, "vert", swap)
+    (store,) = call(
+        terms_kernel,
+        (place, group_weights),
+        (edge_mate, edge, edge_other),
+        (block(TERMS + directions, levels),),
+        (wide(4, levels), wide(levels)),
+    )
+    cells = levels * lax.axis_size("vert") * layers * tiles * spans
     row, value2, middle, sums = call(
-        second_kernel,
-        (place, group_weights),
-        (message, answer, ratio, value, power, ratio2, inverse2, face2, wrow, edge_mate, edge, edge_other),
+        functools.partial(second_kernel, POWER_SCALE / math.sqrt(cells)),
+        (place,),
+        (message, answer, ratio, value, power, ratio2, inverse2, face2, wrow, store),
         (block(fields), block(fields, levels), block(2), (directions, spans)),
-        (wide(fields, levels), wide(4, levels), wide(levels), block(2, levels)),
+        (wide(fields, levels), block(2, levels)),
     )
     answer2 = lax.ppermute(row, "vert", swap)
 
     sums = lax.psum(sums, "core")
-    sums, answer2 = lax.optimization_barrier((sums, answer2))
     count = lax.axis_size("row") * lax.axis_size("vert")
     gathered = lax.all_to_all(
         jnp.broadcast_to(sums[None], (count, directions, spans)), ("row", "vert"), 0, 0, tiled=True
     )
-    cells = levels * lax.axis_size("vert") * layers * tiles * spans
-    power_out = jnp.sum(gathered, axis=(0, 2)) * (POWER_SCALE / math.sqrt(cells))
+    power_out = jnp.sum(gathered, axis=(0, 2))
 
     (tangent_out,) = call(
         third_kernel,

time: 81.8 us -> 77.1 us (0.943)
  the two profiles are of different devices: /device:TPU:2 before, /device:TPU:1 now
where the time goes in v4:
time: 77.1 us; the launch traced here: 76.7 us
  starting transfers between devices  45.9 us (60%)
  waiting for transfers between devices  12.3 us (16%)
  Pallas kernels  11.9 us (15%)
  blocking collectives  2.48 us (3%)
  other arithmetic  1.8 us (2%)
  between operations  1.37 us (2%)
    all_to_all x1, starting transfers between devices, shards(): lax.all_to_all(jnp.broadcast_to(sums[None], (count, directions, spans)),...  18.7 us
    pallas_call x4, Pallas kernels, call(): pl.pallas_call(kernel, out_shape=[jax.ShapeDtypeStruct(shape, jnp.float32...  9.61 us
    ppermute x3, starting transfers between devices, run(): lax.ppermute(block, 'dir', [(o, (o + k) % count) for o in sorted({a, b})])  9.55 us
    ppermute x2, starting transfers between devices, swap_tiles(): lax.ppermute(block, 'core', [(0, 1), (1, 0)])  6.59 us
    ppermute x2, starting transfers between devices, swap_tiles(): lax.ppermute(block, TILE, pairs)  6.24 us
    all_to_all x1, waiting for transfers between devices, shards(): lax.all_to_all(jnp.broadcast_to(sums[None], (count, directions, spans)),...  4.58 us
    ppermute x2, waiting for transfers between devices, swap_tiles(): lax.ppermute(block, TILE, pairs)  4.48 us
    ppermute x1, starting transfers between devices, shards(): answer2 = lax.ppermute(row, 'vert', swap)  2.92 us
  transfers between devices with their start and end apart: 10, of which 4 were waited for; matrix products, arithmetic and copies ran while one was open for 1% of the time, Pallas kernels for 5%

profile of v4, /device:TPU:1, one launch (start us, length us, event | category | flops | bytes accessed | tf_op | source)
XLA Modules:
  0.0 76.7 jit_solution(18278832138611197535)
XLA Ops:
  0.6 2.3 %shard_map.77 = (s32[1]{0:T(128)}, bf16[8,32,4,128]{3,2,1,0:T(4,128)(2,1)S(1)}, bf16[4,32,4,128]{3,2,1,0:T(4,128)(2,1)S(1)}, bf16[1,32,4,128]{3,2,1,0:T(4,128)(2,1)S(1)}) custom-call(s32[16]{0:T(128)} %slots.1, s32[2]{0:T(128)} %steps.1, bf16[4,4,32,4,128]{4,3,2,1,0:T(4,128)(2,1)} %records.1, s32[32,4,128]{2,1,0:T(4,128)} %groups.1), custom_call_target="tpu_custom_call" | custom-call | tf_op jit(solution)/shard_map/pallas_call | solution.py:427
  3.6 0.0 copy-start
  3.6 28.1 %conditional.1 = (bf16[9,32,4,128]{3,2,1,0:T(4,128)(2,1)}, f32[2,3,32,4,128]{4,3,2,1,0:T(4,128)}, f32[2,3,32,4,128]{4,3,2,1,0:T(4,128)}, bf16[9,32,4,128]{3,2,1,0:T(4,128)(2,1)}, bf16[9,32,4,128]{3,2,1,0:T(4,128)(2,1)}) conditional(s32[]{:T(128)} %bitcast.5, (s32[]{:T(128)}, bf16[8,32,4,128]{3,2,1,0:T(4,128)(2,1)S(1)}, ...), branch_computations={%region_0.1_spmd, %region_1.2_spmd, %region_2.3_spmd, %region_3.4_... | conditional | flops 688132 | bytes 10551646 | solution.py:475
  3.7 3.9 %collective-permute-start.23 = (bf16[4,32,4,128]{3,2,1,0:T(4,128)(2,1)S(1)}, bf16[4,32,4,128]{3,2,1,0:T(4,128)(2,1)S(1)}, u32[]{:S(2)}, u32[]{:S(2)}) collective-permute-start(bf16[4,32,4,128]{3,2,1,0:T(4,128)(2,1)S(1)} %get-tuple-element.167), channel_id=1, source_target_pairs={{0,1},{3,0},{4,5},{7,4},{8,9},{11,8},{12,13},{15,12},{16,17},{19,1... | collective-permute-start | bytes 393224 | tf_op jit(solution)/shard_map/cond/branch_3_fun/ppermute | solution.py:461
  7.6 2.2 %collective-permute-start.22 = (bf16[4,32,4,128]{3,2,1,0:T(4,128)(2,1)S(1)}, bf16[4,32,4,128]{3,2,1,0:T(4,128)(2,1)S(1)}, u32[]{:S(2)}, u32[]{:S(2)}) collective-permute-start(bf16[4,32,4,128]{3,2,1,0:T(4,128)(2,1)S(1)} %get-tuple-element.167), channel_id=1, source_target_pairs={{0,2},{3,1},{4,6},{7,5},{8,10},{11,9},{12,14},{15,13},{16,18},{19,... | collective-permute-start | bytes 393224 | tf_op jit(solution)/shard_map/cond/branch_3_fun/ppermute | solution.py:461
  9.8 3.4 %collective-permute-start.21 = (bf16[4,32,4,128]{3,2,1,0:T(4,128)(2,1)S(1)}, bf16[4,32,4,128]{3,2,1,0:T(4,128)(2,1)S(1)}, u32[]{:S(2)}, u32[]{:S(2)}) collective-permute-start(bf16[4,32,4,128]{3,2,1,0:T(4,128)(2,1)S(1)} %get-tuple-element.167), channel_id=1, source_target_pairs={{0,3},{3,2},{4,7},{7,6},{8,11},{11,10},{12,15},{15,14},{16,19},{19... | collective-permute-start | bytes 393224 | tf_op jit(solution)/shard_map/cond/branch_3_fun/ppermute | solution.py:461
  13.2 4.3 %collective-permute-start.25 = (f32[2,3,32,4,128]{4,3,2,1,0:T(4,128)}, f32[2,3,32,4,128]{4,3,2,1,0:T(4,128)}, u32[]{:S(2)}, u32[]{:S(2)}) collective-permute-start(f32[2,3,32,4,128]{4,3,2,1,0:T(4,128)} %get-tuple-element.170), channel_id=1, source_target_pairs={{8,16},{24,32},{40,48},{56,64},{72,80},{88,96},{104,112},{120,128}... | collective-permute-start | bytes 1179656 | tf_op jit(solution)/shard_map/cond/branch_3_fun/ppermute | solution.py:444
  17.6 4.7 %collective-permute-start.24 = (f32[2,3,32,4,128]{4,3,2,1,0:T(4,128)}, f32[2,3,32,4,128]{4,3,2,1,0:T(4,128)}, u32[]{:S(2)}, u32[]{:S(2)}) collective-permute-start(f32[2,3,32,4,128]{4,3,2,1,0:T(4,128)} %get-tuple-element.170), channel_id=1, source_target_pairs={{0,8},{8,0},{1,9},{9,1},{2,10},{10,2},{3,11},{11,3},{4,12},{12,4},... | collective-permute-start | bytes 1179656 | tf_op jit(solution)/shard_map/cond/branch_3_fun/ppermute | solution.py:444
  22.3 0.0 collective-permute-done.23
  22.3 0.0 collective-permute-done.22
  22.3 0.0 collective-permute-done.21
  22.3 0.2 select_select_fusion.6
  22.5 0.9 %pad_maximum_fusion.3 = bf16[9,32,4,128]{3,2,1,0:T(4,128)(2,1)} fusion(bf16[1,32,4,128]{3,2,1,0:T(4,128)(2,1)S(1)} %get-tuple-element.169, bf16[4,32,4,128]{3,2,1,0:T(4,128)(2,1)S(1)} %get-tuple-element.277, bf16[4,32,4,128]{3,2,1,0:T(4,128)(2,1)S(1)} %get-tuple-element.276), kind=kLoop, calls=%fused_computation.8 | loop fusion | flops 294912 | bytes 589824 | tf_op jit(solution)/shard_map/cond/branch_3_fun/concatenate | solution.py:469
  23.4 1.9 %collective-permute-start.27 = (bf16[9,32,4,128]{3,2,1,0:T(4,128)(2,1)}, bf16[9,32,4,128]{3,2,1,0:T(4,128)(2,1)}, u32[]{:S(2)}, u32[]{:S(2)}) collective-permute-start(bf16[9,32,4,128]{3,2,1,0:T(4,128)(2,1)} %pad_maximum_fusion.3), channel_id=1, source_target_pairs={{8,16},{24,32},{40,48},{56,64},{72,80},{88,96},{104,112},{120,128}... | collective-permute-start | bytes 884744 | tf_op jit(solution)/shard_map/cond/branch_3_fun/ppermute | solution.py:444
  25.3 1.9 %collective-permute-start.26 = (bf16[9,32,4,128]{3,2,1,0:T(4,128)(2,1)}, bf16[9,32,4,128]{3,2,1,0:T(4,128)(2,1)}, u32[]{:S(2)}, u32[]{:S(2)}) collective-permute-start(bf16[9,32,4,128]{3,2,1,0:T(4,128)(2,1)} %pad_maximum_fusion.3), channel_id=1, source_target_pairs={{0,8},{8,0},{1,9},{9,1},{2,10},{10,2},{3,11},{11,3},{4,12},{12,4},... | collective-permute-start | bytes 884744 | tf_op jit(solution)/shard_map/cond/branch_3_fun/ppermute | solution.py:444
  27.3 0.0 collective-permute-done.25
  27.3 0.0 collective-permute-done.24
  27.3 4.5 %collective-permute-done.27 = bf16[9,32,4,128]{3,2,1,0:T(4,128)(2,1)} collective-permute-done((bf16[9,32,4,128]{3,2,1,0:T(4,128)(2,1)}, bf16[9,32,4,128]{3,2,1,0:T(4,128)(2,1)}, u32[]{:S(2)}, u32[]{:S(2)}) %collective-permute-start.27) | collective-permute-done | bytes 294944 | tf_op jit(solution)/shard_map/cond/branch_3_fun/ppermute | solution.py:444
  31.8 0.0 collective-permute-done.26
  31.8 0.1 stack.23.place
  31.8 0.0 copy-done
  31.8 3.8 %shard_map.78 = (f32[24,8,128]{2,1,0:T(8,128)S(1)}, f32[32,8,128]{2,1,0:T(8,128)S(1)}, f32[6,32,8,128]{3,2,1,0:T(8,128)S(1)}, f32[2,32,8,128]{3,2,1,0:T(8,128)S(...) custom-call(s32[5]{0:T(128)S(1)} %stack.23.place, ...), custom_call_target="tpu_custom_call" | custom-call | tf_op jit(solution)/shard_map/pallas_call | solution.py:392
  35.6 1.9 %collective-permute-start.112 = (f32[24,8,128]{2,1,0:T(8,128)S(1)}, f32[24,8,128]{2,1,0:T(8,128)S(1)}, u32[]{:S(2)}, u32[]{:S(2)}) collective-permute-start(f32[24,8,128]{2,1,0:T(8,128)S(1)} %get-tuple-element.260.mine), channel_id=1, source_target_pairs={{0,4},{4,0},{1,5},{5,1},{2,6},{6,2},{3,7},{7,3},{8,12},{12,8},{9,1... | collective-permute-start | bytes 294920 | tf_op jit(solution)/shard_map/ppermute | solution.py:513
  37.6 2.2 %shard_map.79.store = f32[22,32,8,128]{3,2,1,0:T(8,128)S(1)} custom-call(s32[5]{0:T(128)S(1)} %stack.23.place, f32[2,8]{1,0:T(2,128)S(1)} %copy-done, bf16[9,32,4,128]{3,2,1,0:T(4,128)(2,1)} %get-tuple-element.257.edge_mate, bf16[9,32,4,128]{3,2,1,0:T(4,128)(2,1)} %get-tuple-element.258.edge, bf16[9,32,4,128]{3,2,1,0:T(4,128)(2,1)} %get-tuple-element.259.edge_other), custom_call_target="tpu_custom_call" | custom-call | tf_op jit(solution)/shard_map/pallas_call | solution.py:392
  39.7 1.3 %collective-permute-done.112.theirs = f32[24,8,128]{2,1,0:T(8,128)S(1)} collective-permute-done((f32[24,8,128]{2,1,0:T(8,128)S(1)}, f32[24,8,128]{2,1,0:T(8,128)S(1)}, u32[]{:S(2)}, u32[]{:S(2)}) %collective-permute-start.112) | collective-permute-done | bytes 98336 | tf_op jit(solution)/shard_map/ppermute | solution.py:513
  41.0 2.2 %shard_map.80 = (f32[6,8,128]{2,1,0:T(8,128)S(1)}, f32[6,32,8,128]{3,2,1,0:T(8,128)S(1)}, f32[2,8,128]{2,1,0:T(8,128)S(1)}, f32[2,128]{1,0:T(2,128)S(1)}) custom-call(s32[5]{0:T(128)S(1)} %stack.23.place, f32[24,8,128]{2,1,0:T(8,128)S(1)} %get-tuple-element.260.mine, f32[24,8,128]{2,1,0:T(8,128)S(1)} %collective-permute-done.112.theirs, ...), custom_call_target="tpu_custom_call" | custom-call | tf_op jit(solution)/shard_map/pallas_call | solution.py:392
  43.2 2.5 %psum.7 = f32[2,128]{1,0:T(2,128)S(1)} all-reduce(f32[2,128]{1,0:T(2,128)S(1)} %get-tuple-element.271), channel_id=1, replica_groups=mesh['row'=32,'core'=2,'vert'=2,'dir'=4] {'core'}, use_global_device_ids=true, to_apply=%region_16.17 | all-reduce | flops 256 | bytes 2048 | tf_op jit(solution)/shard_map/psum | solution.py:531
  45.7 0.6 broadcast_in_dim.2
  46.4 18.7 %all-to-all-start = ((f32[64,2,128]{2,1,0:T(2,128)}), f32[64,2,128]{2,1,0:T(2,128)S(1)}, u32[]{:S(2)}, u32[]{:S(2)}) async-start(f32[64,2,128]{2,1,0:T(2,128)} %broadcast_in_dim.2), calls=%async_computation | async-start | bytes 131072 | tf_op jit(solution)/shard_map/all_to_all | solution.py:533
  65.1 2.9 %collective-permute-start.113 = (f32[6,8,128]{2,1,0:T(8,128)S(1)}, f32[6,8,128]{2,1,0:T(8,128)S(1)}, u32[]{:S(2)}, u32[]{:S(2)}) collective-permute-start(f32[6,8,128]{2,1,0:T(8,128)S(1)} %get-tuple-element.268.mine), channel_id=1, source_target_pairs={{0,4},{4,0},{1,5},{5,1},{2,6},{6,2},{3,7},{7,3},{8,12},{12,8},{9,1... | collective-permute-start | bytes 73736 | tf_op jit(solution)/shard_map/ppermute | solution.py:529
  68.0 1.9 %collective-permute-done.113.theirs = f32[6,8,128]{2,1,0:T(8,128)S(1)} collective-permute-done((f32[6,8,128]{2,1,0:T(8,128)S(1)}, f32[6,8,128]{2,1,0:T(8,128)S(1)}, u32[]{:S(2)}, u32[]{:S(2)}) %collective-permute-start.113) | collective-permute-done | bytes 24608 | tf_op jit(solution)/shard_map/ppermute | solution.py:529
  69.9 1.4 %shard_map.81 = f32[2,3,32,4,128]{4,3,2,1,0:T(4,128)} custom-call(s32[5]{0:T(128)S(1)} %stack.23.place, f32[6,8,128]{2,1,0:T(8,128)S(1)} %get-tuple-element.268.mine, f32[6,8,128]{2,1,0:T(8,128)S(1)} %collective-permute-done.113.theirs, f32[2,8,128]{2,1,0:T(8,128)S(1)} %get-tuple-element.269.middle, f32[32,8,128]{2,1,0:T(8,128)S(1)} %get-tuple-element.264.ratio2_in.ratio_in, ...), custom_call_target="tpu_custom_call" | custom-call | tf_op jit(solution)/shard_map/pallas_call | solution.py:392
  71.4 4.6 %all-to-all-done = f32[64,2,128]{2,1,0:T(2,128)S(1)} async-done(((f32[64,2,128]{2,1,0:T(2,128)}), f32[64,2,128]{2,1,0:T(2,128)S(1)}, u32[]{:S(2)}, u32[]{:S(2)}) %all-to-all-start) | async-done | bytes 65568 | tf_op jit(solution)/shard_map/all_to_all | solution.py:533
  76.0 0.7 reduce_sum.9
Async XLA Ops:
  3.6 28.2 %copy-start = (f32[2,8]{1,0:T(2,128)S(1)}, f32[2,8]{1,0:T(2,128)}, u32[]{:S(2)}) copy-start(f32[2,8]{1,0:T(2,128)} %weights.3) | copy-start | bytes 196
  3.7 18.6 %collective-permute-start.23 = (bf16[4,32,4,128]{3,2,1,0:T(4,128)(2,1)S(1)}, bf16[4,32,4,128]{3,2,1,0:T(4,128)(2,1)S(1)}, u32[]{:S(2)}, u32[]{:S(2)}) collective-permute-start(bf16[4,32,4,128]{3,2,1,0:T(4,128)(2,1)S(1)} %get-tuple-element.167), channel_id=1, source_target_pairs={{0,1},{3,0},{4,5},{7,4},{8,9},{11,8},{12,13},{15,12},{16,17},{19,1... | collective-permute-start | bytes 393224 | tf_op jit(solution)/shard_map/cond/branch_3_fun/ppermute | solution.py:461
  7.6 14.7 %collective-permute-start.22 = (bf16[4,32,4,128]{3,2,1,0:T(4,128)(2,1)S(1)}, bf16[4,32,4,128]{3,2,1,0:T(4,128)(2,1)S(1)}, u32[]{:S(2)}, u32[]{:S(2)}) collective-permute-start(bf16[4,32,4,128]{3,2,1,0:T(4,128)(2,1)S(1)} %get-tuple-element.167), channel_id=1, source_target_pairs={{0,2},{3,1},{4,6},{7,5},{8,10},{11,9},{12,14},{15,13},{16,18},{19,... | collective-permute-start | bytes 393224 | tf_op jit(solution)/shard_map/cond/branch_3_fun/ppermute | solution.py:461
  9.8 12.5 %collective-permute-start.21 = (bf16[4,32,4,128]{3,2,1,0:T(4,128)(2,1)S(1)}, bf16[4,32,4,128]{3,2,1,0:T(4,128)(2,1)S(1)}, u32[]{:S(2)}, u32[]{:S(2)}) collective-permute-start(bf16[4,32,4,128]{3,2,1,0:T(4,128)(2,1)S(1)} %get-tuple-element.167), channel_id=1, source_target_pairs={{0,3},{3,2},{4,7},{7,6},{8,11},{11,10},{12,15},{15,14},{16,19},{19... | collective-permute-start | bytes 393224 | tf_op jit(solution)/shard_map/cond/branch_3_fun/ppermute | solution.py:461
  13.2 14.0 %collective-permute-start.25 = (f32[2,3,32,4,128]{4,3,2,1,0:T(4,128)}, f32[2,3,32,4,128]{4,3,2,1,0:T(4,128)}, u32[]{:S(2)}, u32[]{:S(2)}) collective-permute-start(f32[2,3,32,4,128]{4,3,2,1,0:T(4,128)} %get-tuple-element.170), channel_id=1, source_target_pairs={{8,16},{24,32},{40,48},{56,64},{72,80},{88,96},{104,112},{120,128}... | collective-permute-start | bytes 1179656 | tf_op jit(solution)/shard_map/cond/branch_3_fun/ppermute | solution.py:444
  17.6 9.7 %collective-permute-start.24 = (f32[2,3,32,4,128]{4,3,2,1,0:T(4,128)}, f32[2,3,32,4,128]{4,3,2,1,0:T(4,128)}, u32[]{:S(2)}, u32[]{:S(2)}) collective-permute-start(f32[2,3,32,4,128]{4,3,2,1,0:T(4,128)} %get-tuple-element.170), channel_id=1, source_target_pairs={{0,8},{8,0},{1,9},{9,1},{2,10},{10,2},{3,11},{11,3},{4,12},{12,4},... | collective-permute-start | bytes 1179656 | tf_op jit(solution)/shard_map/cond/branch_3_fun/ppermute | solution.py:444
  23.4 8.3 %collective-permute-start.27 = (bf16[9,32,4,128]{3,2,1,0:T(4,128)(2,1)}, bf16[9,32,4,128]{3,2,1,0:T(4,128)(2,1)}, u32[]{:S(2)}, u32[]{:S(2)}) collective-permute-start(bf16[9,32,4,128]{3,2,1,0:T(4,128)(2,1)} %pad_maximum_fusion.3), channel_id=1, source_target_pairs={{8,16},{24,32},{40,48},{56,64},{72,80},{88,96},{104,112},{120,128}... | collective-permute-start | bytes 884744 | tf_op jit(solution)/shard_map/cond/branch_3_fun/ppermute | solution.py:444
  25.3 6.4 %collective-permute-start.26 = (bf16[9,32,4,128]{3,2,1,0:T(4,128)(2,1)}, bf16[9,32,4,128]{3,2,1,0:T(4,128)(2,1)}, u32[]{:S(2)}, u32[]{:S(2)}) collective-permute-start(bf16[9,32,4,128]{3,2,1,0:T(4,128)(2,1)} %pad_maximum_fusion.3), channel_id=1, source_target_pairs={{0,8},{8,0},{1,9},{9,1},{2,10},{10,2},{3,11},{11,3},{4,12},{12,4},... | collective-permute-start | bytes 884744 | tf_op jit(solution)/shard_map/cond/branch_3_fun/ppermute | solution.py:444
  35.6 5.4 %collective-permute-start.112 = (f32[24,8,128]{2,1,0:T(8,128)S(1)}, f32[24,8,128]{2,1,0:T(8,128)S(1)}, u32[]{:S(2)}, u32[]{:S(2)}) collective-permute-start(f32[24,8,128]{2,1,0:T(8,128)S(1)} %get-tuple-element.260.mine), channel_id=1, source_target_pairs={{0,4},{4,0},{1,5},{5,1},{2,6},{6,2},{3,7},{7,3},{8,12},{12,8},{9,1... | collective-permute-start | bytes 294920 | tf_op jit(solution)/shard_map/ppermute | solution.py:513
  46.4 29.6 %all-to-all-start = ((f32[64,2,128]{2,1,0:T(2,128)}), f32[64,2,128]{2,1,0:T(2,128)S(1)}, u32[]{:S(2)}, u32[]{:S(2)}) async-start(f32[64,2,128]{2,1,0:T(2,128)} %broadcast_in_dim.2), calls=%async_computation | async-start | bytes 131072 | tf_op jit(solution)/shard_map/all_to_all | solution.py:533
  65.1 4.9 %collective-permute-start.113 = (f32[6,8,128]{2,1,0:T(8,128)S(1)}, f32[6,8,128]{2,1,0:T(8,128)S(1)}, u32[]{:S(2)}, u32[]{:S(2)}) collective-permute-start(f32[6,8,128]{2,1,0:T(8,128)S(1)} %get-tuple-element.268.mine), channel_id=1, source_target_pairs={{0,4},{4,0},{1,5},{5,1},{2,6},{6,2},{3,7},{7,3},{8,12},{12,8},{9,1... | collective-permute-start | bytes 73736 | tf_op jit(solution)/shard_map/ppermute | solution.py:529

commit v5 on v4

--- a/solution.py
+++ b/solution.py
@@ -23,7 +23,7 @@
 
 
 def window(ref, field, level, offset=0):
-    return ref[field, level, 2 + offset : 10 + offset, :]
+    return ref[field, level, 8 + offset : 16 + offset, :]
 
 
 def roll_y(values, offset):
@@ -33,7 +33,7 @@
 def wind_terms(winds, turbines, weights, level, above, below, sign):
     wind = [window(winds, c, level) for c in range(3)]
     visc = TIME_STEP * window(winds, 3, level)
-    mask = turbines[level, 2:10, :]
+    mask = turbines[level, 8:16, :]
     turbine = jnp.where(mask > 0.5, 1.0, 0.0)
     square = wind[0] * wind[0] + wind[1] * wind[1]
     inverse = lax.rsqrt(square)
@@ -114,7 +114,7 @@
     return rows
 
 
-def first_kernel(place, weights, mate, own, other, edge_mate, edge, edge_other,
+def first_kernel(place, weights, mate, own, other, edge_mate, edge, edge_other, visc,
                  message, ratio_out, value_out, power_out, ratio2_out, inverse2_out, face2_out,
                  wrow_out, tangents, winds, winds2, turbines):
     levels = own.shape[2]
@@ -128,25 +128,30 @@
 
     for field in range(6):
         d, i = divmod(field, 3)
-        tangents[field, :, 4:8, :] = own[d, i]
+        tangents[field, :, 10:14, :] = own[d, i]
     for c in range(4):
-        winds[c, :, 4:8, :] = edge[c].astype(jnp.float32)
-        winds2[c, :, 4:8, :] = edge[4 + c].astype(jnp.float32)
-    turbines[:, 4:8, :] = edge[8].astype(jnp.float32)
-
-    def sides(low, high, low_edge, high_edge):
+        winds[c, :, 10:14, :] = edge[c].astype(jnp.float32)
+        winds2[c, :, 10:14, :] = (edge[4 + c] if c < 3 else visc[0]).astype(jnp.float32)
+    turbines[:, 10:14, :] = edge[7].astype(jnp.float32)
+
+    def sides(near, far, inner, low_edge, high_edge):
         for field in range(6):
             d, i = divmod(field, 3)
-            tangents[field, :, 0:4, :] = low[d, i]
-            tangents[field, :, 8:12, :] = high[d, i]
+            tangents[field, :, near : near + 4, :] = mate[d, i]
+            tangents[field, :, far : far + 4, :] = other[field].astype(jnp.float32)
+            first = half * (field % 2)
+            low = other[6 + field // 2, first : first + half].astype(jnp.float32)
+            tangents[field, :half, inner : inner + 2, :] += low[:, 0:2]
+            tangents[field, half:, inner : inner + 2, :] += low[:, 2:4]
         for c in range(4):
-            winds[c, :, 0:4, :] = low_edge[c].astype(jnp.float32)
-            winds[c, :, 8:12, :] = high_edge[c].astype(jnp.float32)
-        turbines[:, 0:4, :] = low_edge[8].astype(jnp.float32)
-        turbines[:, 8:12, :] = high_edge[8].astype(jnp.float32)
-
-    pl.when(place[4] == 0)(lambda: sides(other, mate, edge_other, edge_mate))
-    pl.when(place[4] == 1)(lambda: sides(mate, other, edge_mate, edge_other))
+            winds[c, :, 6:10, :] = low_edge[c].astype(jnp.float32)
+            winds[c, :, 14:18, :] = high_edge[c].astype(jnp.float32)
+        turbines[:, 6:10, :] = low_edge[7].astype(jnp.float32)
+        turbines[:, 14:18, :] = high_edge[7].astype(jnp.float32)
+
+    half = levels // 2
+    pl.when(place[4] == 0)(lambda: sides(14, 6, 8, edge_other, edge_mate))
+    pl.when(place[4] == 1)(lambda: sides(6, 14, 14, edge_mate, edge_other))
 
     def level_rows(j, above, below):
         k = at(j)
@@ -211,7 +216,7 @@
 TERMS = len(SINGLE) + 3 + 9
 
 
-def terms_kernel(place, weights, edge_mate, edge, edge_other, out, winds, turbines):
+def terms_kernel(place, weights, edge_mate, edge, edge_other, visc, out, winds, turbines):
     levels = edge.shape[1]
     last = levels - 1
     sign = place[0].astype(jnp.float32)
@@ -223,13 +228,13 @@
         return base + step * j
 
     for c in range(4):
-        winds[c, :, 4:8, :] = edge[4 + c].astype(jnp.float32)
-    turbines[:, 4:8, :] = edge[8].astype(jnp.float32)
+        winds[c, :, 10:14, :] = (edge[4 + c] if c < 3 else visc[0]).astype(jnp.float32)
+    turbines[:, 10:14, :] = edge[7].astype(jnp.float32)
 
     def sides(low_edge, high_edge):
         for c in range(3):
-            winds[c, :, 0:4, :] = low_edge[4 + c].astype(jnp.float32)
-            winds[c, :, 8:12, :] = high_edge[4 + c].astype(jnp.float32)
+            winds[c, :, 6:10, :] = low_edge[4 + c].astype(jnp.float32)
+            winds[c, :, 14:18, :] = high_edge[4 + c].astype(jnp.float32)
 
     pl.when(place[4] == 0)(lambda: sides(edge_other, edge_mate))
     pl.when(place[4] == 1)(lambda: sides(edge_mate, edge_other))
@@ -305,7 +310,7 @@
 
     def keep(k, values, ws, sums):
         for field in range(6):
-            tangents[field, k, 2:10, :] = values[field]
+            tangents[field, k, 8:16, :] = values[field]
         for c in range(2):
             adjoint[c, k] = ws[c]
         return tuple(
@@ -400,7 +405,8 @@
     )(*scalars, *arrays)
 
 
-def prepare_kernel(slots, steps, records, groups, code, both, send, mask, groups_here, arrived):
+def prepare_kernel(slots, steps, records, groups, tangent, code, both, send, mask, packed,
+                   groups_here, own, rest, arrived):
     per_device, fields = records.shape[0], records.shape[1]
     owners = slots.shape[0] // per_device
     slot_a, slot_b = slots[steps[0]], slots[steps[1]]
@@ -412,39 +418,63 @@
         for n, (slot, target) in enumerate(zip((chosen, slot_a, slot_b), targets))
     ]
     copies.append(pltpu.make_async_copy(groups, groups_here, arrived.at[3]))
+    copies.append(pltpu.make_async_copy(tangent, own, arrived.at[4]))
     for copy in copies:
         copy.start()
     code[0] = lax.div(slot_a, per_device) * owners + owner_b
     copies[3].wait()
     mask[0] = groups_here[...].astype(jnp.float32).astype(mask.dtype)
+    copies[4].wait()
+    half = rest.shape[0]
+
+    def pack(inner):
+        for field in range(6):
+            d, i = divmod(field, 3)
+            packed[field] = own[d, i].astype(packed.dtype)
+            near = own[d, i, :, inner : inner + 2, :]
+            near = near - near.astype(packed.dtype).astype(jnp.float32)
+            rest[:, 0:2, :] = near[:half]
+            rest[:, 2:4, :] = near[half:]
+            first = half * (field % 2)
+            packed[6 + field // 2, first : first + half] = rest[...].astype(packed.dtype)
+
+    core = lax.axis_index("core")
+    pl.when(core == 0)(lambda: pack(0))
+    pl.when(core == 1)(lambda: pack(2))
     for copy in copies[:3]:
         copy.wait()
 
 
-def prepare(record_slot, step_record, records, turbine_mask):
+def prepare(record_slot, step_record, records, turbine_mask, tangent_in):
     fields, *block = records.shape[1:]
-    shapes = [(2 * fields, *block), (fields, *block), (1, *block)]
+    shapes = [(2 * fields, *block), (fields, *block), (1, *block), (9, *block)]
     return pl.pallas_call(
         prepare_kernel,
         out_shape=[jax.ShapeDtypeStruct((1,), jnp.int32)]
         + [jax.ShapeDtypeStruct(shape, records.dtype) for shape in shapes],
-        in_specs=[pl.BlockSpec(memory_space=pltpu.SMEM)] * 2 + [pl.BlockSpec(memory_space=pl.ANY)] * 2,
-        out_specs=[pl.BlockSpec(memory_space=pltpu.SMEM)] + [pl.BlockSpec(memory_space=pltpu.VMEM)] * 3,
+        in_specs=[pl.BlockSpec(memory_space=pltpu.SMEM)] * 2 + [pl.BlockSpec(memory_space=pl.ANY)] * 3,
+        out_specs=[pl.BlockSpec(memory_space=pltpu.SMEM)] + [pl.BlockSpec(memory_space=pltpu.VMEM)] * 4,
         scratch_shapes=[
             pltpu.VMEM(turbine_mask.shape, turbine_mask.dtype),
-            pltpu.SemaphoreType.DMA((4,)),
+            pltpu.VMEM(tangent_in.shape, tangent_in.dtype),
+            pltpu.VMEM((block[0] // 2, *block[1:]), jnp.float32),
+            pltpu.SemaphoreType.DMA((5,)),
         ],
-    )(record_slot, step_record, records, turbine_mask)
-
-
-def swap_tiles(block):
+    )(record_slot, step_record, records, turbine_mask, tangent_in)
+
+
+def from_mate(block):
+    return lax.ppermute(block, "core", [(0, 1), (1, 0)])
+
+
+def from_other(block):
     count = lax.axis_size("row")
     pairs = [(2 * i + 1, 2 * i + 2) for i in range(count - 1)]
     pairs += [(right, left) for left, right in pairs]
-    return lax.ppermute(block, "core", [(0, 1), (1, 0)]), lax.ppermute(block, TILE, pairs)
-
-
-def gather_inputs(code, both, send, tangent_in, mask):
+    return lax.ppermute(block, TILE, pairs)
+
+
+def gather_inputs(code, both, send, tangent_in, packed, mask):
     count = lax.axis_size("dir")
     here = lax.axis_index("dir")
     fields = send.shape[0]
@@ -455,24 +485,27 @@
         return record
 
     def branch(a, b):
-        def run(both, send, tangent, mask):
+        def run(both, send, tangent, packed, mask):
             block = both if a == b else send
             got = [
                 lax.ppermute(block, "dir", [(o, (o + k) % count) for o in sorted({a, b})])
                 for k in range(1, count)
             ]
-            tangents = swap_tiles(tangent)
+            tangents = from_mate(tangent), from_other(packed)
             if a == b:
-                recs = [take(both, a, got)]
+                recs = take(both, a, got)
+                recs, visc = recs[:-1], recs[-1:]
             else:
-                recs = [take(both[:fields], a, got), take(both[fields:], b, got)]
-            edge = jnp.concatenate([*recs, mask], axis=0)
-            return edge, *tangents, *swap_tiles(edge)
+                rec_b = take(both[fields:], b, got)
+                recs = jnp.concatenate([take(both[:fields], a, got), rec_b[:-1]], axis=0)
+                visc = rec_b[-1:]
+            edge = jnp.concatenate([recs, mask], axis=0)
+            return edge, visc, *tangents, from_mate(edge), from_other(edge)
 
         return run
 
     branches = [branch(a, b) for a in range(count) for b in range(count)]
-    return lax.switch(code, branches, both, send, tangent_in, mask)
+    return lax.switch(code, branches, both, send, tangent_in, packed, mask)
 
 
 def shards(tangent_in, records, record_slot, step_record, turbine_mask, group_weights):
@@ -491,21 +524,23 @@
         lax.axis_index("core"),
     ]).astype(jnp.int32)
 
-    code, both, send, mask = prepare(record_slot, step_record, records, turbine_mask)
-    edge, mate, other, edge_mate, edge_other = gather_inputs(
-        code[0], both, send, tangent_in, mask
+    code, both, send, mask, packed = prepare(
+        record_slot, step_record, records, turbine_mask, tangent_in
+    )
+    edge, visc, mate, other, edge_mate, edge_other = gather_inputs(
+        code[0], both, send, tangent_in, packed, mask
     )
 
     def block(*lead):
         return (*lead, 8, spans)
 
     def wide(*lead):
-        return (*lead, 16, spans)
+        return (*lead, 24, spans)
 
     message, ratio, value, power, ratio2, inverse2, face2, wrow = call(
         first_kernel,
         (place, group_weights),
-        (mate, tangent_in, other, edge_mate, edge, edge_other),
+        (mate, tangent_in, other, edge_mate, edge, edge_other, visc),
         (block(FIELDS), block(levels), block(fields, levels), block(2, levels),
          block(levels), block(levels), block(levels), block(2, levels)),
         (wide(fields, levels), wide(4, levels), wide(4, levels), wide(levels)),
@@ -514,7 +549,7 @@
     (store,) = call(
         terms_kernel,
         (place, group_weights),
-        (edge_mate, edge, edge_other),
+        (edge_mate, edge, edge_other, visc),
         (block(TERMS + directions, levels),),
         (wide(4, levels), wide(levels)),
     )

time: 77.1 us -> 75.7 us (0.982)
  the two profiles are of different devices: /device:TPU:1 before, /device:TPU:4 now
where the time goes in v5:
time: 75.7 us; the launch traced here: 75.2 us
  starting transfers between devices  39.6 us (52%)
  waiting for transfers between devices  17.1 us (23%)
  Pallas kernels  12 us (16%)
  blocking collectives  2.47 us (3%)
  other arithmetic  1.66 us (2%)
  between operations  1.37 us (2%)
  local copies, waits for them, and re-layouts  0.83 us (1%)
    all_to_all x1, starting transfers between devices, shards(): lax.all_to_all(jnp.broadcast_to(sums[None], (count, directions, spans)),...  18.2 us
    pallas_call x4, Pallas kernels, call(): pl.pallas_call(kernel, out_shape=[jax.ShapeDtypeStruct(shape, jnp.float32...  9.28 us
    ppermute x2, starting transfers between devices, from_mate(): return lax.ppermute(block, 'core', [(0, 1), (1, 0)])  8.26 us
    ppermute x3, waiting for transfers between devices, run(): lax.ppermute(block, 'dir', [(o, (o + k) % count) for o in sorted({a, b})])  7.32 us
    all_to_all x1, waiting for transfers between devices, shards(): lax.all_to_all(jnp.broadcast_to(sums[None], (count, directions, spans)),...  4.87 us
    ppermute x1, starting transfers between devices, shards(): answer = lax.ppermute(message, 'vert', swap)  4.28 us
    ppermute x1, starting transfers between devices, shards(): answer2 = lax.ppermute(row, 'vert', swap)  3.48 us
    ppermute x2, starting transfers between devices, from_other(): return lax.ppermute(block, TILE, pairs)  2.76 us
  transfers between devices with their start and end apart: 10, of which 5 were waited for; matrix products, arithmetic and copies ran while one was open for 1% of the time, Pallas kernels for 5%

profile of v5, /device:TPU:4, one launch (start us, length us, event | category | flops | bytes accessed | tf_op | source)
XLA Modules:
  0.0 75.2 jit_solution(6837741158609841914)
XLA Ops:
  0.6 2.7 %shard_map.77 = (s32[1]{0:T(128)}, bf16[8,32,4,128]{3,2,1,0:T(4,128)(2,1)S(1)}, bf16[4,32,4,128]{3,2,1,0:T(4,128)(2,1)S(1)}, bf16[1,32,4,128]{3,2,1,0:T(4,128)(2,1)S(1)}, bf16[9,32,4,128]{3,2,1,0:T(4,128)(2,1)S(1)}) custom-call(s32[16]{0:T(128)} %slots.1, s32[2]{0:T(128)} %steps.1, bf16[4,4,32,4,128]{4,3,2,1,0:T(4,128)(2,1)} %records.1, ...), custom_call_target="tpu_custom_call" | custom-call | tf_op jit(solution)/shard_map/pallas_call | solution.py:451
  4.0 0.0 copy-start
  4.0 23.6 %conditional.1 = (bf16[8,32,4,128]{3,2,1,0:T(4,128)(2,1)}, bf16[1,32,4,128]{3,2,1,0:T(4,128)(2,1)S(1)}, f32[2,3,32,4,128]{4,3,2,1,0:T(4,128)}, bf16[9,32,4,128]{...) conditional(s32[]{:T(128)} %bitcast.5, (s32[]{:T(128)}, ...), branch_computations={%region_0.1_spmd, %region_1.2_spmd, %region_2.3_spmd, %region_3.4_... | conditional | flops 655364 | bytes 10355046 | solution.py:508
  4.0 0.7 collective-permute-start.2
  4.7 1.3 %collective-permute-start.1 = (bf16[8,32,4,128]{3,2,1,0:T(4,128)(2,1)S(1)}, bf16[8,32,4,128]{3,2,1,0:T(4,128)(2,1)S(1)}, u32[]{:S(2)}, u32[]{:S(2)}) collective-permute-start(bf16[8,32,4,128]{3,2,1,0:T(4,128)(2,1)S(1)} %get-tuple-element.185), channel_id=1, source_target_pairs={{0,2},{4,6},{8,10},{12,14},{16,18},{20,22},{24,26},{28,30},{32,34}... | collective-permute-start | bytes 786440 | tf_op jit(solution)/shard_map/cond/branch_0_fun/ppermute | solution.py:491
  6.0 0.7 collective-permute-start
  6.7 1.4 %collective-permute-start.4 = (bf16[9,32,4,128]{3,2,1,0:T(4,128)(2,1)S(1)}, bf16[9,32,4,128]{3,2,1,0:T(4,128)(2,1)}, u32[]{:S(2)}, u32[]{:S(2)}) collective-permute-start(bf16[9,32,4,128]{3,2,1,0:T(4,128)(2,1)S(1)} %get-tuple-element.188), channel_id=1, source_target_pairs={{8,16},{24,32},{40,48},{56,64},{72,80},{88,96},{104,112},{120,128}... | collective-permute-start | bytes 884744 | tf_op jit(solution)/shard_map/cond/branch_0_fun/ppermute | solution.py:474
  8.1 4.1 %collective-permute-start.3 = (f32[2,3,32,4,128]{4,3,2,1,0:T(4,128)}, f32[2,3,32,4,128]{4,3,2,1,0:T(4,128)}, u32[]{:S(2)}, u32[]{:S(2)}) collective-permute-start(f32[2,3,32,4,128]{4,3,2,1,0:T(4,128)} %get-tuple-element.187), channel_id=1, source_target_pairs={{0,8},{8,0},{1,9},{9,1},{2,10},{10,2},{3,11},{11,3},{4,12},{12,4},... | collective-permute-start | bytes 1179656 | tf_op jit(solution)/shard_map/cond/branch_0_fun/ppermute | solution.py:467
  12.2 0.0 collective-permute-done.2
  12.3 7.3 %collective-permute-done.1 = bf16[8,32,4,128]{3,2,1,0:T(4,128)(2,1)S(1)} collective-permute-done((bf16[8,32,4,128]{3,2,1,0:T(4,128)(2,1)S(1)}, bf16[8,32,4,128]{3,2,1,0:T(4,128)(2,1)S(1)}, u32[]{:S(2)}, u32[]{:S(2)}) %collective-permute-start.1) | collective-permute-done | bytes 262176 | tf_op jit(solution)/shard_map/cond/branch_0_fun/ppermute | solution.py:491
  19.6 0.0 collective-permute-done
  19.6 0.1 select_select_fusion
  19.7 0.1 slice.168
  19.7 0.9 %pad_maximum_fusion = bf16[8,32,4,128]{3,2,1,0:T(4,128)(2,1)} fusion(bf16[1,32,4,128]{3,2,1,0:T(4,128)(2,1)S(1)} %get-tuple-element.186, bf16[7,32,4,128]{3,2,1,0:T(4,128)(2,1)S(1)} %slice.168), kind=kLoop, calls=%fused_computation | loop fusion | flops 131072 | bytes 524288 | tf_op jit(solution)/shard_map/cond/branch_0_fun/concatenate | solution.py:502
  20.6 1.4 %collective-permute-start.6 = (bf16[8,32,4,128]{3,2,1,0:T(4,128)(2,1)}, bf16[8,32,4,128]{3,2,1,0:T(4,128)(2,1)}, u32[]{:S(2)}, u32[]{:S(2)}) collective-permute-start(bf16[8,32,4,128]{3,2,1,0:T(4,128)(2,1)} %pad_maximum_fusion), channel_id=1, source_target_pairs={{8,16},{24,32},{40,48},{56,64},{72,80},{88,96},{104,112},{120,128}... | collective-permute-start | bytes 786440 | tf_op jit(solution)/shard_map/cond/branch_0_fun/ppermute | solution.py:474
  22.0 4.1 %collective-permute-start.5 = (bf16[8,32,4,128]{3,2,1,0:T(4,128)(2,1)}, bf16[8,32,4,128]{3,2,1,0:T(4,128)(2,1)}, u32[]{:S(2)}, u32[]{:S(2)}) collective-permute-start(bf16[8,32,4,128]{3,2,1,0:T(4,128)(2,1)} %pad_maximum_fusion), channel_id=1, source_target_pairs={{0,8},{8,0},{1,9},{9,1},{2,10},{10,2},{3,11},{11,3},{4,12},{12,4},... | collective-permute-start | bytes 786440 | tf_op jit(solution)/shard_map/cond/branch_0_fun/ppermute | solution.py:467
  26.2 0.0 collective-permute-done.4
  26.2 0.0 collective-permute-done.3
  26.2 0.0 collective-permute-done.6
  26.2 1.4 %collective-permute-done.5 = bf16[8,32,4,128]{3,2,1,0:T(4,128)(2,1)} collective-permute-done((bf16[8,32,4,128]{3,2,1,0:T(4,128)(2,1)}, bf16[8,32,4,128]{3,2,1,0:T(4,128)(2,1)}, u32[]{:S(2)}, u32[]{:S(2)}) %collective-permute-start.5) | collective-permute-done | bytes 262176 | tf_op jit(solution)/shard_map/cond/branch_0_fun/ppermute | solution.py:467
  27.6 0.1 stack.23.place
  27.7 0.0 copy-done
  27.7 3.7 %shard_map.78 = (f32[24,8,128]{2,1,0:T(8,128)S(1)}, f32[32,8,128]{2,1,0:T(8,128)S(1)}, f32[6,32,8,128]{3,2,1,0:T(8,128)S(1)}, f32[2,32,8,128]{3,2,1,0:T(8,128)S(...) custom-call(s32[5]{0:T(128)S(1)} %stack.23.place, ...), custom_call_target="tpu_custom_call" | custom-call | tf_op jit(solution)/shard_map/pallas_call | solution.py:397
  31.4 4.3 %collective-permute-start.112 = (f32[24,8,128]{2,1,0:T(8,128)S(1)}, f32[24,8,128]{2,1,0:T(8,128)S(1)}, u32[]{:S(2)}, u32[]{:S(2)}) collective-permute-start(f32[24,8,128]{2,1,0:T(8,128)S(1)} %get-tuple-element.312.mine), channel_id=1, source_target_pairs={{0,4},{4,0},{1,5},{5,1},{2,6},{6,2},{3,7},{7,3},{8,12},{12,8},{9,1... | collective-permute-start | bytes 294920 | tf_op jit(solution)/shard_map/ppermute | solution.py:548
  35.7 2.1 %shard_map.79.store = f32[22,32,8,128]{3,2,1,0:T(8,128)S(1)} custom-call(s32[5]{0:T(128)S(1)} %stack.23.place, f32[2,8]{1,0:T(2,128)S(1)} %copy-done, bf16[8,32,4,128]{3,2,1,0:T(4,128)(2,1)} %get-tuple-element.308.edge_mate, bf16[8,32,4,128]{3,2,1,0:T(4,128)(2,1)} %get-tuple-element.309.edge, bf16[8,32,4,128]{3,2,1,0:T(4,128)(2,1)} %get-tuple-element.310.edge_other, ...), custom_call_target="tpu_custom_call" | custom-call | tf_op jit(solution)/shard_map/pallas_call | solution.py:397
  37.8 1.3 %collective-permute-done.112.theirs = f32[24,8,128]{2,1,0:T(8,128)S(1)} collective-permute-done((f32[24,8,128]{2,1,0:T(8,128)S(1)}, f32[24,8,128]{2,1,0:T(8,128)S(1)}, u32[]{:S(2)}, u32[]{:S(2)}) %collective-permute-start.112) | collective-permute-done | bytes 98336 | tf_op jit(solution)/shard_map/ppermute | solution.py:548
  39.1 2.0 %shard_map.80 = (f32[6,8,128]{2,1,0:T(8,128)S(1)}, f32[6,32,8,128]{3,2,1,0:T(8,128)S(1)}, f32[2,8,128]{2,1,0:T(8,128)S(1)}, f32[2,128]{1,0:T(2,128)S(1)}) custom-call(s32[5]{0:T(128)S(1)} %stack.23.place, f32[24,8,128]{2,1,0:T(8,128)S(1)} %get-tuple-element.312.mine, f32[24,8,128]{2,1,0:T(8,128)S(1)} %collective-permute-done.112.theirs, ...), custom_call_target="tpu_custom_call" | custom-call | tf_op jit(solution)/shard_map/pallas_call | solution.py:397
  41.1 2.5 %psum.7 = f32[2,128]{1,0:T(2,128)S(1)} all-reduce(f32[2,128]{1,0:T(2,128)S(1)} %get-tuple-element.323), channel_id=1, replica_groups=mesh['row'=32,'core'=2,'vert'=2,'dir'=4] {'core'}, use_global_device_ids=true, to_apply=%region_16.17 | all-reduce | flops 256 | bytes 2048 | tf_op jit(solution)/shard_map/psum | solution.py:566
  43.6 0.6 broadcast_in_dim.2
  44.2 18.2 %all-to-all-start = ((f32[64,2,128]{2,1,0:T(2,128)}), f32[64,2,128]{2,1,0:T(2,128)S(1)}, u32[]{:S(2)}, u32[]{:S(2)}) async-start(f32[64,2,128]{2,1,0:T(2,128)} %broadcast_in_dim.2), calls=%async_computation | async-start | bytes 131072 | tf_op jit(solution)/shard_map/all_to_all | solution.py:568
  62.4 3.5 %collective-permute-start.113 = (f32[6,8,128]{2,1,0:T(8,128)S(1)}, f32[6,8,128]{2,1,0:T(8,128)S(1)}, u32[]{:S(2)}, u32[]{:S(2)}) collective-permute-start(f32[6,8,128]{2,1,0:T(8,128)S(1)} %get-tuple-element.320.mine), channel_id=1, source_target_pairs={{0,4},{4,0},{1,5},{5,1},{2,6},{6,2},{3,7},{7,3},{8,12},{12,8},{9,1... | collective-permute-start | bytes 73736 | tf_op jit(solution)/shard_map/ppermute | solution.py:564
  65.9 2.2 %collective-permute-done.113.theirs = f32[6,8,128]{2,1,0:T(8,128)S(1)} collective-permute-done((f32[6,8,128]{2,1,0:T(8,128)S(1)}, f32[6,8,128]{2,1,0:T(8,128)S(1)}, u32[]{:S(2)}, u32[]{:S(2)}) %collective-permute-start.113) | collective-permute-done | bytes 24608 | tf_op jit(solution)/shard_map/ppermute | solution.py:564
  68.2 1.4 %shard_map.81 = f32[2,3,32,4,128]{4,3,2,1,0:T(4,128)} custom-call(s32[5]{0:T(128)S(1)} %stack.23.place, f32[6,8,128]{2,1,0:T(8,128)S(1)} %get-tuple-element.320.mine, f32[6,8,128]{2,1,0:T(8,128)S(1)} %collective-permute-done.113.theirs, f32[2,8,128]{2,1,0:T(8,128)S(1)} %get-tuple-element.321.middle, f32[32,8,128]{2,1,0:T(8,128)S(1)} %get-tuple-element.316.ratio2_in.ratio_in, ...), custom_call_target="tpu_custom_call" | custom-call | tf_op jit(solution)/shard_map/pallas_call | solution.py:397
  69.6 4.9 %all-to-all-done = f32[64,2,128]{2,1,0:T(2,128)S(1)} async-done(((f32[64,2,128]{2,1,0:T(2,128)}), f32[64,2,128]{2,1,0:T(2,128)S(1)}, u32[]{:S(2)}, u32[]{:S(2)}) %all-to-all-start) | async-done | bytes 65568 | tf_op jit(solution)/shard_map/all_to_all | solution.py:568
  74.5 0.7 reduce_sum.9
  (1 shorter events, 0.0 us)
Async XLA Ops:
  4.0 23.7 %copy-start = (f32[2,8]{1,0:T(2,128)S(1)}, f32[2,8]{1,0:T(2,128)}, u32[]{:S(2)}) copy-start(f32[2,8]{1,0:T(2,128)} %weights.3) | copy-start | bytes 196
  4.0 8.2 %collective-permute-start.2 = (bf16[8,32,4,128]{3,2,1,0:T(4,128)(2,1)S(1)}, bf16[8,32,4,128]{3,2,1,0:T(4,128)(2,1)S(1)}, u32[]{:S(2)}, u32[]{:S(2)}) collective-permute-start(bf16[8,32,4,128]{3,2,1,0:T(4,128)(2,1)S(1)} %get-tuple-element.185), channel_id=1, source_target_pairs={{0,1},{4,5},{8,9},{12,13},{16,17},{20,21},{24,25},{28,29},{32,33},... | collective-permute-start | bytes 786440 | tf_op jit(solution)/shard_map/cond/branch_0_fun/ppermute | solution.py:491
  4.7 14.8 %collective-permute-start.1 = (bf16[8,32,4,128]{3,2,1,0:T(4,128)(2,1)S(1)}, bf16[8,32,4,128]{3,2,1,0:T(4,128)(2,1)S(1)}, u32[]{:S(2)}, u32[]{:S(2)}) collective-permute-start(bf16[8,32,4,128]{3,2,1,0:T(4,128)(2,1)S(1)} %get-tuple-element.185), channel_id=1, source_target_pairs={{0,2},{4,6},{8,10},{12,14},{16,18},{20,22},{24,26},{28,30},{32,34}... | collective-permute-start | bytes 786440 | tf_op jit(solution)/shard_map/cond/branch_0_fun/ppermute | solution.py:491
  6.0 13.5 %collective-permute-start = (bf16[8,32,4,128]{3,2,1,0:T(4,128)(2,1)S(1)}, bf16[8,32,4,128]{3,2,1,0:T(4,128)(2,1)S(1)}, u32[]{:S(2)}, u32[]{:S(2)}) collective-permute-start(bf16[8,32,4,128]{3,2,1,0:T(4,128)(2,1)S(1)} %get-tuple-element.185), channel_id=1, source_target_pairs={{0,3},{4,7},{8,11},{12,15},{16,19},{20,23},{24,27},{28,31},{32,35}... | collective-permute-start | bytes 786440 | tf_op jit(solution)/shard_map/cond/branch_0_fun/ppermute | solution.py:491
  6.7 19.5 %collective-permute-start.4 = (bf16[9,32,4,128]{3,2,1,0:T(4,128)(2,1)S(1)}, bf16[9,32,4,128]{3,2,1,0:T(4,128)(2,1)}, u32[]{:S(2)}, u32[]{:S(2)}) collective-permute-start(bf16[9,32,4,128]{3,2,1,0:T(4,128)(2,1)S(1)} %get-tuple-element.188), channel_id=1, source_target_pairs={{8,16},{24,32},{40,48},{56,64},{72,80},{88,96},{104,112},{120,128}... | collective-permute-start | bytes 884744 | tf_op jit(solution)/shard_map/cond/branch_0_fun/ppermute | solution.py:474
  8.1 18.1 %collective-permute-start.3 = (f32[2,3,32,4,128]{4,3,2,1,0:T(4,128)}, f32[2,3,32,4,128]{4,3,2,1,0:T(4,128)}, u32[]{:S(2)}, u32[]{:S(2)}) collective-permute-start(f32[2,3,32,4,128]{4,3,2,1,0:T(4,128)} %get-tuple-element.187), channel_id=1, source_target_pairs={{0,8},{8,0},{1,9},{9,1},{2,10},{10,2},{3,11},{11,3},{4,12},{12,4},... | collective-permute-start | bytes 1179656 | tf_op jit(solution)/shard_map/cond/branch_0_fun/ppermute | solution.py:467
  20.6 5.6 %collective-permute-start.6 = (bf16[8,32,4,128]{3,2,1,0:T(4,128)(2,1)}, bf16[8,32,4,128]{3,2,1,0:T(4,128)(2,1)}, u32[]{:S(2)}, u32[]{:S(2)}) collective-permute-start(bf16[8,32,4,128]{3,2,1,0:T(4,128)(2,1)} %pad_maximum_fusion), channel_id=1, source_target_pairs={{8,16},{24,32},{40,48},{56,64},{72,80},{88,96},{104,112},{120,128}... | collective-permute-start | bytes 786440 | tf_op jit(solution)/shard_map/cond/branch_0_fun/ppermute | solution.py:474
  22.0 5.6 %collective-permute-start.5 = (bf16[8,32,4,128]{3,2,1,0:T(4,128)(2,1)}, bf16[8,32,4,128]{3,2,1,0:T(4,128)(2,1)}, u32[]{:S(2)}, u32[]{:S(2)}) collective-permute-start(bf16[8,32,4,128]{3,2,1,0:T(4,128)(2,1)} %pad_maximum_fusion), channel_id=1, source_target_pairs={{0,8},{8,0},{1,9},{9,1},{2,10},{10,2},{3,11},{11,3},{4,12},{12,4},... | collective-permute-start | bytes 786440 | tf_op jit(solution)/shard_map/cond/branch_0_fun/ppermute | solution.py:467
  31.4 7.6 %collective-permute-start.112 = (f32[24,8,128]{2,1,0:T(8,128)S(1)}, f32[24,8,128]{2,1,0:T(8,128)S(1)}, u32[]{:S(2)}, u32[]{:S(2)}) collective-permute-start(f32[24,8,128]{2,1,0:T(8,128)S(1)} %get-tuple-element.312.mine), channel_id=1, source_target_pairs={{0,4},{4,0},{1,5},{5,1},{2,6},{6,2},{3,7},{7,3},{8,12},{12,8},{9,1... | collective-permute-start | bytes 294920 | tf_op jit(solution)/shard_map/ppermute | solution.py:548
  44.2 30.3 %all-to-all-start = ((f32[64,2,128]{2,1,0:T(2,128)}), f32[64,2,128]{2,1,0:T(2,128)S(1)}, u32[]{:S(2)}, u32[]{:S(2)}) async-start(f32[64,2,128]{2,1,0:T(2,128)} %broadcast_in_dim.2), calls=%async_computation | async-start | bytes 131072 | tf_op jit(solution)/shard_map/all_to_all | solution.py:568
  62.4 5.7 %collective-permute-start.113 = (f32[6,8,128]{2,1,0:T(8,128)S(1)}, f32[6,8,128]{2,1,0:T(8,128)S(1)}, u32[]{:S(2)}, u32[]{:S(2)}) collective-permute-start(f32[6,8,128]{2,1,0:T(8,128)S(1)} %get-tuple-element.320.mine), channel_id=1, source_target_pairs={{0,4},{4,0},{1,5},{5,1},{2,6},{6,2},{3,7},{7,3},{8,12},{12,8},{9,1... | collective-permute-start | bytes 73736 | tf_op jit(solution)/shard_map/ppermute | solution.py:564

commit v6 on v5

--- a/solution.py
+++ b/solution.py
@@ -15,7 +15,7 @@
 POWER_SCALE = 0.01
 VERTICAL_ASPECT = 400.0
 TILE = ("row", "core")
-UNROLL = 10
+UNROLL = 15
 HALF = 0.5 * TIME_STEP
 FACE = 0.5 * TIME_STEP * VERTICAL_ASPECT
 

time: 75.7 us -> 74.6 us (0.985)
  the two profiles are of different devices: /device:TPU:4 before, /device:TPU:1 now
where the time goes in v6:
time: 74.6 us
  starting transfers between devices  46.7 us (63%)
  Pallas kernels  11.8 us (16%)
  waiting for transfers between devices  9.65 us (13%)
  blocking collectives  2.48 us (3%)
  other arithmetic  1.77 us (2%)
  between operations  1.37 us (2%)
  local copies, waits for them, and re-layouts  0.79 us (1%)
    all_to_all x1, starting transfers between devices, shards(): lax.all_to_all(jnp.broadcast_to(sums[None], (count, directions, spans)),...  18.4 us
    ppermute x3, starting transfers between devices, run(): lax.ppermute(block, 'dir', [(o, (o + k) % count) for o in sorted({a, b})])  9.61 us
    pallas_call x4, Pallas kernels, call(): pl.pallas_call(kernel, out_shape=[jax.ShapeDtypeStruct(shape, jnp.float32...  9.07 us
    ppermute x2, starting transfers between devices, from_other(): return lax.ppermute(block, TILE, pairs)  7.9 us
    all_to_all x1, waiting for transfers between devices, shards(): lax.all_to_all(jnp.broadcast_to(sums[None], (count, directions, spans)),...  4.57 us
    ppermute x1, starting transfers between devices, shards(): answer = lax.ppermute(message, 'vert', swap)  3.99 us
    ppermute x2, starting transfers between devices, from_mate(): return lax.ppermute(block, 'core', [(0, 1), (1, 0)])  3.85 us
    ppermute x1, starting transfers between devices, shards(): answer2 = lax.ppermute(row, 'vert', swap)  2.92 us
  transfers between devices with their start and end apart: 10, of which 4 were waited for; matrix products, arithmetic and copies ran while one was open for 2% of the time, Pallas kernels for 5%

profile of v6, /device:TPU:1, one launch (start us, length us, event | category | flops | bytes accessed | tf_op | source)
XLA Modules:
  0.0 74.6 jit_solution(13491660742136808251)
XLA Ops:
  0.6 2.7 %shard_map.77 = (s32[1]{0:T(128)}, bf16[8,32,4,128]{3,2,1,0:T(4,128)(2,1)S(1)}, bf16[4,32,4,128]{3,2,1,0:T(4,128)(2,1)S(1)}, bf16[1,32,4,128]{3,2,1,0:T(4,128)(2,1)S(1)}, bf16[9,32,4,128]{3,2,1,0:T(4,128)(2,1)S(1)}) custom-call(s32[16]{0:T(128)} %slots.1, s32[2]{0:T(128)} %steps.1, bf16[4,4,32,4,128]{4,3,2,1,0:T(4,128)(2,1)} %records.1, ...), custom_call_target="tpu_custom_call" | custom-call | tf_op jit(solution)/shard_map/pallas_call | solution.py:451
  4.0 0.0 copy-start
  4.0 25.1 %conditional.1 = (bf16[8,32,4,128]{3,2,1,0:T(4,128)(2,1)}, bf16[1,32,4,128]{3,2,1,0:T(4,128)(2,1)S(1)}, f32[2,3,32,4,128]{4,3,2,1,0:T(4,128)}, bf16[9,32,4,128]{...) conditional(s32[]{:T(128)} %bitcast.5, (s32[]{:T(128)}, ...), branch_computations={%region_0.1_spmd, %region_1.2_spmd, %region_2.3_spmd, %region_3.4_... | conditional | flops 655364 | bytes 10355046 | solution.py:508
  4.0 4.0 %collective-permute-start.58 = (bf16[4,32,4,128]{3,2,1,0:T(4,128)(2,1)S(1)}, bf16[4,32,4,128]{3,2,1,0:T(4,128)(2,1)S(1)}, u32[]{:S(2)}, u32[]{:S(2)}) collective-permute-start(bf16[4,32,4,128]{3,2,1,0:T(4,128)(2,1)S(1)} %get-tuple-element.231), channel_id=1, source_target_pairs={{0,1},{2,3},{4,5},{6,7},{8,9},{10,11},{12,13},{14,15},{16,17},{18,... | collective-permute-start | bytes 393224 | tf_op jit(solution)/shard_map/cond/branch_8_fun/ppermute | solution.py:491
  8.0 4.4 %collective-permute-start.57 = (bf16[4,32,4,128]{3,2,1,0:T(4,128)(2,1)S(1)}, bf16[4,32,4,128]{3,2,1,0:T(4,128)(2,1)S(1)}, u32[]{:S(2)}, u32[]{:S(2)}) collective-permute-start(bf16[4,32,4,128]{3,2,1,0:T(4,128)(2,1)S(1)} %get-tuple-element.231), channel_id=1, source_target_pairs={{0,2},{2,0},{4,6},{6,4},{8,10},{10,8},{12,14},{14,12},{16,18},{18,... | collective-permute-start | bytes 393224 | tf_op jit(solution)/shard_map/cond/branch_8_fun/ppermute | solution.py:491
  12.4 1.3 %collective-permute-start.56 = (bf16[4,32,4,128]{3,2,1,0:T(4,128)(2,1)S(1)}, bf16[4,32,4,128]{3,2,1,0:T(4,128)(2,1)S(1)}, u32[]{:S(2)}, u32[]{:S(2)}) collective-permute-start(bf16[4,32,4,128]{3,2,1,0:T(4,128)(2,1)S(1)} %get-tuple-element.231), channel_id=1, source_target_pairs={{0,3},{2,1},{4,7},{6,5},{8,11},{10,9},{12,15},{14,13},{16,19},{18,... | collective-permute-start | bytes 393224 | tf_op jit(solution)/shard_map/cond/branch_8_fun/ppermute | solution.py:491
  13.7 4.3 %collective-permute-start.60 = (bf16[9,32,4,128]{3,2,1,0:T(4,128)(2,1)S(1)}, bf16[9,32,4,128]{3,2,1,0:T(4,128)(2,1)}, u32[]{:S(2)}, u32[]{:S(2)}) collective-permute-start(bf16[9,32,4,128]{3,2,1,0:T(4,128)(2,1)S(1)} %get-tuple-element.235), channel_id=1, source_target_pairs={{8,16},{24,32},{40,48},{56,64},{72,80},{88,96},{104,112},{120,128}... | collective-permute-start | bytes 884744 | tf_op jit(solution)/shard_map/cond/branch_8_fun/ppermute | solution.py:474
  18.0 1.9 %collective-permute-start.59 = (f32[2,3,32,4,128]{4,3,2,1,0:T(4,128)}, f32[2,3,32,4,128]{4,3,2,1,0:T(4,128)}, u32[]{:S(2)}, u32[]{:S(2)}) collective-permute-start(f32[2,3,32,4,128]{4,3,2,1,0:T(4,128)} %get-tuple-element.234), channel_id=1, source_target_pairs={{0,8},{8,0},{1,9},{9,1},{2,10},{10,2},{3,11},{11,3},{4,12},{12,4},... | collective-permute-start | bytes 1179656 | tf_op jit(solution)/shard_map/cond/branch_8_fun/ppermute | solution.py:467
  20.0 0.0 collective-permute-done.58
  20.0 0.0 collective-permute-done.57
  20.0 0.0 collective-permute-done.56
  20.0 0.2 select_select_fusion.15
  20.2 0.9 %pad_maximum_fusion.8 = bf16[8,32,4,128]{3,2,1,0:T(4,128)(2,1)} fusion(bf16[1,32,4,128]{3,2,1,0:T(4,128)(2,1)S(1)} %get-tuple-element.233, bf16[3,32,4,128]{3,2,1,0:T(4,128)(2,1)S(1)} %slice.184, bf16[4,32,4,128]{3,2,1,0:T(4,128)(2,1)S(1)} %get-tuple-element.336), kind=kLoop, calls=%fused_computation.22 | loop fusion | flops 262144 | bytes 524288 | tf_op jit(solution)/shard_map/cond/branch_8_fun/concatenate | solution.py:502
  21.1 3.6 %collective-permute-start.62 = (bf16[8,32,4,128]{3,2,1,0:T(4,128)(2,1)}, bf16[8,32,4,128]{3,2,1,0:T(4,128)(2,1)}, u32[]{:S(2)}, u32[]{:S(2)}) collective-permute-start(bf16[8,32,4,128]{3,2,1,0:T(4,128)(2,1)} %pad_maximum_fusion.8), channel_id=1, source_target_pairs={{8,16},{24,32},{40,48},{56,64},{72,80},{88,96},{104,112},{120,128}... | collective-permute-start | bytes 786440 | tf_op jit(solution)/shard_map/cond/branch_8_fun/ppermute | solution.py:474
  24.7 1.9 %collective-permute-start.61 = (bf16[8,32,4,128]{3,2,1,0:T(4,128)(2,1)}, bf16[8,32,4,128]{3,2,1,0:T(4,128)(2,1)}, u32[]{:S(2)}, u32[]{:S(2)}) collective-permute-start(bf16[8,32,4,128]{3,2,1,0:T(4,128)(2,1)} %pad_maximum_fusion.8), channel_id=1, source_target_pairs={{0,8},{8,0},{1,9},{9,1},{2,10},{10,2},{3,11},{11,3},{4,12},{12,4},... | collective-permute-start | bytes 786440 | tf_op jit(solution)/shard_map/cond/branch_8_fun/ppermute | solution.py:467
  26.6 0.0 collective-permute-done.60
  26.7 2.4 %collective-permute-done.62 = bf16[8,32,4,128]{3,2,1,0:T(4,128)(2,1)} collective-permute-done((bf16[8,32,4,128]{3,2,1,0:T(4,128)(2,1)}, bf16[8,32,4,128]{3,2,1,0:T(4,128)(2,1)}, u32[]{:S(2)}, u32[]{:S(2)}) %collective-permute-start.62) | collective-permute-done | bytes 262176 | tf_op jit(solution)/shard_map/cond/branch_8_fun/ppermute | solution.py:474
  29.1 0.0 collective-permute-done.61
  29.1 0.0 collective-permute-done.59
  29.1 0.1 stack.23.place
  29.2 0.0 copy-done
  29.2 3.6 %shard_map.78 = (f32[24,8,128]{2,1,0:T(8,128)S(1)}, f32[32,8,128]{2,1,0:T(8,128)S(1)}, f32[6,32,8,128]{3,2,1,0:T(8,128)S(1)}, f32[2,32,8,128]{3,2,1,0:T(8,128)S(...) custom-call(s32[5]{0:T(128)S(1)} %stack.23.place, ...), custom_call_target="tpu_custom_call" | custom-call | tf_op jit(solution)/shard_map/pallas_call | solution.py:397
  32.8 4.0 %collective-permute-start.112 = (f32[24,8,128]{2,1,0:T(8,128)S(1)}, f32[24,8,128]{2,1,0:T(8,128)S(1)}, u32[]{:S(2)}, u32[]{:S(2)}) collective-permute-start(f32[24,8,128]{2,1,0:T(8,128)S(1)} %get-tuple-element.312.mine), channel_id=1, source_target_pairs={{0,4},{4,0},{1,5},{5,1},{2,6},{6,2},{3,7},{7,3},{8,12},{12,8},{9,1... | collective-permute-start | bytes 294920 | tf_op jit(solution)/shard_map/ppermute | solution.py:548
  36.8 2.0 %shard_map.79.store = f32[22,32,8,128]{3,2,1,0:T(8,128)S(1)} custom-call(s32[5]{0:T(128)S(1)} %stack.23.place, f32[2,8]{1,0:T(2,128)S(1)} %copy-done, bf16[8,32,4,128]{3,2,1,0:T(4,128)(2,1)} %get-tuple-element.308.edge_mate, bf16[8,32,4,128]{3,2,1,0:T(4,128)(2,1)} %get-tuple-element.309.edge, bf16[8,32,4,128]{3,2,1,0:T(4,128)(2,1)} %get-tuple-element.310.edge_other, ...), custom_call_target="tpu_custom_call" | custom-call | tf_op jit(solution)/shard_map/pallas_call | solution.py:397
  38.9 0.7 collective-permute-done.112.theirs
  39.5 2.0 %shard_map.80 = (f32[6,8,128]{2,1,0:T(8,128)S(1)}, f32[6,32,8,128]{3,2,1,0:T(8,128)S(1)}, f32[2,8,128]{2,1,0:T(8,128)S(1)}, f32[2,128]{1,0:T(2,128)S(1)}) custom-call(s32[5]{0:T(128)S(1)} %stack.23.place, f32[24,8,128]{2,1,0:T(8,128)S(1)} %get-tuple-element.312.mine, f32[24,8,128]{2,1,0:T(8,128)S(1)} %collective-permute-done.112.theirs, ...), custom_call_target="tpu_custom_call" | custom-call | tf_op jit(solution)/shard_map/pallas_call | solution.py:397
  41.5 2.5 %psum.7 = f32[2,128]{1,0:T(2,128)S(1)} all-reduce(f32[2,128]{1,0:T(2,128)S(1)} %get-tuple-element.323), channel_id=1, replica_groups=mesh['row'=32,'core'=2,'vert'=2,'dir'=4] {'core'}, use_global_device_ids=true, to_apply=%region_16.17 | all-reduce | flops 256 | bytes 2048 | tf_op jit(solution)/shard_map/psum | solution.py:566
  44.0 0.6 broadcast_in_dim.2
  44.6 18.4 %all-to-all-start = ((f32[64,2,128]{2,1,0:T(2,128)}), f32[64,2,128]{2,1,0:T(2,128)S(1)}, u32[]{:S(2)}, u32[]{:S(2)}) async-start(f32[64,2,128]{2,1,0:T(2,128)} %broadcast_in_dim.2), calls=%async_computation | async-start | bytes 131072 | tf_op jit(solution)/shard_map/all_to_all | solution.py:568
  63.0 2.9 %collective-permute-start.113 = (f32[6,8,128]{2,1,0:T(8,128)S(1)}, f32[6,8,128]{2,1,0:T(8,128)S(1)}, u32[]{:S(2)}, u32[]{:S(2)}) collective-permute-start(f32[6,8,128]{2,1,0:T(8,128)S(1)} %get-tuple-element.320.mine), channel_id=1, source_target_pairs={{0,4},{4,0},{1,5},{5,1},{2,6},{6,2},{3,7},{7,3},{8,12},{12,8},{9,1... | collective-permute-start | bytes 73736 | tf_op jit(solution)/shard_map/ppermute | solution.py:564
  66.0 2.0 %collective-permute-done.113.theirs = f32[6,8,128]{2,1,0:T(8,128)S(1)} collective-permute-done((f32[6,8,128]{2,1,0:T(8,128)S(1)}, f32[6,8,128]{2,1,0:T(8,128)S(1)}, u32[]{:S(2)}, u32[]{:S(2)}) %collective-permute-start.113) | collective-permute-done | bytes 24608 | tf_op jit(solution)/shard_map/ppermute | solution.py:564
  67.9 1.4 %shard_map.81 = f32[2,3,32,4,128]{4,3,2,1,0:T(4,128)} custom-call(s32[5]{0:T(128)S(1)} %stack.23.place, f32[6,8,128]{2,1,0:T(8,128)S(1)} %get-tuple-element.320.mine, f32[6,8,128]{2,1,0:T(8,128)S(1)} %collective-permute-done.113.theirs, f32[2,8,128]{2,1,0:T(8,128)S(1)} %get-tuple-element.321.middle, f32[32,8,128]{2,1,0:T(8,128)S(1)} %get-tuple-element.316.ratio2_in.ratio_in, ...), custom_call_target="tpu_custom_call" | custom-call | tf_op jit(solution)/shard_map/pallas_call | solution.py:397
  69.4 4.6 %all-to-all-done = f32[64,2,128]{2,1,0:T(2,128)S(1)} async-done(((f32[64,2,128]{2,1,0:T(2,128)}), f32[64,2,128]{2,1,0:T(2,128)S(1)}, u32[]{:S(2)}, u32[]{:S(2)}) %all-to-all-start) | async-done | bytes 65568 | tf_op jit(solution)/shard_map/all_to_all | solution.py:568
  73.9 0.7 reduce_sum.9
  (2 shorter events, 0.1 us)
Async XLA Ops:
  4.0 25.2 %copy-start = (f32[2,8]{1,0:T(2,128)S(1)}, f32[2,8]{1,0:T(2,128)}, u32[]{:S(2)}) copy-start(f32[2,8]{1,0:T(2,128)} %weights.3) | copy-start | bytes 196
  4.0 15.9 %collective-permute-start.58 = (bf16[4,32,4,128]{3,2,1,0:T(4,128)(2,1)S(1)}, bf16[4,32,4,128]{3,2,1,0:T(4,128)(2,1)S(1)}, u32[]{:S(2)}, u32[]{:S(2)}) collective-permute-start(bf16[4,32,4,128]{3,2,1,0:T(4,128)(2,1)S(1)} %get-tuple-element.231), channel_id=1, source_target_pairs={{0,1},{2,3},{4,5},{6,7},{8,9},{10,11},{12,13},{14,15},{16,17},{18,... | collective-permute-start | bytes 393224 | tf_op jit(solution)/shard_map/cond/branch_8_fun/ppermute | solution.py:491
  8.0 12.0 %collective-permute-start.57 = (bf16[4,32,4,128]{3,2,1,0:T(4,128)(2,1)S(1)}, bf16[4,32,4,128]{3,2,1,0:T(4,128)(2,1)S(1)}, u32[]{:S(2)}, u32[]{:S(2)}) collective-permute-start(bf16[4,32,4,128]{3,2,1,0:T(4,128)(2,1)S(1)} %get-tuple-element.231), channel_id=1, source_target_pairs={{0,2},{2,0},{4,6},{6,4},{8,10},{10,8},{12,14},{14,12},{16,18},{18,... | collective-permute-start | bytes 393224 | tf_op jit(solution)/shard_map/cond/branch_8_fun/ppermute | solution.py:491
  12.4 7.6 %collective-permute-start.56 = (bf16[4,32,4,128]{3,2,1,0:T(4,128)(2,1)S(1)}, bf16[4,32,4,128]{3,2,1,0:T(4,128)(2,1)S(1)}, u32[]{:S(2)}, u32[]{:S(2)}) collective-permute-start(bf16[4,32,4,128]{3,2,1,0:T(4,128)(2,1)S(1)} %get-tuple-element.231), channel_id=1, source_target_pairs={{0,3},{2,1},{4,7},{6,5},{8,11},{10,9},{12,15},{14,13},{16,19},{18,... | collective-permute-start | bytes 393224 | tf_op jit(solution)/shard_map/cond/branch_8_fun/ppermute | solution.py:491
  13.7 13.0 %collective-permute-start.60 = (bf16[9,32,4,128]{3,2,1,0:T(4,128)(2,1)S(1)}, bf16[9,32,4,128]{3,2,1,0:T(4,128)(2,1)}, u32[]{:S(2)}, u32[]{:S(2)}) collective-permute-start(bf16[9,32,4,128]{3,2,1,0:T(4,128)(2,1)S(1)} %get-tuple-element.235), channel_id=1, source_target_pairs={{8,16},{24,32},{40,48},{56,64},{72,80},{88,96},{104,112},{120,128}... | collective-permute-start | bytes 884744 | tf_op jit(solution)/shard_map/cond/branch_8_fun/ppermute | solution.py:474
  18.0 11.1 %collective-permute-start.59 = (f32[2,3,32,4,128]{4,3,2,1,0:T(4,128)}, f32[2,3,32,4,128]{4,3,2,1,0:T(4,128)}, u32[]{:S(2)}, u32[]{:S(2)}) collective-permute-start(f32[2,3,32,4,128]{4,3,2,1,0:T(4,128)} %get-tuple-element.234), channel_id=1, source_target_pairs={{0,8},{8,0},{1,9},{9,1},{2,10},{10,2},{3,11},{11,3},{4,12},{12,4},... | collective-permute-start | bytes 1179656 | tf_op jit(solution)/shard_map/cond/branch_8_fun/ppermute | solution.py:467
  21.1 8.0 %collective-permute-start.62 = (bf16[8,32,4,128]{3,2,1,0:T(4,128)(2,1)}, bf16[8,32,4,128]{3,2,1,0:T(4,128)(2,1)}, u32[]{:S(2)}, u32[]{:S(2)}) collective-permute-start(bf16[8,32,4,128]{3,2,1,0:T(4,128)(2,1)} %pad_maximum_fusion.8), channel_id=1, source_target_pairs={{8,16},{24,32},{40,48},{56,64},{72,80},{88,96},{104,112},{120,128}... | collective-permute-start | bytes 786440 | tf_op jit(solution)/shard_map/cond/branch_8_fun/ppermute | solution.py:474
  24.7 4.4 %collective-permute-start.61 = (bf16[8,32,4,128]{3,2,1,0:T(4,128)(2,1)}, bf16[8,32,4,128]{3,2,1,0:T(4,128)(2,1)}, u32[]{:S(2)}, u32[]{:S(2)}) collective-permute-start(bf16[8,32,4,128]{3,2,1,0:T(4,128)(2,1)} %pad_maximum_fusion.8), channel_id=1, source_target_pairs={{0,8},{8,0},{1,9},{9,1},{2,10},{10,2},{3,11},{11,3},{4,12},{12,4},... | collective-permute-start | bytes 786440 | tf_op jit(solution)/shard_map/cond/branch_8_fun/ppermute | solution.py:467
  32.8 6.7 %collective-permute-start.112 = (f32[24,8,128]{2,1,0:T(8,128)S(1)}, f32[24,8,128]{2,1,0:T(8,128)S(1)}, u32[]{:S(2)}, u32[]{:S(2)}) collective-permute-start(f32[24,8,128]{2,1,0:T(8,128)S(1)} %get-tuple-element.312.mine), channel_id=1, source_target_pairs={{0,4},{4,0},{1,5},{5,1},{2,6},{6,2},{3,7},{7,3},{8,12},{12,8},{9,1... | collective-permute-start | bytes 294920 | tf_op jit(solution)/shard_map/ppermute | solution.py:548
  44.6 29.3 %all-to-all-start = ((f32[64,2,128]{2,1,0:T(2,128)}), f32[64,2,128]{2,1,0:T(2,128)S(1)}, u32[]{:S(2)}, u32[]{:S(2)}) async-start(f32[64,2,128]{2,1,0:T(2,128)} %broadcast_in_dim.2), calls=%async_computation | async-start | bytes 131072 | tf_op jit(solution)/shard_map/all_to_all | solution.py:568
  63.0 4.9 %collective-permute-start.113 = (f32[6,8,128]{2,1,0:T(8,128)S(1)}, f32[6,8,128]{2,1,0:T(8,128)S(1)}, u32[]{:S(2)}, u32[]{:S(2)}) collective-permute-start(f32[6,8,128]{2,1,0:T(8,128)S(1)} %get-tuple-element.320.mine), channel_id=1, source_target_pairs={{0,4},{4,0},{1,5},{5,1},{2,6},{6,2},{3,7},{7,3},{8,12},{12,8},{9,1... | collective-permute-start | bytes 73736 | tf_op jit(solution)/shard_map/ppermute | solution.py:564
